TPU v7x, 32 devices: a whole 2x2x4 slice. The times are simulated.
32 devices in a mesh: band: 4 (over y, core), slab: 8 (over z, x).
Axes of the slice: x: 2, y: 2, z: 4, core: 2. Of those that a mesh axis runs over, the one named last changes fastest.
Arguments:
- bands: float32 [2, 256, 32768], P(None, ('band', 'slab')), may hold values from -6 to 6
- projectors: float32 [4096, 512], P('slab'), may hold values from -0.625 to 0.625
- slot_atom: int32 [4096], P('slab'), may hold values from -1 to 767, as said below
- slot_box: int32 [4096], P('slab'), may hold values from 0 to 63
- channels: int32 [768], replicated, may hold values from 1 to 8
- coupling: float32 [8, 8, 768], replicated, may hold values from -2 to 2
Outputs:
- applied: float32 [2, 256, 32768], P(None, ('band', 'slab'))
Inputs may be any that keep to these rules, and one draw needn't show every extreme that they name: `slot_atom`: atom a is owned by slab a // 96. A live slot k names an atom owned by slab k // 512 or by the slab before it, cyclically. In each slab's 512 slots the live ones come first; some slab has all of its slots live.
All inputs are finite; a program needn't handle non-finite values.
Results may differ from a plain program's by a relative error of at most 0.0003.
Values sent between devices are 32-bit elements; how exact they have to be, the bound alone decides.
No kernel may reach another device: no remote copies, remote signals or barrier semaphores. Data moves between devices by JAX's collectives and lax.ppermute only.
A program may use at most 128 MiB of HBM per device.

v0:
```python
import collections
import functools
import math

import jax
import jax.numpy as jnp
import numpy as np
from jax import lax
from jax.experimental import pallas as pl
from jax.experimental.pallas import tpu as pltpu
from jax.sharding import PartitionSpec as P

BOXPTS = 64
GROUP = 16
INFO = 8
UNROLL = 8
AXES = ("band", "slab")
MIB = 1 << 20


def round_up(value, step):
    return (value + step - 1) // step * step


def cycle_tables(nslab):
    order = list(range(0, nslab, 2)) + list(range(nslab - 1 - nslab % 2, 0, -2))
    place = {s: i for i, s in enumerate(order)}
    return order, place


def params(limit):
    return pltpu.CompilerParams(vmem_limit_bytes=limit)


VMEM = pl.BlockSpec(memory_space=pltpu.VMEM)
SMEM = pl.BlockSpec(memory_space=pltpu.SMEM)
ANY = pl.BlockSpec(memory_space=pl.ANY)


def split_bands_kernel(atom_dev, x_ref, coupling_ref, channels_ref, out_ref, masked_ref, whole):
    @pl.when(pl.program_id(0) == 0)
    def _():
        channel = channels_ref.shape[0]
        natoms = channels_ref.shape[1]
        number = lax.broadcasted_iota(jnp.int32, (channel, natoms), 0)
        mask = jnp.where(number < channels_ref[...], 1.0, 0.0)
        for c in range(channel):
            own = slice(c * channel, (c + 1) * channel)
            whole[own, :] = coupling_ref[own, :] * mask * mask[c : c + 1, :]
        lanes = masked_ref.shape[2]
        for slab in range(masked_ref.shape[0]):
            base = slab * atom_dev // 128 * 128
            part = whole[:, base : min(base + lanes + 128, natoms)]
            if part.shape[1] < lanes:
                part = jnp.concatenate([part, part[:, : lanes - part.shape[1]]], axis=1)
            if slab * atom_dev != base:
                part = pltpu.roll(part, part.shape[1] - (slab * atom_dev - base), 1)
            masked_ref[slab] = part[:, :lanes]

    rows = x_ref.shape[0]
    low_half = lax.broadcasted_iota(jnp.int32, (rows, 128), 1) < BOXPTS
    zero = jnp.zeros((rows, 128), jnp.float32)

    def step(pair, carry):
        x = x_ref[:, pl.ds(pl.multiple_of(pair * 128, 128), 128)]
        high = x.astype(jnp.bfloat16).astype(jnp.float32)
        low = x - high
        high_turned = pltpu.roll(high, BOXPTS, 1)
        low_turned = pltpu.roll(low, BOXPTS, 1)
        out_ref[2 * pair, :, 0:128] = jnp.where(low_half, high, high_turned).astype(jnp.bfloat16)
        out_ref[2 * pair, :, 128:256] = jnp.where(low_half, low, zero).astype(jnp.bfloat16)
        out_ref[2 * pair + 1, :, 0:128] = jnp.where(low_half, high_turned, high).astype(jnp.bfloat16)
        out_ref[2 * pair + 1, :, 128:256] = jnp.where(low_half, low_turned, zero).astype(jnp.bfloat16)
        return carry

    lax.fori_loop(0, x_ref.shape[1] // 128, step, 0, unroll=4)


def split_bands(x, coupling, channels, nslab, lanes):
    rows, ngrid = x.shape
    channel, natoms = coupling.shape[1:]
    span = ngrid // nslab
    boxes = span // BOXPTS
    return pl.pallas_call(
        functools.partial(split_bands_kernel, natoms // nslab),
        grid=(nslab,),
        out_shape=[
            jax.ShapeDtypeStruct((ngrid // BOXPTS, rows, 256), jnp.bfloat16),
            jax.ShapeDtypeStruct((nslab, channel * channel, lanes), jnp.float32),
        ],
        in_specs=[
            pl.BlockSpec((rows, span), lambda i: (0, i)),
            pl.BlockSpec((channel * channel, natoms), lambda i: (0, 0)),
            pl.BlockSpec((channel, natoms), lambda i: (0, 0)),
        ],
        out_specs=[
            pl.BlockSpec((boxes, rows, 256), lambda i: (i, 0, 0)),
            pl.BlockSpec((nslab, channel * channel, lanes), lambda i: (0, 0, 0)),
        ],
        scratch_shapes=[pltpu.VMEM((channel * channel, natoms), jnp.float32)],
        compiler_params=params(16 * MIB),
        cost_estimate=pl.CostEstimate(
            flops=8 * x.size, bytes_accessed=12 * x.size, transcendentals=0
        ),
        name="split_bands",
    )(
        pltpu.with_memory_space_constraint(x, pltpu.HBM),
        coupling.reshape(channel * channel, natoms),
        jnp.broadcast_to(channels[None, :], (channel, natoms)),
    )


def slot_weights(values, low_half, axis):
    full, top = [], []
    for t in range(values.shape[1] // 128):
        x = values[:, t * 128 : (t + 1) * 128]
        high = x.astype(jnp.bfloat16).astype(jnp.float32)
        low = x - high
        turned = pltpu.roll(high, BOXPTS, 1)
        full.append(jnp.where(low_half, high, pltpu.roll(low, BOXPTS, 1)).astype(jnp.bfloat16))
        full.append(jnp.where(low_half, turned, low).astype(jnp.bfloat16))
        top.append(jnp.where(low_half, high, 0.0).astype(jnp.bfloat16))
        top.append(jnp.where(low_half, turned, 0.0).astype(jnp.bfloat16))
    return jnp.concatenate(
        [jnp.concatenate(full, axis=0), jnp.concatenate(top, axis=0)], axis=axis
    )


def live_groups(live, start, length):
    return lax.div(jnp.clip(live - start, 0, length) + (GROUP - 1), GROUP)


def begin_kernel(natoms, lanes, atom_ref, box_ref, projector_ref, info_ref, mine_ref, info_sem, half_sem):
    nslab = lax.axis_size("slab")
    half = mine_ref.shape[0] - INFO
    core = lax.rem(lax.axis_index("band"), 2)
    copy = pltpu.make_async_copy(
        projector_ref.at[pl.ds(pl.multiple_of(core * half, GROUP), half), :],
        mine_ref.at[pl.ds(INFO, half), :],
        half_sem,
    )
    copy.start()
    atom_dev = natoms // nslab
    below = lax.rem(lax.axis_index("slab") + nslab - 1, nslab) * atom_dev
    atom = atom_ref[...]
    slots = atom.shape[1]
    relative = atom - below
    relative = jnp.where(relative < 0, relative + natoms, relative)
    column = jnp.where(relative < atom_dev, relative, relative + (lanes - atom_dev))
    live = jnp.sum(jnp.where(atom >= 0, 1.0, 0.0), axis=1, keepdims=True)
    info_ref[...] = jnp.zeros(info_ref.shape, jnp.float32)
    info_ref[0:1, 0:slots] = box_ref[...].astype(jnp.float32)
    info_ref[1:2, 0:slots] = jnp.broadcast_to(live, (1, slots))
    info_ref[2:3, 0:slots] = jnp.where(atom >= 0, column, -1).astype(jnp.float32)
    head = pltpu.make_async_copy(info_ref, mine_ref.at[pl.ds(0, INFO), :], info_sem)
    head.start()
    head.wait()
    copy.wait()


def begin(slot_atom, slot_box, projectors, natoms, lanes):
    slots, depth = projectors.shape
    return pl.pallas_call(
        functools.partial(begin_kernel, natoms, lanes),
        out_shape=[
            jax.ShapeDtypeStruct((INFO, depth), jnp.float32),
            jax.ShapeDtypeStruct((INFO + slots // 2, depth), jnp.float32),
        ],
        in_specs=[VMEM, VMEM, ANY],
        out_specs=[VMEM, ANY],
        scratch_shapes=[pltpu.SemaphoreType.DMA(()), pltpu.SemaphoreType.DMA(())],
        compiler_params=params(8 * MIB),
        name="begin",
    )(
        slot_atom.reshape(1, slots),
        slot_box.reshape(1, slots),
        pltpu.with_memory_space_constraint(projectors, pltpu.HBM),
    )


def scalar_row(info, first):
    return jnp.concatenate([info[0:1, :] + first, info[1:2, 0:128]], axis=1).astype(jnp.int32)


def project_kernel(pieces, infos, place_ref, x_ref, *refs):
    arrays = refs[: -len(pieces) - 4]
    outs = refs[-len(pieces) - 4 : -4]
    whole, proj, table, sem = refs[-4:]
    for k, index in enumerate(infos):
        whole[k : k + 1, :] = scalar_row(arrays[index][0:INFO, :], 0)
    copy = pltpu.make_async_copy(whole, table, sem)
    copy.start()
    rows = x_ref.shape[1]
    slots = arrays[infos[0]].shape[1]
    width = proj.shape[3]
    chunk = width // GROUP
    lane_block = lax.broadcasted_iota(jnp.int32, (rows, width), 1) // GROUP
    low_half = lax.broadcasted_iota(jnp.int32, (GROUP, 128), 1) < BOXPTS
    lane_slot = lax.broadcasted_iota(jnp.int32, (rows, width), 1) % GROUP
    proj[...] = jnp.zeros(proj.shape, jnp.float32)
    copy.wait()
    for which, p in enumerate(pieces):
        array = arrays[p.array]
        start = place_ref[3 * p.index + 1]
        box_base = place_ref[3 * p.index + 2]
        info = infos.index(p.info)
        count = live_groups(table[info, slots], start, p.rows)

        def step(block, carry):
            groups = [block * UNROLL + u for u in range(UNROLL)]
            weights, patches = [], []
            for g in groups:
                first = pl.multiple_of(p.offset + g * GROUP, 8)
                weights.append(slot_weights(array[pl.ds(first, GROUP), :], low_half, 1))
                boxes = [table[info, start + g * GROUP + s] for s in range(GROUP)]
                patches.append(jnp.concatenate([x_ref[box_base + b] for b in boxes], axis=0))
            totals = []
            for w, p_ in zip(weights, patches):
                product = lax.dot_general(
                    p_, w, (((1,), (1,)), ((), ())), preferred_element_type=jnp.float32
                )
                total = product[0:rows]
                for s in range(1, GROUP):
                    total = jnp.where(lane_slot == s, product[s * rows : (s + 1) * rows], total)
                totals.append(total)
            for g, total in zip(groups, totals):
                proj[which, g] = total
            return carry

        lax.fori_loop(0, lax.div(count + (UNROLL - 1), UNROLL), step, 0)

    for which, (p, out) in enumerate(zip(pieces, outs)):
        start = place_ref[3 * p.index + 1]
        columns = arrays[p.info][2:3, :]
        columns = pltpu.roll(columns, lax.rem(columns.shape[1] - start, columns.shape[1]), 1)
        nchunk = (p.rows // GROUP + chunk - 1) // chunk
        value = jnp.concatenate(
            [
                jnp.concatenate(
                    swap_blocks(
                        [proj[which, k * chunk + i] for i in range(chunk)], lane_block, width
                    ),
                    axis=0,
                )
                for k in range(nchunk)
            ],
            axis=1,
        )
        both = lax.dot_general(
            stacked_split(value),
            selector(columns[:, : nchunk * width], out.shape[1]),
            (((1,), (1,)), ((), ())),
            preferred_element_type=jnp.float32,
        )
        half = both.shape[0] // 2
        out[...] = both[:half] + both[half:]


def project(arrays, pieces, place, x, lanes):
    channel = arrays[0].shape[1] // BOXPTS
    used = sorted({p.array for p in pieces} | {p.info for p in pieces})
    local = [
        p._replace(array=used.index(p.array), info=used.index(p.info)) for p in pieces
    ]
    infos = sorted({p.info for p in local})
    shapes = [
        jax.ShapeDtypeStruct((channel * x.shape[1], 2 * lanes), jnp.float32) for p in pieces
    ]
    size = sum(p.rows for p in pieces) * arrays[0].shape[1]
    table = (round_up(len(infos), 8), arrays[0].shape[1] + 128)
    groups = round_up(max(p.rows for p in pieces), channel * GROUP) // GROUP
    return pl.pallas_call(
        functools.partial(project_kernel, local, infos),
        out_shape=shapes,
        in_specs=[SMEM, VMEM] + [VMEM] * len(used),
        out_specs=[VMEM] * len(pieces),
        scratch_shapes=[
            pltpu.VMEM(table, jnp.int32),
            pltpu.VMEM((len(pieces), groups, x.shape[1], channel * GROUP), jnp.float32),
            pltpu.SMEM(table, jnp.int32),
            pltpu.SemaphoreType.DMA(()),
        ],
        compiler_params=params(40 * MIB),
        cost_estimate=pl.CostEstimate(
            flops=2 * 16 * 16 * size, bytes_accessed=4 * size + 2 * x.size, transcendentals=0
        ),
        name="project",
    )(place, x, *[arrays[i] for i in used])


def swap_blocks(tiles, lane_block, width):
    tiles = list(tiles)
    bit = 1
    while bit < len(tiles):
        upper = (lane_block & bit) != 0
        for i in range(len(tiles)):
            if not i & bit:
                a, b = tiles[i], tiles[i | bit]
                tiles[i] = jnp.where(upper, pltpu.roll(b, GROUP * bit, 1), a)
                tiles[i | bit] = jnp.where(upper, b, pltpu.roll(a, width - GROUP * bit, 1))
        bit *= 2
    return tiles


def selector(columns, count):
    shape = (count, columns.shape[1])
    row = lax.broadcasted_iota(jnp.int32, shape, 0).astype(jnp.float32)
    return jnp.where(jnp.broadcast_to(columns, shape) == row, 1.0, 0.0).astype(jnp.bfloat16)


def stacked_split(value):
    high = value.astype(jnp.bfloat16)
    low = (value - high.astype(jnp.float32)).astype(jnp.bfloat16)
    return jnp.concatenate([high, low], axis=0)


def apply_kernel(nslab, slots, nsum, pieces, infos, place_ref, coupling_ref, *refs):
    npiece = len(pieces)
    proj, loaded, parts, beta, done, masks, info, whole, table = refs[-13:-4]
    sums = refs[-13 - nsum : -13]
    beta_sem, proj_sem, info_sem, out_sem = refs[-4:]
    base = len(refs) - 14 - nsum
    out_ref = refs[base]
    projections = refs[base - npiece : base]
    arrays = refs[: base - npiece]
    groups = slots // GROUP
    rows, width = proj.shape[1], proj.shape[2]
    channel = width // GROUP
    lanes = parts.shape[2] // 2
    boxes = out_ref.shape[1] // BOXPTS // nslab
    chunk = width // GROUP
    info_copies, copies, beta_copies = [], [], []
    for i, (array, index) in enumerate(infos):
        slab = place_ref[3 * index]
        info_copies.append(
            pltpu.make_async_copy(arrays[array].at[0:INFO, :], info.at[slab], info_sem.at[i])
        )
    for i, p in enumerate(pieces):
        slab, start = place_ref[3 * p.index], place_ref[3 * p.index + 1]
        j = i % loaded.shape[0]
        copies.append(
            pltpu.make_async_copy(projections[i], loaded.at[j], proj_sem.at[i])
        )
        first = pl.multiple_of(slab * slots + start, GROUP)
        beta_copies.append(
            pltpu.make_async_copy(
                arrays[p.array].at[p.offset : p.offset + p.rows, :],
                beta.at[pl.ds(first, p.rows), :],
                beta_sem.at[i],
            )
        )
    for c in info_copies + copies[: loaded.shape[0]] + beta_copies:
        c.start()
    lane_slot = lax.broadcasted_iota(jnp.int32, (rows, width), 1) % GROUP
    for s in range(GROUP):
        masks[s] = jnp.where(lane_slot == s, 1.0, 0.0).astype(jnp.bfloat16)
    for total in sums:
        total[...] = jnp.zeros(total.shape, jnp.float32)
    parts[...] = jnp.zeros(parts.shape, jnp.float32)
    for c in info_copies:
        c.wait()
    for slab in range(nslab):
        whole[slab : slab + 1, :] = scalar_row(info[slab], float(slab * boxes))
    to_scalars = pltpu.make_async_copy(whole, table, info_sem.at[0])
    to_scalars.start()
    for first in range(0, npiece, loaded.shape[0]):
        wave = range(first, min(first + loaded.shape[0], npiece))
        for i in wave:
            if first > 0:
                copies[i].start()
        for i in wave:
            copies[i].wait()
        for i in wave:
            slab = place_ref[3 * pieces[i].index]
            parts[slab] = parts[slab] + loaded[i % loaded.shape[0]]

    lane_block = lax.broadcasted_iota(jnp.int32, (rows, width), 1) // GROUP
    def couple(slab, carry):
        following = lax.rem(slab + 1, nslab)
        total = parts[slab, :, lanes:] + parts[following, :, :lanes]
        for c in range(channel):
            mixed = jnp.zeros((rows, lanes), jnp.float32)
            for e in range(channel):
                factor = coupling_ref[slab, pl.ds(c * channel + e, 1), :]
                mixed = mixed + factor * total[e * rows : (e + 1) * rows]
            parts[slab, c * rows : (c + 1) * rows, lanes:] = mixed
        return carry

    lax.fori_loop(0, nslab, couple, 0)

    def spread(slab, carry):
        below = lax.rem(slab + nslab - 1, nslab)
        value = jnp.concatenate([parts[below, :, lanes:], parts[slab, :, lanes:]], axis=1)
        value = stacked_split(value)

        both = jnp.dot(
            value, selector(info[slab, 2:3, 0:slots], 2 * lanes), preferred_element_type=jnp.float32
        )
        half = both.shape[0] // 2
        both = both[:half] + both[half:]
        for k in range(groups // chunk):
            tiles = [
                both[c * rows : (c + 1) * rows, k * width : (k + 1) * width]
                for c in range(channel)
            ]
            for i, tile in enumerate(swap_blocks(tiles, lane_block, width)):
                proj[slab * groups + k * chunk + i] = tile
        return carry

    lax.fori_loop(0, nslab, spread, 0, unroll=4 if nsum > 1 else 1)
    to_scalars.wait()

    for c in beta_copies:
        c.wait()

    low_half = lax.broadcasted_iota(jnp.int32, (GROUP, 128), 1) < BOXPTS
    pair_half = lax.broadcasted_iota(jnp.int32, (rows, 128), 1) < BOXPTS
    span = boxes * BOXPTS

    def leaving(slab):
        slot = lax.rem(slab, 2)
        return pltpu.make_async_copy(
            done.at[slot],
            out_ref.at[:, pl.ds(pl.multiple_of(slab * span, 128), span)],
            out_sem.at[slot],
        )

    def slab_step(slab, carry):
        def step(block, inner):
            products = []
            for u in range(UNROLL):
                g = block * UNROLL + u
                slot_base = pl.multiple_of(slab * slots + g * GROUP, GROUP)
                weights = slot_weights(beta[pl.ds(slot_base, GROUP), :], low_half, 0)
                c = proj[slab * groups + g]
                high = c.astype(jnp.bfloat16)
                low = (c - high.astype(jnp.float32)).astype(jnp.bfloat16)
                left = jnp.concatenate(
                    [
                        jnp.concatenate([high * masks[s], low * masks[s]], axis=1)
                        for s in range(GROUP)
                    ],
                    axis=0,
                )
                products.append((slot_base, jnp.dot(left, weights, preferred_element_type=jnp.float32)))
            for u, (slot_base, product) in enumerate(products):
                for s in range(GROUP):
                    box = table[slab, block * (UNROLL * GROUP) + u * GROUP + s]
                    j = (u * GROUP + s) % nsum
                    sums[j][box] = sums[j][box] + product[s * rows : (s + 1) * rows]
            return inner

        count = live_groups(table[slab, info.shape[2]], 0, slots)
        lax.fori_loop(0, lax.div(count + (UNROLL - 1), UNROLL), step, 0)

        @pl.when(slab >= 2)
        def _():
            leaving(slab - 2).wait()

        def finish(pair, inner):
            folded = []
            for i in range(2):
                box = slab * boxes + 2 * pair + i
                value = sums[0][box]
                for j in range(1, nsum):
                    value = value + sums[j][box]
                folded.append(value + pltpu.roll(value, BOXPTS, 1))
            done[lax.rem(slab, 2), :, pl.ds(pl.multiple_of(pair * 128, 128), 128)] = jnp.where(
                pair_half, folded[0], folded[1]
            )
            return inner

        lax.fori_loop(0, span // 128, finish, 0, unroll=min(32, span // 128))
        leaving(slab).start()
        return carry

    lax.fori_loop(0, nslab, slab_step, 0)
    for slab in range(max(nslab - 2, 0), nslab):
        leaving(slab).wait()


def apply(arrays, pieces, infos, projections, place, coupling, nslab, slots, rows, ngrid):
    width = projections[0].shape[0] // rows * GROUP
    lanes = coupling.shape[2]
    depth = arrays[0].shape[1]
    one_sum = ngrid // BOXPTS * rows * 128 * 4
    nsum = 2 if one_sum <= 8 * MIB else 1
    buffers = [pltpu.VMEM((ngrid // BOXPTS, rows, 128), jnp.float32) for _ in range(nsum)]
    buffers += [
        pltpu.VMEM((nslab * slots // GROUP, rows, width), jnp.float32),
        pltpu.VMEM((len(pieces) if len(pieces) <= 24 else 1,) + projections[0].shape, jnp.float32),
        pltpu.VMEM((nslab,) + projections[0].shape, jnp.float32),
        pltpu.VMEM((nslab * slots, depth), jnp.float32),
        pltpu.VMEM((2, rows, ngrid // nslab), jnp.float32),
        pltpu.VMEM((GROUP, rows, width), jnp.bfloat16),
        pltpu.VMEM((nslab, INFO, depth), jnp.float32),
        pltpu.VMEM((nslab, depth + 128), jnp.int32),
    ]
    need = sum(math.prod(b.shape) * b.dtype.itemsize for b in buffers)
    scratch = buffers + [
        pltpu.SMEM((nslab, depth + 128), jnp.int32),
        pltpu.SemaphoreType.DMA((len(pieces),)),
        pltpu.SemaphoreType.DMA((len(pieces),)),
        pltpu.SemaphoreType.DMA((len(infos),)),
        pltpu.SemaphoreType.DMA((2,)),
    ]
    return pl.pallas_call(
        functools.partial(apply_kernel, nslab, slots, nsum, pieces, infos),
        out_shape=jax.ShapeDtypeStruct((rows, ngrid), jnp.float32),
        in_specs=[SMEM, VMEM] + [ANY] * (len(arrays) + len(pieces)),
        out_specs=ANY,
        scratch_shapes=scratch,
        compiler_params=params(min(need + 4 * MIB, 63 * MIB)),
        name="apply",
    )(place, coupling, *arrays, *projections)


Piece = collections.namedtuple("Piece", ["array", "offset", "rows", "info", "index"])


def gather_and_project(projectors, described, mine, split, lanes, nband, nslab):
    slots = projectors.shape[0]
    order, at = cycle_tables(nslab)
    half = slots // 2
    quarter = half // 2
    reach = nslab // 2
    onward = [
        (b * nslab + order[i], b * nslab + order[(i + 1) % nslab])
        for b in range(nband)
        for i in range(nslab)
    ]
    backward = [(d, s) for s, d in onward]
    sibling = [(b * nslab + s, (b ^ 1) * nslab + s) for b in range(nband) for s in range(nslab)]

    where = [(0, 0, None)]
    for step in range(1, reach):
        where += [(1 - step, 0, True), (step - 1, 0, True)] if step > 1 else []
        where += [(-step, 0, False), (step, 0, False)]
    where += [(1 - reach, 0, True), (reach - 1, 0, True)]
    where += [(reach, 0, False), (reach, quarter, False), (reach, 0, True), (reach, quarter, True)]
    boxes = split.shape[0] // nslab

    def entry(core, slab, distance, start, other):
        there = order[(at[slab] + distance) % nslab]
        if other is not None:
            start += half * ((1 - core) if other else core)
        return there, start, there * boxes

    table = [[entry(b % 2, s, *w) for w in where] for b in range(nband) for s in range(nslab)]
    me = lax.axis_index("band") * nslab + lax.axis_index("slab")
    place = lax.dynamic_index_in_dim(
        jnp.asarray(np.array(table, np.int32)), me, 0, keepdims=False
    ).reshape(-1)

    arrays, pieces, infos, projections = [described, projectors], [], [(0, 0)], []

    def add(array, info=None):
        arrays.append(array)
        own = len(arrays) - 1
        offset = INFO if info is None else 0
        pieces.append(
            Piece(own, offset, array.shape[0] - offset, own if info is None else info, len(pieces))
        )
        return own

    pieces.append(Piece(1, 0, slots, 0, 0))
    up = lax.ppermute(mine, AXES, onward)
    down = lax.ppermute(mine, AXES, backward)
    done = 0

    def project_new():
        nonlocal done
        projections.extend(project(arrays, pieces[done:], place, split, lanes))
        done = len(pieces)

    project_new()
    up, down, projections, place = lax.optimization_barrier((up, down, projections, place))
    projections = list(projections)
    near = []
    for step in range(1, reach + 1):
        last = step == reach
        for array in near:
            add(array)
        for array in (up,) if last else (up, down):
            infos.append((add(array), len(pieces) - 1))
        if last:
            add(down, len(arrays) - 1)
        near = [lax.ppermute(up, AXES, sibling), lax.ppermute(down, AXES, sibling)]
        if step + 1 < reach:
            up = lax.ppermute(up, AXES, onward)
            down = lax.ppermute(down, AXES, backward)
        elif not last:
            up = lax.ppermute(up[: INFO + quarter], AXES, onward)
            down = lax.ppermute(down[INFO + quarter :], AXES, backward)
        project_new()
        up, down, near, projections = lax.optimization_barrier((up, down, near, projections))
        near, projections = list(near), list(projections)
    add(near[0])
    add(near[1], len(arrays) - 1)
    project_new()
    return arrays, pieces, infos, projections, place


def body(bands, projectors, slot_atom, slot_box, channels, coupling):
    nblock, band_local, ngrid = bands.shape
    nband, nslab = lax.axis_size("band"), lax.axis_size("slab")
    natoms = channels.shape[0]
    atom_dev = natoms // nslab
    slots = slot_atom.shape[0]
    lanes = round_up(atom_dev, 128)

    described, mine = begin(slot_atom, slot_box, projectors, natoms, lanes)
    rows = nblock * band_local
    padded = round_up(rows, GROUP)
    x = bands.reshape(rows, ngrid)
    if padded != rows:
        x = jnp.pad(x, ((0, padded - rows), (0, 0)))
    split, masked = split_bands(x, coupling, channels, nslab, lanes)
    arrays, pieces, infos, projections, place = gather_and_project(
        projectors, described, mine, split, lanes, nband, nslab
    )
    out = apply(arrays, pieces, infos, projections, place, masked, nslab, slots, padded, ngrid)
    return out[:rows].reshape(nblock, band_local, ngrid)


def solution(mesh):
    in_specs = (P(None, ("band", "slab"), None), P("slab", None), P("slab"), P("slab"), P(), P())
    out_specs = P(None, ("band", "slab"), None)
    return jax.shard_map(body, mesh=mesh, in_specs=in_specs, out_specs=out_specs, check_vma=False)
```

profile of v0, /device:TPU:1, one launch (start us, length us, event | category | flops | bytes accessed | tf_op | source)
XLA Modules:
  0.0 89.6 jit_solution(13805514430241798365)
XLA Ops:
  0.0 0.8 copy-done.2
  1.5 1.1 %begin.1 = (f32[8,512]{1,0:T(8,128)S(1)}, f32[264,512]{1,0:T(8,128)S(1)}) custom-call(s32[1,512]{1,0:T(1,128)S(1)} %bitcast.6, s32[1,512]{1,0:T(1,128)S(1)} %bitcast.7, f32[512,512]{1,0:T(8,128)} %refs_1_.3), custom_call_target="tpu_custom_call" | custom-call | tf_op jit(solution)/shard_map/begin/pallas_call | solution.py:163
  2.5 2.2 %collective-permute-start = (f32[264,512]{1,0:T(8,128)S(1)}, f32[264,512]{1,0:T(8,128)S(1)}, u32[]{:S(2)}, u32[]{:S(2)}) collective-permute-start(f32[264,512]{1,0:T(8,128)S(1)} %get-tuple-element.79), channel_id=1, source_target_pairs={{0,2},{2,4},{4,6},{6,7},{7,5},{5,3},{3,1},{1,0},{8,10},{10,12},{12... | collective-permute-start | bytes 1622024 | tf_op jit(solution)/shard_map/ppermute | solution.py:567
  6.2 0.9 %copy-done.1 = f32[8,8,768]{2,1,0:T(8,128)S(1)} copy-done((f32[8,8,768]{2,1,0:T(8,128)S(1)}, f32[8,8,768]{2,1,0:T(8,128)}, u32[]{:S(2)}) %copy-start.1) | copy-done | bytes 196632
  7.1 7.4 %split_bands.1 = (bf16[512,16,256]{2,1,0:T(8,128)(2,1)S(1)}, f32[8,64,128]{2,1,0:T(8,128)S(1)}) custom-call(f32[16,32768]{1,0:T(8,128)} %bitcast.8, f32[64,768]{1,0:T(8,128)S(1)} %bitcast.5, s32[8,768]{1,0:T(8,128)S(1)} %broadcast_in_dim.2.channels_ref), custom_call_target="tpu_custom_call" | custom-call | flops 4194304 | bytes 6291456 | tf_op jit(solution)/shard_map/split_bands/pallas_call | solution.py:84
  14.6 3.0 %project.6.refs_18_ = f32[128,256]{1,0:T(8,128)S(1)} custom-call(s32[51]{0:T(128)S(1)} %reshape.22.place_ref, bf16[512,16,256]{2,1,0:T(8,128)(2,1)S(1)} %get-tuple-element.80.x_ref, f32[8,512]{1,0:T(8,128)S(1)} %get-tuple-element.81.refs_0_, f32[512,512]{1,0:T(8,128)S(1)} %copy-done), custom_call_target="tpu_custom_call" | custom-call | flops 134217728 | bytes 5242880 | tf_op jit(solution)/shard_map/project/pallas_call | solution.py:272
  17.6 1.5 %collective-permute-start.2 = (f32[264,512]{1,0:T(8,128)S(1)}, f32[264,512]{1,0:T(8,128)S(1)}, u32[]{:S(2)}, u32[]{:S(2)}) collective-permute-start(f32[264,512]{1,0:T(8,128)S(1)} %collective-permute-done.refs_0_.refs_2_), channel_id=1, source_target_pairs={{0,2},{2,4},{4,6},{6,7},{7,5},{5,3},{3,1},{1,0},{8,10},{10,12},{12... | collective-permute-start | bytes 1622024 | tf_op jit(solution)/shard_map/ppermute | solution.py:590
  19.1 1.0 %collective-permute-start.3 = (f32[264,512]{1,0:T(8,128)S(1)}, f32[264,512]{1,0:T(8,128)S(1)}, u32[]{:S(2)}, u32[]{:S(2)}) collective-permute-start(f32[264,512]{1,0:T(8,128)S(1)} %collective-permute-done.1.refs_1_.refs_3_), channel_id=1, source_target_pairs={{2,0},{4,2},{6,4},{7,6},{5,7},{3,5},{1,3},{0,1},{10,8},{12,10},{14... | collective-permute-start | bytes 1622024 | tf_op jit(solution)/shard_map/ppermute | solution.py:591
  20.1 1.5 %collective-permute-start.4 = (f32[264,512]{1,0:T(8,128)S(1)}, f32[264,512]{1,0:T(8,128)S(1)}, u32[]{:S(2)}, u32[]{:S(2)}) collective-permute-start(f32[264,512]{1,0:T(8,128)S(1)} %collective-permute-done.refs_0_.refs_2_), channel_id=1, source_target_pairs={{0,8},{1,9},{2,10},{3,11},{4,12},{5,13},{6,14},{7,15},{8,0},{9,1},... | collective-permute-start | bytes 1622024 | tf_op jit(solution)/shard_map/ppermute | solution.py:588
  21.7 3.0 %project.7 = (f32[128,256]{1,0:T(8,128)S(1)}, f32[128,256]{1,0:T(8,128)S(1)}) custom-call(s32[51]{0:T(128)S(1)} %reshape.22.place_ref, bf16[512,16,256]{2,1,0:T(8,128)(2,1)S(1)} %get-tuple-element.80.x_ref, f32[264,512]{1,0:T(8,128)S(1)} %collective-permute-done.refs_0_.refs_2_, f32[264,512]{1,0:T(8,128)S(1)} %collective-permute-done.1.refs_1_.refs_3_), custom_call_target="tpu_custom_call" | custom-call | flops 134217728 | bytes 5242880 | tf_op jit(solution)/shard_map/project/pallas_call | solution.py:272
  24.6 6.8 %collective-permute-done.2.refs_2_.refs_6_ = f32[264,512]{1,0:T(8,128)S(1)} collective-permute-done((f32[264,512]{1,0:T(8,128)S(1)}, f32[264,512]{1,0:T(8,128)S(1)}, u32[]{:S(2)}, u32[]{:S(2)}) %collective-permute-start.2) | collective-permute-done | bytes 540704 | tf_op jit(solution)/shard_map/ppermute | solution.py:590
  31.8 1.2 %collective-permute-start.7 = (f32[264,512]{1,0:T(8,128)S(1)}, f32[264,512]{1,0:T(8,128)S(1)}, u32[]{:S(2)}, u32[]{:S(2)}) collective-permute-start(f32[264,512]{1,0:T(8,128)S(1)} %collective-permute-done.3.refs_3_.refs_7_), channel_id=1, source_target_pairs={{2,0},{4,2},{6,4},{7,6},{5,7},{3,5},{1,3},{0,1},{10,8},{12,10},{14... | collective-permute-start | bytes 1622024 | tf_op jit(solution)/shard_map/ppermute | solution.py:591
  33.0 2.9 %collective-permute-start.8 = (f32[264,512]{1,0:T(8,128)S(1)}, f32[264,512]{1,0:T(8,128)S(1)}, u32[]{:S(2)}, u32[]{:S(2)}) collective-permute-start(f32[264,512]{1,0:T(8,128)S(1)} %collective-permute-done.2.refs_2_.refs_6_), channel_id=1, source_target_pairs={{0,8},{1,9},{2,10},{3,11},{4,12},{5,13},{6,14},{7,15},{8,0},{9,1},... | collective-permute-start | bytes 1622024 | tf_op jit(solution)/shard_map/ppermute | solution.py:588
  35.8 4.4 %project.8 = (f32[128,256]{1,0:T(8,128)S(1)}, f32[128,256]{1,0:T(8,128)S(1)}, f32[128,256]{1,0:T(8,128)S(1)}, f32[128,256]{1,0:T(8,128)S(1)}) custom-call(s32[51]{0:T(128)S(1)} %reshape.22.place_ref, bf16[512,16,256]{2,1,0:T(8,128)(2,1)S(1)} %get-tuple-element.80.x_ref, f32[264,512]{1,0:T(8,128)S(1)} %collective-permute-done.4.refs_0_.refs_4_, ...), custom_call_target="tpu_custom_call" | custom-call | flops 268435456 | bytes 6291456 | tf_op jit(solution)/shard_map/project/pallas_call | solution.py:272
  40.2 2.8 %collective-permute-done.6.refs_2_.refs_10_ = f32[264,512]{1,0:T(8,128)S(1)} collective-permute-done((f32[264,512]{1,0:T(8,128)S(1)}, f32[264,512]{1,0:T(8,128)S(1)}, u32[]{:S(2)}, u32[]{:S(2)}) %collective-permute-start.6) | collective-permute-done | bytes 540704 | tf_op jit(solution)/shard_map/ppermute | solution.py:590
  43.0 1.2 %collective-permute-done.7.refs_3_.refs_11_ = f32[264,512]{1,0:T(8,128)S(1)} collective-permute-done((f32[264,512]{1,0:T(8,128)S(1)}, f32[264,512]{1,0:T(8,128)S(1)}, u32[]{:S(2)}, u32[]{:S(2)}) %collective-permute-start.7) | collective-permute-done | bytes 540704 | tf_op jit(solution)/shard_map/ppermute | solution.py:591
  44.1 3.3 %collective-permute-start.12 = (f32[264,512]{1,0:T(8,128)S(1)}, f32[264,512]{1,0:T(8,128)S(1)}, u32[]{:S(2)}, u32[]{:S(2)}) collective-permute-start(f32[264,512]{1,0:T(8,128)S(1)} %collective-permute-done.6.refs_2_.refs_10_), channel_id=1, source_target_pairs={{0,8},{1,9},{2,10},{3,11},{4,12},{5,13},{6,14},{7,15},{8,0},{9,1},... | collective-permute-start | bytes 1622024 | tf_op jit(solution)/shard_map/ppermute | solution.py:588
  47.6 1.5 %collective-permute-start.10 = (f32[136,512]{1,0:T(8,128)S(1)}, f32[136,512]{1,0:T(8,128)S(1)}, u32[]{:S(2)}, u32[]{:S(2)}) collective-permute-start(f32[136,512]{1,0:T(8,128)S(1)} %slice.6), channel_id=1, source_target_pairs={{0,2},{2,4},{4,6},{6,7},{7,5},{5,3},{3,1},{1,0},{8,10},{10,12},{12... | collective-permute-start | bytes 835592 | tf_op jit(solution)/shard_map/ppermute | solution.py:593
  49.2 4.9 %project.9 = (f32[128,256]{1,0:T(8,128)S(1)}, f32[128,256]{1,0:T(8,128)S(1)}, f32[128,256]{1,0:T(8,128)S(1)}, f32[128,256]{1,0:T(8,128)S(1)}) custom-call(s32[51]{0:T(128)S(1)} %reshape.22.place_ref, bf16[512,16,256]{2,1,0:T(8,128)(2,1)S(1)} %get-tuple-element.80.x_ref, f32[264,512]{1,0:T(8,128)S(1)} %collective-permute-done.8.refs_0_.refs_8_, ...), custom_call_target="tpu_custom_call" | custom-call | flops 268435456 | bytes 6291456 | tf_op jit(solution)/shard_map/project/pallas_call | solution.py:272
  54.1 2.2 %collective-permute-done.11.refs_3_.refs_15_ = f32[128,512]{1,0:T(8,128)S(1)} collective-permute-done((f32[128,512]{1,0:T(8,128)S(1)}, f32[128,512]{1,0:T(8,128)S(1)}, u32[]{:S(2)}, u32[]{:S(2)}) %collective-permute-start.11) | collective-permute-done | bytes 262176 | tf_op jit(solution)/shard_map/ppermute | solution.py:594
  56.3 1.7 %collective-permute-start.14 = (f32[136,512]{1,0:T(8,128)S(1)}, f32[136,512]{1,0:T(8,128)S(1)}, u32[]{:S(2)}, u32[]{:S(2)}) collective-permute-start(f32[136,512]{1,0:T(8,128)S(1)} %collective-permute-done.10.refs_2_.refs_14_), channel_id=1, source_target_pairs={{0,8},{1,9},{2,10},{3,11},{4,12},{5,13},{6,14},{7,15},{8,0},{9,1},... | collective-permute-start | bytes 835592 | tf_op jit(solution)/shard_map/ppermute | solution.py:588
  58.1 4.4 %project.10 = (f32[128,256]{1,0:T(8,128)S(1)}, f32[128,256]{1,0:T(8,128)S(1)}, f32[128,256]{1,0:T(8,128)S(1)}, f32[128,256]{1,0:T(8,128)S(1)}) custom-call(s32[51]{0:T(128)S(1)} %reshape.22.place_ref, bf16[512,16,256]{2,1,0:T(8,128)(2,1)S(1)} %get-tuple-element.80.x_ref, f32[264,512]{1,0:T(8,128)S(1)} %collective-permute-done.12.refs_0_.refs_12_, ...), custom_call_target="tpu_custom_call" | custom-call | flops 201326592 | bytes 5767168 | tf_op jit(solution)/shard_map/project/pallas_call | solution.py:272
  62.5 2.9 %project.11 = (f32[128,256]{1,0:T(8,128)S(1)}, f32[128,256]{1,0:T(8,128)S(1)}) custom-call(s32[51]{0:T(128)S(1)} %reshape.22.place_ref, bf16[512,16,256]{2,1,0:T(8,128)(2,1)S(1)} %get-tuple-element.80.x_ref, f32[136,512]{1,0:T(8,128)S(1)} %collective-permute-done.14.refs_0_.refs_16_, f32[128,512]{1,0:T(8,128)S(1)} %collective-permute-done.15.refs_1_.refs_17_), custom_call_target="tpu_custom_call" | custom-call | flops 67108864 | bytes 4718592 | tf_op jit(solution)/shard_map/project/pallas_call | solution.py:272
  65.5 24.0 %apply.1 = f32[16,32768]{1,0:T(8,128)} custom-call(s32[51]{0:T(128)S(1)} %reshape.22.place_ref, f32[8,64,128]{2,1,0:T(8,128)S(1)} %get-tuple-element.83.coupling_ref, f32[8,512]{1,0:T(8,128)S(1)} %get-tuple-element.81.refs_0_, f32[512,512]{1,0:T(8,128)S(1)} %copy-done, f32[264,512]{1,0:T(8,128)S(1)} %collective-permute-done.refs_0_.refs_2_, ...), custom_call_target="tpu_custom_call" | custom-call | tf_op jit(solution)/shard_map/apply/pallas_call | solution.py:507
  (30 shorter events, 2.8 us)
Async XLA Ops:
  0.0 14.6 %copy-start = (f32[512,512]{1,0:T(8,128)S(1)}, f32[512,512]{1,0:T(8,128)}, u32[]{:S(2)}) copy-start(f32[512,512]{1,0:T(8,128)} %refs_1_.3) | copy-start | bytes 3145732
  0.0 0.8 copy-start.2
  0.8 0.7 copy-start.3
  2.5 15.0 %collective-permute-start = (f32[264,512]{1,0:T(8,128)S(1)}, f32[264,512]{1,0:T(8,128)S(1)}, u32[]{:S(2)}, u32[]{:S(2)}) collective-permute-start(f32[264,512]{1,0:T(8,128)S(1)} %get-tuple-element.79), channel_id=1, source_target_pairs={{0,2},{2,4},{4,6},{6,7},{7,5},{5,3},{3,1},{1,0},{8,10},{10,12},{12... | collective-permute-start | bytes 1622024 | tf_op jit(solution)/shard_map/ppermute | solution.py:567
  4.7 12.9 %collective-permute-start.1 = (f32[264,512]{1,0:T(8,128)S(1)}, f32[264,512]{1,0:T(8,128)S(1)}, u32[]{:S(2)}, u32[]{:S(2)}) collective-permute-start(f32[264,512]{1,0:T(8,128)S(1)} %get-tuple-element.79), channel_id=1, source_target_pairs={{2,0},{4,2},{6,4},{7,6},{5,7},{3,5},{1,3},{0,1},{10,8},{12,10},{14... | collective-permute-start | bytes 1622024 | tf_op jit(solution)/shard_map/ppermute | solution.py:568
  6.2 0.9 %copy-start.1 = (f32[8,8,768]{2,1,0:T(8,128)S(1)}, f32[8,8,768]{2,1,0:T(8,128)}, u32[]{:S(2)}) copy-start(f32[8,8,768]{2,1,0:T(8,128)} %param.12) | copy-start | bytes 589828
  17.6 13.9 %collective-permute-start.2 = (f32[264,512]{1,0:T(8,128)S(1)}, f32[264,512]{1,0:T(8,128)S(1)}, u32[]{:S(2)}, u32[]{:S(2)}) collective-permute-start(f32[264,512]{1,0:T(8,128)S(1)} %collective-permute-done.refs_0_.refs_2_), channel_id=1, source_target_pairs={{0,2},{2,4},{4,6},{6,7},{7,5},{5,3},{3,1},{1,0},{8,10},{10,12},{12... | collective-permute-start | bytes 1622024 | tf_op jit(solution)/shard_map/ppermute | solution.py:590
  19.1 12.3 %collective-permute-start.3 = (f32[264,512]{1,0:T(8,128)S(1)}, f32[264,512]{1,0:T(8,128)S(1)}, u32[]{:S(2)}, u32[]{:S(2)}) collective-permute-start(f32[264,512]{1,0:T(8,128)S(1)} %collective-permute-done.1.refs_1_.refs_3_), channel_id=1, source_target_pairs={{2,0},{4,2},{6,4},{7,6},{5,7},{3,5},{1,3},{0,1},{10,8},{12,10},{14... | collective-permute-start | bytes 1622024 | tf_op jit(solution)/shard_map/ppermute | solution.py:591
  20.1 11.3 %collective-permute-start.4 = (f32[264,512]{1,0:T(8,128)S(1)}, f32[264,512]{1,0:T(8,128)S(1)}, u32[]{:S(2)}, u32[]{:S(2)}) collective-permute-start(f32[264,512]{1,0:T(8,128)S(1)} %collective-permute-done.refs_0_.refs_2_), channel_id=1, source_target_pairs={{0,8},{1,9},{2,10},{3,11},{4,12},{5,13},{6,14},{7,15},{8,0},{9,1},... | collective-permute-start | bytes 1622024 | tf_op jit(solution)/shard_map/ppermute | solution.py:588
  21.7 9.8 %collective-permute-start.5 = (f32[264,512]{1,0:T(8,128)S(1)}, f32[264,512]{1,0:T(8,128)S(1)}, u32[]{:S(2)}, u32[]{:S(2)}) collective-permute-start(f32[264,512]{1,0:T(8,128)S(1)} %collective-permute-done.1.refs_1_.refs_3_), channel_id=1, source_target_pairs={{0,8},{1,9},{2,10},{3,11},{4,12},{5,13},{6,14},{7,15},{8,0},{9,1},... | collective-permute-start | bytes 1622024 | tf_op jit(solution)/shard_map/ppermute | solution.py:588
  31.5 11.5 %collective-permute-start.6 = (f32[264,512]{1,0:T(8,128)S(1)}, f32[264,512]{1,0:T(8,128)S(1)}, u32[]{:S(2)}, u32[]{:S(2)}) collective-permute-start(f32[264,512]{1,0:T(8,128)S(1)} %collective-permute-done.2.refs_2_.refs_6_), channel_id=1, source_target_pairs={{0,2},{2,4},{4,6},{6,7},{7,5},{5,3},{3,1},{1,0},{8,10},{10,12},{12... | collective-permute-start | bytes 1622024 | tf_op jit(solution)/shard_map/ppermute | solution.py:590
  31.8 12.4 %collective-permute-start.7 = (f32[264,512]{1,0:T(8,128)S(1)}, f32[264,512]{1,0:T(8,128)S(1)}, u32[]{:S(2)}, u32[]{:S(2)}) collective-permute-start(f32[264,512]{1,0:T(8,128)S(1)} %collective-permute-done.3.refs_3_.refs_7_), channel_id=1, source_target_pairs={{2,0},{4,2},{6,4},{7,6},{5,7},{3,5},{1,3},{0,1},{10,8},{12,10},{14... | collective-permute-start | bytes 1622024 | tf_op jit(solution)/shard_map/ppermute | solution.py:591
  33.0 11.2 %collective-permute-start.8 = (f32[264,512]{1,0:T(8,128)S(1)}, f32[264,512]{1,0:T(8,128)S(1)}, u32[]{:S(2)}, u32[]{:S(2)}) collective-permute-start(f32[264,512]{1,0:T(8,128)S(1)} %collective-permute-done.2.refs_2_.refs_6_), channel_id=1, source_target_pairs={{0,8},{1,9},{2,10},{3,11},{4,12},{5,13},{6,14},{7,15},{8,0},{9,1},... | collective-permute-start | bytes 1622024 | tf_op jit(solution)/shard_map/ppermute | solution.py:588
  35.8 8.3 %collective-permute-start.9 = (f32[264,512]{1,0:T(8,128)S(1)}, f32[264,512]{1,0:T(8,128)S(1)}, u32[]{:S(2)}, u32[]{:S(2)}) collective-permute-start(f32[264,512]{1,0:T(8,128)S(1)} %collective-permute-done.3.refs_3_.refs_7_), channel_id=1, source_target_pairs={{0,8},{1,9},{2,10},{3,11},{4,12},{5,13},{6,14},{7,15},{8,0},{9,1},... | collective-permute-start | bytes 1622024 | tf_op jit(solution)/shard_map/ppermute | solution.py:588
  44.1 12.2 %collective-permute-start.12 = (f32[264,512]{1,0:T(8,128)S(1)}, f32[264,512]{1,0:T(8,128)S(1)}, u32[]{:S(2)}, u32[]{:S(2)}) collective-permute-start(f32[264,512]{1,0:T(8,128)S(1)} %collective-permute-done.6.refs_2_.refs_10_), channel_id=1, source_target_pairs={{0,8},{1,9},{2,10},{3,11},{4,12},{5,13},{6,14},{7,15},{8,0},{9,1},... | collective-permute-start | bytes 1622024 | tf_op jit(solution)/shard_map/ppermute | solution.py:588
  47.5 8.8 %collective-permute-start.13 = (f32[264,512]{1,0:T(8,128)S(1)}, f32[264,512]{1,0:T(8,128)S(1)}, u32[]{:S(2)}, u32[]{:S(2)}) collective-permute-start(f32[264,512]{1,0:T(8,128)S(1)} %collective-permute-done.7.refs_3_.refs_11_), channel_id=1, source_target_pairs={{0,8},{1,9},{2,10},{3,11},{4,12},{5,13},{6,14},{7,15},{8,0},{9,1},... | collective-permute-start | bytes 1622024 | tf_op jit(solution)/shard_map/ppermute | solution.py:588
  47.6 8.7 %collective-permute-start.10 = (f32[136,512]{1,0:T(8,128)S(1)}, f32[136,512]{1,0:T(8,128)S(1)}, u32[]{:S(2)}, u32[]{:S(2)}) collective-permute-start(f32[136,512]{1,0:T(8,128)S(1)} %slice.6), channel_id=1, source_target_pairs={{0,2},{2,4},{4,6},{6,7},{7,5},{5,3},{3,1},{1,0},{8,10},{10,12},{12... | collective-permute-start | bytes 835592 | tf_op jit(solution)/shard_map/ppermute | solution.py:593
  49.1 7.2 %collective-permute-start.11 = (f32[128,512]{1,0:T(8,128)S(1)}, f32[128,512]{1,0:T(8,128)S(1)}, u32[]{:S(2)}, u32[]{:S(2)}) collective-permute-start(f32[128,512]{1,0:T(8,128)S(1)} %slice.7), channel_id=1, source_target_pairs={{2,0},{4,2},{6,4},{7,6},{5,7},{3,5},{1,3},{0,1},{10,8},{12,10},{14... | collective-permute-start | bytes 786440 | tf_op jit(solution)/shard_map/ppermute | solution.py:594
  56.3 6.2 %collective-permute-start.14 = (f32[136,512]{1,0:T(8,128)S(1)}, f32[136,512]{1,0:T(8,128)S(1)}, u32[]{:S(2)}, u32[]{:S(2)}) collective-permute-start(f32[136,512]{1,0:T(8,128)S(1)} %collective-permute-done.10.refs_2_.refs_14_), channel_id=1, source_target_pairs={{0,8},{1,9},{2,10},{3,11},{4,12},{5,13},{6,14},{7,15},{8,0},{9,1},... | collective-permute-start | bytes 835592 | tf_op jit(solution)/shard_map/ppermute | solution.py:588
  58.0 4.5 %collective-permute-start.15 = (f32[128,512]{1,0:T(8,128)S(1)}, f32[128,512]{1,0:T(8,128)S(1)}, u32[]{:S(2)}, u32[]{:S(2)}) collective-permute-start(f32[128,512]{1,0:T(8,128)S(1)} %collective-permute-done.11.refs_3_.refs_15_), channel_id=1, source_target_pairs={{0,8},{1,9},{2,10},{3,11},{4,12},{5,13},{6,14},{7,15},{8,0},{9,1},... | collective-permute-start | bytes 786440 | tf_op jit(solution)/shard_map/ppermute | solution.py:588
where the time goes:
time: 89.9 us; the launch traced here: 89.6 us
  Pallas kernels  55.1 us (61%)
  starting transfers between devices  17.4 us (19%)
  waiting for transfers between devices  12.9 us (14%)
  local copies, waits for them, and re-layouts  3.91 us (4%)
    pallas_call x1, Pallas kernels, apply(): pl.pallas_call(functools.partial(apply_kernel, nslab, slots, nsum, pieces...  24 us
    pallas_call x6, Pallas kernels, project(): pl.pallas_call(functools.partial(project_kernel, local, infos), out_shape...  22.7 us
    ppermute x2, waiting for transfers between devices, gather_and_project(): up = lax.ppermute(up, AXES, onward)  9.56 us
    ppermute x8, starting transfers between devices, gather_and_project(): near = [lax.ppermute(up, AXES, sibling), lax.ppermute(down, AXES, sibling)]  9.53 us
    pallas_call x1, Pallas kernels, split_bands(): pl.pallas_call(functools.partial(split_bands_kernel, natoms // nslab), gr...  7.44 us
    unnamed x8, local copies, waits for them, and re-layouts  2.38 us
    ppermute x2, starting transfers between devices, gather_and_project(): down = lax.ppermute(down, AXES, backward)  2.25 us
    ppermute x1, starting transfers between devices, gather_and_project(): up = lax.ppermute(mine, AXES, onward)  2.18 us
  transfers between devices with their start and end apart: 16, of which 4 were waited for; matrix products, arithmetic and copies ran while one was open for 2% of the time, Pallas kernels for 30%

commit v1 on v0

--- a/solution.py
+++ b/solution.py
@@ -130,16 +130,17 @@
     return lax.div(jnp.clip(live - start, 0, length) + (GROUP - 1), GROUP)
 
 
-def begin_kernel(natoms, lanes, atom_ref, box_ref, projector_ref, info_ref, mine_ref, info_sem, half_sem):
+def begin_kernel(
+    natoms, lanes, atom_ref, box_ref, projector_ref, info_ref, first_ref, second_ref, sem
+):
     nslab = lax.axis_size("slab")
-    half = mine_ref.shape[0] - INFO
-    core = lax.rem(lax.axis_index("band"), 2)
-    copy = pltpu.make_async_copy(
-        projector_ref.at[pl.ds(pl.multiple_of(core * half, GROUP), half), :],
-        mine_ref.at[pl.ds(INFO, half), :],
-        half_sem,
-    )
-    copy.start()
+    count = second_ref.shape[0]
+    start = lax.rem(lax.axis_index("band"), 2) * (2 * count)
+    copies = []
+    for k, out in enumerate((first_ref.at[pl.ds(INFO, count), :], second_ref)):
+        rows = pl.ds(pl.multiple_of(start + k * count, GROUP), count)
+        copies.append(pltpu.make_async_copy(projector_ref.at[rows, :], out, sem.at[k]))
+        copies[-1].start()
     atom_dev = natoms // nslab
     below = lax.rem(lax.axis_index("slab") + nslab - 1, nslab) * atom_dev
     atom = atom_ref[...]
@@ -152,10 +153,11 @@
     info_ref[0:1, 0:slots] = box_ref[...].astype(jnp.float32)
     info_ref[1:2, 0:slots] = jnp.broadcast_to(live, (1, slots))
     info_ref[2:3, 0:slots] = jnp.where(atom >= 0, column, -1).astype(jnp.float32)
-    head = pltpu.make_async_copy(info_ref, mine_ref.at[pl.ds(0, INFO), :], info_sem)
+    head = pltpu.make_async_copy(info_ref, first_ref.at[pl.ds(0, INFO), :], sem.at[2])
     head.start()
     head.wait()
-    copy.wait()
+    for c in copies:
+        c.wait()
 
 
 def begin(slot_atom, slot_box, projectors, natoms, lanes):
@@ -164,11 +166,12 @@
         functools.partial(begin_kernel, natoms, lanes),
         out_shape=[
             jax.ShapeDtypeStruct((INFO, depth), jnp.float32),
-            jax.ShapeDtypeStruct((INFO + slots // 2, depth), jnp.float32),
+            jax.ShapeDtypeStruct((INFO + slots // 4, depth), jnp.float32),
+            jax.ShapeDtypeStruct((slots // 4, depth), jnp.float32),
         ],
         in_specs=[VMEM, VMEM, ANY],
-        out_specs=[VMEM, ANY],
-        scratch_shapes=[pltpu.SemaphoreType.DMA(()), pltpu.SemaphoreType.DMA(())],
+        out_specs=[VMEM, ANY, ANY],
+        scratch_shapes=[pltpu.SemaphoreType.DMA((3,))],
         compiler_params=params(8 * MIB),
         name="begin",
     )(
@@ -182,9 +185,15 @@
     return jnp.concatenate([info[0:1, :] + first, info[1:2, 0:128]], axis=1).astype(jnp.int32)
 
 
+def in_units(pieces):
+    order = sorted({p.unit for p in pieces})
+    return [[i for i, p in enumerate(pieces) if p.unit == u] for u in order]
+
+
 def project_kernel(pieces, infos, place_ref, x_ref, *refs):
-    arrays = refs[: -len(pieces) - 4]
-    outs = refs[-len(pieces) - 4 : -4]
+    units = in_units(pieces)
+    arrays = refs[: -len(units) - 4]
+    outs = refs[-len(units) - 4 : -4]
     whole, proj, table, sem = refs[-4:]
     for k, index in enumerate(infos):
         whole[k : k + 1, :] = scalar_row(arrays[index][0:INFO, :], 0)
@@ -229,18 +238,17 @@
 
         lax.fori_loop(0, lax.div(count + (UNROLL - 1), UNROLL), step, 0)
 
-    for which, (p, out) in enumerate(zip(pieces, outs)):
-        start = place_ref[3 * p.index + 1]
-        columns = arrays[p.info][2:3, :]
+    for unit, out in zip(units, outs):
+        head = pieces[unit[0]]
+        start = place_ref[3 * head.index + 1]
+        columns = arrays[head.info][2:3, :]
         columns = pltpu.roll(columns, lax.rem(columns.shape[1] - start, columns.shape[1]), 1)
-        nchunk = (p.rows // GROUP + chunk - 1) // chunk
+        tiles = [proj[i, g] for i in unit for g in range(pieces[i].rows // GROUP)]
+        nchunk = len(tiles) // chunk
         value = jnp.concatenate(
             [
                 jnp.concatenate(
-                    swap_blocks(
-                        [proj[which, k * chunk + i] for i in range(chunk)], lane_block, width
-                    ),
-                    axis=0,
+                    swap_blocks(tiles[k * chunk : (k + 1) * chunk], lane_block, width), axis=0
                 )
                 for k in range(nchunk)
             ],
@@ -263,8 +271,9 @@
         p._replace(array=used.index(p.array), info=used.index(p.info)) for p in pieces
     ]
     infos = sorted({p.info for p in local})
+    units = in_units(pieces)
     shapes = [
-        jax.ShapeDtypeStruct((channel * x.shape[1], 2 * lanes), jnp.float32) for p in pieces
+        jax.ShapeDtypeStruct((channel * x.shape[1], 2 * lanes), jnp.float32) for _ in units
     ]
     size = sum(p.rows for p in pieces) * arrays[0].shape[1]
     table = (round_up(len(infos), 8), arrays[0].shape[1] + 128)
@@ -273,7 +282,7 @@
         functools.partial(project_kernel, local, infos),
         out_shape=shapes,
         in_specs=[SMEM, VMEM] + [VMEM] * len(used),
-        out_specs=[VMEM] * len(pieces),
+        out_specs=[VMEM] * len(units),
         scratch_shapes=[
             pltpu.VMEM(table, jnp.int32),
             pltpu.VMEM((len(pieces), groups, x.shape[1], channel * GROUP), jnp.float32),
@@ -315,21 +324,26 @@
 
 
 def apply_kernel(nslab, slots, nsum, pieces, infos, place_ref, coupling_ref, *refs):
-    npiece = len(pieces)
     proj, loaded, parts, beta, done, masks, info, whole, table = refs[-13:-4]
     sums = refs[-13 - nsum : -13]
     beta_sem, proj_sem, info_sem, out_sem = refs[-4:]
     base = len(refs) - 14 - nsum
+    units = in_units(pieces)
+    nunit = len(units)
     out_ref = refs[base]
-    projections = refs[base - npiece : base]
-    arrays = refs[: base - npiece]
+    projections = refs[base - nunit : base]
+    arrays = refs[: base - nunit]
     groups = slots // GROUP
     rows, width = proj.shape[1], proj.shape[2]
     channel = width // GROUP
     lanes = parts.shape[2] // 2
     boxes = out_ref.shape[1] // BOXPTS // nslab
     chunk = width // GROUP
-    info_copies, copies, beta_copies = [], [], []
+    info_copies, beta_copies = [], []
+    copies = [
+        pltpu.make_async_copy(projections[i], loaded.at[i % loaded.shape[0]], proj_sem.at[i])
+        for i in range(nunit)
+    ]
     for i, (array, index) in enumerate(infos):
         slab = place_ref[3 * index]
         info_copies.append(
@@ -337,10 +351,6 @@
         )
     for i, p in enumerate(pieces):
         slab, start = place_ref[3 * p.index], place_ref[3 * p.index + 1]
-        j = i % loaded.shape[0]
-        copies.append(
-            pltpu.make_async_copy(projections[i], loaded.at[j], proj_sem.at[i])
-        )
         first = pl.multiple_of(slab * slots + start, GROUP)
         beta_copies.append(
             pltpu.make_async_copy(
@@ -363,15 +373,15 @@
         whole[slab : slab + 1, :] = scalar_row(info[slab], float(slab * boxes))
     to_scalars = pltpu.make_async_copy(whole, table, info_sem.at[0])
     to_scalars.start()
-    for first in range(0, npiece, loaded.shape[0]):
-        wave = range(first, min(first + loaded.shape[0], npiece))
+    for first in range(0, nunit, loaded.shape[0]):
+        wave = range(first, min(first + loaded.shape[0], nunit))
         for i in wave:
             if first > 0:
                 copies[i].start()
         for i in wave:
             copies[i].wait()
         for i in wave:
-            slab = place_ref[3 * pieces[i].index]
+            slab = place_ref[3 * pieces[units[i][0]].index]
             parts[slab] = parts[slab] + loaded[i % loaded.shape[0]]
 
     lane_block = lax.broadcasted_iota(jnp.int32, (rows, width), 1) // GROUP
@@ -488,7 +498,9 @@
     buffers = [pltpu.VMEM((ngrid // BOXPTS, rows, 128), jnp.float32) for _ in range(nsum)]
     buffers += [
         pltpu.VMEM((nslab * slots // GROUP, rows, width), jnp.float32),
-        pltpu.VMEM((len(pieces) if len(pieces) <= 24 else 1,) + projections[0].shape, jnp.float32),
+        pltpu.VMEM(
+            (len(projections) if len(projections) <= 24 else 1,) + projections[0].shape, jnp.float32
+        ),
         pltpu.VMEM((nslab,) + projections[0].shape, jnp.float32),
         pltpu.VMEM((nslab * slots, depth), jnp.float32),
         pltpu.VMEM((2, rows, ngrid // nslab), jnp.float32),
@@ -500,14 +512,14 @@
     scratch = buffers + [
         pltpu.SMEM((nslab, depth + 128), jnp.int32),
         pltpu.SemaphoreType.DMA((len(pieces),)),
-        pltpu.SemaphoreType.DMA((len(pieces),)),
+        pltpu.SemaphoreType.DMA((len(projections),)),
         pltpu.SemaphoreType.DMA((len(infos),)),
         pltpu.SemaphoreType.DMA((2,)),
     ]
     return pl.pallas_call(
         functools.partial(apply_kernel, nslab, slots, nsum, pieces, infos),
         out_shape=jax.ShapeDtypeStruct((rows, ngrid), jnp.float32),
-        in_specs=[SMEM, VMEM] + [ANY] * (len(arrays) + len(pieces)),
+        in_specs=[SMEM, VMEM] + [ANY] * (len(arrays) + len(projections)),
         out_specs=ANY,
         scratch_shapes=scratch,
         compiler_params=params(min(need + 4 * MIB, 63 * MIB)),
@@ -515,10 +527,10 @@
     )(place, coupling, *arrays, *projections)
 
 
-Piece = collections.namedtuple("Piece", ["array", "offset", "rows", "info", "index"])
-
-
-def gather_and_project(projectors, described, mine, split, lanes, nband, nslab):
+Piece = collections.namedtuple("Piece", ["array", "offset", "rows", "info", "index", "unit"])
+
+
+def gather_and_project(projectors, described, first, second, split, lanes, nband, nslab):
     slots = projectors.shape[0]
     order, at = cycle_tables(nslab)
     half = slots // 2
@@ -533,11 +545,11 @@
     sibling = [(b * nslab + s, (b ^ 1) * nslab + s) for b in range(nband) for s in range(nslab)]
 
     where = [(0, 0, None)]
-    for step in range(1, reach):
-        where += [(1 - step, 0, True), (step - 1, 0, True)] if step > 1 else []
-        where += [(-step, 0, False), (step, 0, False)]
-    where += [(1 - reach, 0, True), (reach - 1, 0, True)]
-    where += [(reach, 0, False), (reach, quarter, False), (reach, 0, True), (reach, quarter, True)]
+    for step in range(1, reach + 1):
+        for distance, other in ((1 - step, True), (step - 1, True), (-step, False), (step, False)):
+            if distance != 0 and distance != reach:
+                where += [(distance, 0, other), (distance, quarter, other)]
+    where += [(reach, 0, True), (reach, quarter, True)]
     boxes = split.shape[0] // nslab
 
     def entry(core, slab, distance, start, other):
@@ -554,18 +566,18 @@
 
     arrays, pieces, infos, projections = [described, projectors], [], [(0, 0)], []
 
-    def add(array, info=None):
-        arrays.append(array)
-        own = len(arrays) - 1
-        offset = INFO if info is None else 0
-        pieces.append(
-            Piece(own, offset, array.shape[0] - offset, own if info is None else info, len(pieces))
-        )
-        return own
-
-    pieces.append(Piece(1, 0, slots, 0, 0))
-    up = lax.ppermute(mine, AXES, onward)
-    down = lax.ppermute(mine, AXES, backward)
+    pieces.append(Piece(1, 0, slots, 0, 0, 0))
+    units = 1
+
+    def add(one, two):
+        nonlocal units
+        arrays.extend([one, two])
+        index, info = len(pieces), len(arrays) - 2
+        pieces.append(Piece(info, INFO, one.shape[0] - INFO, info, index, units))
+        pieces.append(Piece(info + 1, 0, two.shape[0], info, index + 1, units))
+        units += 1
+        return info, index
+
     done = 0
 
     def project_new():
@@ -573,30 +585,38 @@
         projections.extend(project(arrays, pieces[done:], place, split, lanes))
         done = len(pieces)
 
-    project_new()
-    up, down, projections, place = lax.optimization_barrier((up, down, projections, place))
-    projections = list(projections)
     near = []
-    for step in range(1, reach + 1):
-        last = step == reach
-        for array in near:
-            add(array)
-        for array in (up,) if last else (up, down):
-            infos.append((add(array), len(pieces) - 1))
-        if last:
-            add(down, len(arrays) - 1)
-        near = [lax.ppermute(up, AXES, sibling), lax.ppermute(down, AXES, sibling)]
+    up, down = (first, second), (first, second)
+    for step in range(reach + 1):
+        for pair in near:
+            add(*pair)
+        if step == 0:
+            near = []
+        elif step < reach:
+            infos.extend([add(*up), add(*down)])
+            near = [up, down]
+        else:
+            infos.append(add(up[0], down[1]))
+            near = [(up[0], down[1])]
+        near = [tuple(lax.ppermute(x, AXES, sibling) for x in pair) for pair in near]
         if step + 1 < reach:
-            up = lax.ppermute(up, AXES, onward)
-            down = lax.ppermute(down, AXES, backward)
-        elif not last:
-            up = lax.ppermute(up[: INFO + quarter], AXES, onward)
-            down = lax.ppermute(down[INFO + quarter :], AXES, backward)
+            ahead = [lax.ppermute(x, AXES, onward) for x in up]
+            ahead += [lax.ppermute(x, AXES, backward) for x in down]
+        elif step + 1 == reach:
+            ahead = [lax.ppermute(up[0], AXES, onward), lax.ppermute(down[1], AXES, backward)]
+        else:
+            ahead = []
         project_new()
-        up, down, near, projections = lax.optimization_barrier((up, down, near, projections))
-        near, projections = list(near), list(projections)
-    add(near[0])
-    add(near[1], len(arrays) - 1)
+        if step + 1 < reach:
+            ones, projections = lax.optimization_barrier((ahead[0::2], projections))
+            twos, near, projections = lax.optimization_barrier((ahead[1::2], near, projections))
+            up, down = (ones[0], twos[0]), (ones[1], twos[1])
+        elif step + 1 == reach:
+            ahead, near, projections = lax.optimization_barrier((ahead, near, projections))
+            up, down = (ahead[0], None), (None, ahead[1])
+        projections = list(projections)
+    for pair in near:
+        add(*pair)
     project_new()
     return arrays, pieces, infos, projections, place
 
@@ -609,7 +629,7 @@
     slots = slot_atom.shape[0]
     lanes = round_up(atom_dev, 128)
 
-    described, mine = begin(slot_atom, slot_box, projectors, natoms, lanes)
+    described, first, second = begin(slot_atom, slot_box, projectors, natoms, lanes)
     rows = nblock * band_local
     padded = round_up(rows, GROUP)
     x = bands.reshape(rows, ngrid)
@@ -617,7 +637,7 @@
         x = jnp.pad(x, ((0, padded - rows), (0, 0)))
     split, masked = split_bands(x, coupling, channels, nslab, lanes)
     arrays, pieces, infos, projections, place = gather_and_project(
-        projectors, described, mine, split, lanes, nband, nslab
+        projectors, described, first, second, split, lanes, nband, nslab
     )
     out = apply(arrays, pieces, infos, projections, place, masked, nslab, slots, padded, ngrid)
     return out[:rows].reshape(nblock, band_local, ngrid)

time: 89.9 us -> 108 us (1.20); the launches traced: 89.6 us -> 106 us
  starting transfers between devices: 17.4 us -> 28 us
  waiting for transfers between devices: 12.9 us -> 21.2 us
  Pallas kernels: 55.1 us -> 52.9 us
    ppermute x16 -> x28, starting transfers between devices: 17.4 us -> 28 us  [the longest x14 14.9 us: gather_and_project(): lax.ppermute(x, AXES, sibling)]
    ppermute x16 -> x28, waiting for transfers between devices: 12.9 us -> 21.2 us  [the longest x6 16.2 us: gather_and_project(): ahead = [lax.ppermute(x, AXES, onward) for x in up]]
    pallas_call x1, Pallas kernels: 24 us -> 22.5 us  [apply(): pl.pallas_call(functools.partial(apply_kernel, nslab, slots, nsum, pieces...]
  transfers between devices with their start and end apart: 16 -> 28, of which waited for: 4 -> 4; matrix products, arithmetic and copies ran while one was open for 2% -> 1% of each run, Pallas kernels for 30% -> 25%
where the time goes in v1:
time: 108 us; the launch traced here: 106 us
  Pallas kernels  52.9 us (49%)
  starting transfers between devices  28 us (26%)
  waiting for transfers between devices  21.2 us (20%)
  local copies, waits for them, and re-layouts  3.89 us (4%)
    pallas_call x1, Pallas kernels, apply(): pl.pallas_call(functools.partial(apply_kernel, nslab, slots, nsum, pieces...  22.5 us
    pallas_call x6, Pallas kernels, project(): pl.pallas_call(functools.partial(project_kernel, local, infos), out_shape...  21.9 us
    ppermute x6, waiting for transfers between devices, gather_and_project(): ahead = [lax.ppermute(x, AXES, onward) for x in up]  16.2 us
    ppermute x14, starting transfers between devices, gather_and_project(): lax.ppermute(x, AXES, sibling)  14.9 us
    pallas_call x1, Pallas kernels, split_bands(): pl.pallas_call(functools.partial(split_bands_kernel, natoms // nslab), gr...  7.44 us
    ppermute x6, starting transfers between devices, gather_and_project(): ahead += [lax.ppermute(x, AXES, backward) for x in down]  6.38 us
    ppermute x6, starting transfers between devices, gather_and_project(): ahead = [lax.ppermute(x, AXES, onward) for x in up]  5.16 us
    ppermute x1, waiting for transfers between devices, gather_and_project(): lax.ppermute(down[1], AXES, backward)  3.73 us
  transfers between devices with their start and end apart: 28, of which 4 were waited for; matrix products, arithmetic and copies ran while one was open for 1% of the time, Pallas kernels for 25%

profile of v1, /device:TPU:1, one launch (start us, length us, event | category | flops | bytes accessed | tf_op | source)
XLA Modules:
  0.0 106.4 jit_solution(3393695290779796795)
XLA Ops:
  2.5 2.2 %collective-permute-start = (f32[136,512]{1,0:T(8,128)S(1)}, f32[136,512]{1,0:T(8,128)S(1)}, u32[]{:S(2)}, u32[]{:S(2)}) collective-permute-start(f32[136,512]{1,0:T(8,128)S(1)} %get-tuple-element.84), channel_id=1, source_target_pairs={{0,2},{2,4},{4,6},{6,7},{7,5},{5,3},{3,1},{1,0},{8,10},{10,12},{12... | collective-permute-start | bytes 835592 | tf_op jit(solution)/shard_map/ppermute | solution.py:603
  4.7 1.5 %collective-permute-start.2 = (f32[128,512]{1,0:T(8,128)S(1)}, f32[128,512]{1,0:T(8,128)S(1)}, u32[]{:S(2)}, u32[]{:S(2)}) collective-permute-start(f32[128,512]{1,0:T(8,128)S(1)} %get-tuple-element.87), channel_id=1, source_target_pairs={{0,2},{2,4},{4,6},{6,7},{7,5},{5,3},{3,1},{1,0},{8,10},{10,12},{12... | collective-permute-start | bytes 786440 | tf_op jit(solution)/shard_map/ppermute | solution.py:603
  8.6 7.4 %split_bands.1 = (bf16[512,16,256]{2,1,0:T(8,128)(2,1)S(1)}, f32[8,64,128]{2,1,0:T(8,128)S(1)}) custom-call(f32[16,32768]{1,0:T(8,128)} %bitcast.8, f32[64,768]{1,0:T(8,128)S(1)} %bitcast.5, s32[8,768]{1,0:T(8,128)S(1)} %broadcast_in_dim.2.channels_ref), custom_call_target="tpu_custom_call" | custom-call | flops 4194304 | bytes 6291456 | tf_op jit(solution)/shard_map/split_bands/pallas_call | solution.py:84
  16.1 3.0 %project.6.refs_30_ = f32[128,256]{1,0:T(8,128)S(1)} custom-call(s32[87]{0:T(128)S(1)} %reshape.20.place_ref, bf16[512,16,256]{2,1,0:T(8,128)(2,1)S(1)} %get-tuple-element.85.x_ref, f32[8,512]{1,0:T(8,128)S(1)} %get-tuple-element.83.refs_0_, f32[512,512]{1,0:T(8,128)S(1)} %copy-done), custom_call_target="tpu_custom_call" | custom-call | flops 134217728 | bytes 5242880 | tf_op jit(solution)/shard_map/project/pallas_call | solution.py:281
  21.5 2.6 %collective-permute-start.6 = (f32[136,512]{1,0:T(8,128)S(1)}, f32[136,512]{1,0:T(8,128)S(1)}, u32[]{:S(2)}, u32[]{:S(2)}) collective-permute-start(f32[136,512]{1,0:T(8,128)S(1)} %collective-permute-done.refs_0_.refs_2_), channel_id=1, source_target_pairs={{0,8},{1,9},{2,10},{3,11},{4,12},{5,13},{6,14},{7,15},{8,0},{9,1},... | collective-permute-start | bytes 835592 | tf_op jit(solution)/shard_map/ppermute | solution.py:601
  24.2 7.7 %collective-permute-done.4.refs_5_.refs_11_ = f32[128,512]{1,0:T(8,128)S(1)} collective-permute-done((f32[128,512]{1,0:T(8,128)S(1)}, f32[128,512]{1,0:T(8,128)S(1)}, u32[]{:S(2)}, u32[]{:S(2)}) %collective-permute-start.4) | collective-permute-done | bytes 262176 | tf_op jit(solution)/shard_map/ppermute | solution.py:603
  31.8 1.8 %collective-permute-start.5 = (f32[128,512]{1,0:T(8,128)S(1)}, f32[128,512]{1,0:T(8,128)S(1)}, u32[]{:S(2)}, u32[]{:S(2)}) collective-permute-start(f32[128,512]{1,0:T(8,128)S(1)} %collective-permute-done.3.refs_3_.refs_5_), channel_id=1, source_target_pairs={{2,0},{4,2},{6,4},{7,6},{5,7},{3,5},{1,3},{0,1},{10,8},{12,10},{14... | collective-permute-start | bytes 786440 | tf_op jit(solution)/shard_map/ppermute | solution.py:604
  33.7 2.7 %collective-permute-start.7 = (f32[128,512]{1,0:T(8,128)S(1)}, f32[128,512]{1,0:T(8,128)S(1)}, u32[]{:S(2)}, u32[]{:S(2)}) collective-permute-start(f32[128,512]{1,0:T(8,128)S(1)} %collective-permute-done.2.refs_1_.refs_3_), channel_id=1, source_target_pairs={{0,8},{1,9},{2,10},{3,11},{4,12},{5,13},{6,14},{7,15},{8,0},{9,1},... | collective-permute-start | bytes 786440 | tf_op jit(solution)/shard_map/ppermute | solution.py:601
  36.5 2.5 %project.7 = (f32[128,256]{1,0:T(8,128)S(1)}, f32[128,256]{1,0:T(8,128)S(1)}) custom-call(s32[87]{0:T(128)S(1)} %reshape.20.place_ref, bf16[512,16,256]{2,1,0:T(8,128)(2,1)S(1)} %get-tuple-element.85.x_ref, f32[136,512]{1,0:T(8,128)S(1)} %collective-permute-done.refs_0_.refs_2_, f32[128,512]{1,0:T(8,128)S(1)} %collective-permute-done.2.refs_1_.refs_3_, ...), custom_call_target="tpu_custom_call" | custom-call | flops 134217728 | bytes 5242880 | tf_op jit(solution)/shard_map/project/pallas_call | solution.py:281
  39.0 2.0 %collective-permute-start.19 = (f32[136,512]{1,0:T(8,128)S(1)}, f32[136,512]{1,0:T(8,128)S(1)}, u32[]{:S(2)}, u32[]{:S(2)}) collective-permute-start(f32[136,512]{1,0:T(8,128)S(1)} %collective-permute-done.11.refs_6_.refs_12_), channel_id=1, source_target_pairs={{2,0},{4,2},{6,4},{7,6},{5,7},{3,5},{1,3},{0,1},{10,8},{12,10},{14... | collective-permute-start | bytes 835592 | tf_op jit(solution)/shard_map/ppermute | solution.py:604
  41.1 2.3 %collective-permute-start.14 = (f32[136,512]{1,0:T(8,128)S(1)}, f32[136,512]{1,0:T(8,128)S(1)}, u32[]{:S(2)}, u32[]{:S(2)}) collective-permute-start(f32[136,512]{1,0:T(8,128)S(1)} %collective-permute-done.10.refs_4_.refs_10_), channel_id=1, source_target_pairs={{0,8},{1,9},{2,10},{3,11},{4,12},{5,13},{6,14},{7,15},{8,0},{9,1},... | collective-permute-start | bytes 835592 | tf_op jit(solution)/shard_map/ppermute | solution.py:601
  43.5 8.6 %collective-permute-done.12.refs_5_.refs_19_ = f32[128,512]{1,0:T(8,128)S(1)} collective-permute-done((f32[128,512]{1,0:T(8,128)S(1)}, f32[128,512]{1,0:T(8,128)S(1)}, u32[]{:S(2)}, u32[]{:S(2)}) %collective-permute-start.12) | collective-permute-done | bytes 262176 | tf_op jit(solution)/shard_map/ppermute | solution.py:603
  52.1 2.2 %collective-permute-start.15 = (f32[128,512]{1,0:T(8,128)S(1)}, f32[128,512]{1,0:T(8,128)S(1)}, u32[]{:S(2)}, u32[]{:S(2)}) collective-permute-start(f32[128,512]{1,0:T(8,128)S(1)} %collective-permute-done.4.refs_5_.refs_11_), channel_id=1, source_target_pairs={{0,8},{1,9},{2,10},{3,11},{4,12},{5,13},{6,14},{7,15},{8,0},{9,1},... | collective-permute-start | bytes 786440 | tf_op jit(solution)/shard_map/ppermute | solution.py:601
  54.2 1.5 %collective-permute-start.13 = (f32[128,512]{1,0:T(8,128)S(1)}, f32[128,512]{1,0:T(8,128)S(1)}, u32[]{:S(2)}, u32[]{:S(2)}) collective-permute-start(f32[128,512]{1,0:T(8,128)S(1)} %collective-permute-done.5.refs_7_.refs_13_), channel_id=1, source_target_pairs={{2,0},{4,2},{6,4},{7,6},{5,7},{3,5},{1,3},{0,1},{10,8},{12,10},{14... | collective-permute-start | bytes 786440 | tf_op jit(solution)/shard_map/ppermute | solution.py:604
  56.0 5.0 %project.8 = (f32[128,256]{1,0:T(8,128)S(1)}, f32[128,256]{1,0:T(8,128)S(1)}, f32[128,256]{1,0:T(8,128)S(1)}, f32[128,256]{1,0:T(8,128)S(1)}) custom-call(s32[87]{0:T(128)S(1)} %reshape.20.place_ref, bf16[512,16,256]{2,1,0:T(8,128)(2,1)S(1)} %get-tuple-element.85.x_ref, f32[136,512]{1,0:T(8,128)S(1)} %collective-permute-done.6.refs_0_.refs_6_, ...), custom_call_target="tpu_custom_call" | custom-call | flops 268435456 | bytes 6291456 | tf_op jit(solution)/shard_map/project/pallas_call | solution.py:281
  61.0 1.2 %collective-permute-done.13.refs_7_.refs_21_ = f32[128,512]{1,0:T(8,128)S(1)} collective-permute-done((f32[128,512]{1,0:T(8,128)S(1)}, f32[128,512]{1,0:T(8,128)S(1)}, u32[]{:S(2)}, u32[]{:S(2)}) %collective-permute-start.13) | collective-permute-done | bytes 262176 | tf_op jit(solution)/shard_map/ppermute | solution.py:604
  62.2 1.5 %collective-permute-start.21 = (f32[128,512]{1,0:T(8,128)S(1)}, f32[128,512]{1,0:T(8,128)S(1)}, u32[]{:S(2)}, u32[]{:S(2)}) collective-permute-start(f32[128,512]{1,0:T(8,128)S(1)} %collective-permute-done.13.refs_7_.refs_21_), channel_id=1, source_target_pairs={{2,0},{4,2},{6,4},{7,6},{5,7},{3,5},{1,3},{0,1},{10,8},{12,10},{14... | collective-permute-start | bytes 786440 | tf_op jit(solution)/shard_map/ppermute | solution.py:606
  63.7 1.3 %collective-permute-start.22 = (f32[136,512]{1,0:T(8,128)S(1)}, f32[136,512]{1,0:T(8,128)S(1)}, u32[]{:S(2)}, u32[]{:S(2)}) collective-permute-start(f32[136,512]{1,0:T(8,128)S(1)} %collective-permute-done.18.refs_4_.refs_18_), channel_id=1, source_target_pairs={{0,8},{1,9},{2,10},{3,11},{4,12},{5,13},{6,14},{7,15},{8,0},{9,1},... | collective-permute-start | bytes 835592 | tf_op jit(solution)/shard_map/ppermute | solution.py:601
  65.6 3.7 %collective-permute-done.21.refs_5_.refs_27_ = f32[128,512]{1,0:T(8,128)S(1)} collective-permute-done((f32[128,512]{1,0:T(8,128)S(1)}, f32[128,512]{1,0:T(8,128)S(1)}, u32[]{:S(2)}, u32[]{:S(2)}) %collective-permute-start.21) | collective-permute-done | bytes 262176 | tf_op jit(solution)/shard_map/ppermute | solution.py:606
  69.3 1.7 %collective-permute-start.25 = (f32[128,512]{1,0:T(8,128)S(1)}, f32[128,512]{1,0:T(8,128)S(1)}, u32[]{:S(2)}, u32[]{:S(2)}) collective-permute-start(f32[128,512]{1,0:T(8,128)S(1)} %collective-permute-done.13.refs_7_.refs_21_), channel_id=1, source_target_pairs={{0,8},{1,9},{2,10},{3,11},{4,12},{5,13},{6,14},{7,15},{8,0},{9,1},... | collective-permute-start | bytes 786440 | tf_op jit(solution)/shard_map/ppermute | solution.py:601
  71.0 4.1 %project.9 = (f32[128,256]{1,0:T(8,128)S(1)}, f32[128,256]{1,0:T(8,128)S(1)}, f32[128,256]{1,0:T(8,128)S(1)}, f32[128,256]{1,0:T(8,128)S(1)}) custom-call(s32[87]{0:T(128)S(1)} %reshape.20.place_ref, bf16[512,16,256]{2,1,0:T(8,128)(2,1)S(1)} %get-tuple-element.85.x_ref, f32[136,512]{1,0:T(8,128)S(1)} %collective-permute-done.14.refs_0_.refs_14_, ...), custom_call_target="tpu_custom_call" | custom-call | flops 268435456 | bytes 6291456 | tf_op jit(solution)/shard_map/project/pallas_call | solution.py:281
  76.3 4.2 %project.10 = (f32[128,256]{1,0:T(8,128)S(1)}, f32[128,256]{1,0:T(8,128)S(1)}, f32[128,256]{1,0:T(8,128)S(1)}) custom-call(s32[87]{0:T(128)S(1)} %reshape.20.place_ref, bf16[512,16,256]{2,1,0:T(8,128)(2,1)S(1)} %get-tuple-element.85.x_ref, f32[136,512]{1,0:T(8,128)S(1)} %collective-permute-done.22.refs_0_.refs_22_, ...), custom_call_target="tpu_custom_call" | custom-call | flops 201326592 | bytes 5767168 | tf_op jit(solution)/shard_map/project/pallas_call | solution.py:281
  80.6 3.1 %project.11.refs_44_ = f32[128,256]{1,0:T(8,128)S(1)} custom-call(s32[87]{0:T(128)S(1)} %reshape.20.place_ref, bf16[512,16,256]{2,1,0:T(8,128)(2,1)S(1)} %get-tuple-element.85.x_ref, f32[136,512]{1,0:T(8,128)S(1)} %collective-permute-done.26.refs_0_.refs_28_, f32[128,512]{1,0:T(8,128)S(1)} %collective-permute-done.27.refs_1_.refs_29_), custom_call_target="tpu_custom_call" | custom-call | flops 67108864 | bytes 4718592 | tf_op jit(solution)/shard_map/project/pallas_call | solution.py:281
  83.7 22.5 %apply.1 = f32[16,32768]{1,0:T(8,128)} custom-call(s32[87]{0:T(128)S(1)} %reshape.20.place_ref, f32[8,64,128]{2,1,0:T(8,128)S(1)} %get-tuple-element.82.coupling_ref, f32[8,512]{1,0:T(8,128)S(1)} %get-tuple-element.83.refs_0_, f32[512,512]{1,0:T(8,128)S(1)} %copy-done, f32[136,512]{1,0:T(8,128)S(1)} %collective-permute-done.refs_0_.refs_2_, ...), custom_call_target="tpu_custom_call" | custom-call | tf_op jit(solution)/shard_map/apply/pallas_call | solution.py:519
  (52 shorter events, 9.7 us)
Async XLA Ops:
  2.5 16.5 %collective-permute-start = (f32[136,512]{1,0:T(8,128)S(1)}, f32[136,512]{1,0:T(8,128)S(1)}, u32[]{:S(2)}, u32[]{:S(2)}) collective-permute-start(f32[136,512]{1,0:T(8,128)S(1)} %get-tuple-element.84), channel_id=1, source_target_pairs={{0,2},{2,4},{4,6},{6,7},{7,5},{5,3},{3,1},{1,0},{8,10},{10,12},{12... | collective-permute-start | bytes 835592 | tf_op jit(solution)/shard_map/ppermute | solution.py:603
  4.7 14.4 %collective-permute-start.1 = (f32[136,512]{1,0:T(8,128)S(1)}, f32[136,512]{1,0:T(8,128)S(1)}, u32[]{:S(2)}, u32[]{:S(2)}) collective-permute-start(f32[136,512]{1,0:T(8,128)S(1)} %get-tuple-element.84), channel_id=1, source_target_pairs={{2,0},{4,2},{6,4},{7,6},{5,7},{3,5},{1,3},{0,1},{10,8},{12,10},{14... | collective-permute-start | bytes 835592 | tf_op jit(solution)/shard_map/ppermute | solution.py:604
  4.7 16.4 %collective-permute-start.2 = (f32[128,512]{1,0:T(8,128)S(1)}, f32[128,512]{1,0:T(8,128)S(1)}, u32[]{:S(2)}, u32[]{:S(2)}) collective-permute-start(f32[128,512]{1,0:T(8,128)S(1)} %get-tuple-element.87), channel_id=1, source_target_pairs={{0,2},{2,4},{4,6},{6,7},{7,5},{5,3},{3,1},{1,0},{8,10},{10,12},{12... | collective-permute-start | bytes 786440 | tf_op jit(solution)/shard_map/ppermute | solution.py:603
  6.2 14.9 %collective-permute-start.3 = (f32[128,512]{1,0:T(8,128)S(1)}, f32[128,512]{1,0:T(8,128)S(1)}, u32[]{:S(2)}, u32[]{:S(2)}) collective-permute-start(f32[128,512]{1,0:T(8,128)S(1)} %get-tuple-element.87), channel_id=1, source_target_pairs={{2,0},{4,2},{6,4},{7,6},{5,7},{3,5},{1,3},{0,1},{10,8},{12,10},{14... | collective-permute-start | bytes 786440 | tf_op jit(solution)/shard_map/ppermute | solution.py:604
  19.1 14.6 %collective-permute-start.10 = (f32[136,512]{1,0:T(8,128)S(1)}, f32[136,512]{1,0:T(8,128)S(1)}, u32[]{:S(2)}, u32[]{:S(2)}) collective-permute-start(f32[136,512]{1,0:T(8,128)S(1)} %collective-permute-done.refs_0_.refs_2_), channel_id=1, source_target_pairs={{0,2},{2,4},{4,6},{6,7},{7,5},{5,3},{3,1},{1,0},{8,10},{10,12},{12... | collective-permute-start | bytes 835592 | tf_op jit(solution)/shard_map/ppermute | solution.py:603
  20.1 16.3 %collective-permute-start.11 = (f32[136,512]{1,0:T(8,128)S(1)}, f32[136,512]{1,0:T(8,128)S(1)}, u32[]{:S(2)}, u32[]{:S(2)}) collective-permute-start(f32[136,512]{1,0:T(8,128)S(1)} %collective-permute-done.1.refs_2_.refs_4_), channel_id=1, source_target_pairs={{2,0},{4,2},{6,4},{7,6},{5,7},{3,5},{1,3},{0,1},{10,8},{12,10},{14... | collective-permute-start | bytes 835592 | tf_op jit(solution)/shard_map/ppermute | solution.py:604
  21.1 10.7 %collective-permute-start.4 = (f32[128,512]{1,0:T(8,128)S(1)}, f32[128,512]{1,0:T(8,128)S(1)}, u32[]{:S(2)}, u32[]{:S(2)}) collective-permute-start(f32[128,512]{1,0:T(8,128)S(1)} %collective-permute-done.2.refs_1_.refs_3_), channel_id=1, source_target_pairs={{0,2},{2,4},{4,6},{6,7},{7,5},{5,3},{3,1},{1,0},{8,10},{10,12},{12... | collective-permute-start | bytes 786440 | tf_op jit(solution)/shard_map/ppermute | solution.py:603
  21.5 19.5 %collective-permute-start.6 = (f32[136,512]{1,0:T(8,128)S(1)}, f32[136,512]{1,0:T(8,128)S(1)}, u32[]{:S(2)}, u32[]{:S(2)}) collective-permute-start(f32[136,512]{1,0:T(8,128)S(1)} %collective-permute-done.refs_0_.refs_2_), channel_id=1, source_target_pairs={{0,8},{1,9},{2,10},{3,11},{4,12},{5,13},{6,14},{7,15},{8,0},{9,1},... | collective-permute-start | bytes 835592 | tf_op jit(solution)/shard_map/ppermute | solution.py:601
  24.2 16.9 %collective-permute-start.8 = (f32[136,512]{1,0:T(8,128)S(1)}, f32[136,512]{1,0:T(8,128)S(1)}, u32[]{:S(2)}, u32[]{:S(2)}) collective-permute-start(f32[136,512]{1,0:T(8,128)S(1)} %collective-permute-done.1.refs_2_.refs_4_), channel_id=1, source_target_pairs={{0,8},{1,9},{2,10},{3,11},{4,12},{5,13},{6,14},{7,15},{8,0},{9,1},... | collective-permute-start | bytes 835592 | tf_op jit(solution)/shard_map/ppermute | solution.py:601
  31.8 7.1 %collective-permute-start.5 = (f32[128,512]{1,0:T(8,128)S(1)}, f32[128,512]{1,0:T(8,128)S(1)}, u32[]{:S(2)}, u32[]{:S(2)}) collective-permute-start(f32[128,512]{1,0:T(8,128)S(1)} %collective-permute-done.3.refs_3_.refs_5_), channel_id=1, source_target_pairs={{2,0},{4,2},{6,4},{7,6},{5,7},{3,5},{1,3},{0,1},{10,8},{12,10},{14... | collective-permute-start | bytes 786440 | tf_op jit(solution)/shard_map/ppermute | solution.py:604
  39.0 15.3 %collective-permute-start.18 = (f32[136,512]{1,0:T(8,128)S(1)}, f32[136,512]{1,0:T(8,128)S(1)}, u32[]{:S(2)}, u32[]{:S(2)}) collective-permute-start(f32[136,512]{1,0:T(8,128)S(1)} %collective-permute-done.10.refs_4_.refs_10_), channel_id=1, source_target_pairs={{0,2},{2,4},{4,6},{6,7},{7,5},{5,3},{3,1},{1,0},{8,10},{10,12},{12... | collective-permute-start | bytes 835592 | tf_op jit(solution)/shard_map/ppermute | solution.py:603
  39.0 16.7 %collective-permute-start.19 = (f32[136,512]{1,0:T(8,128)S(1)}, f32[136,512]{1,0:T(8,128)S(1)}, u32[]{:S(2)}, u32[]{:S(2)}) collective-permute-start(f32[136,512]{1,0:T(8,128)S(1)} %collective-permute-done.11.refs_6_.refs_12_), channel_id=1, source_target_pairs={{2,0},{4,2},{6,4},{7,6},{5,7},{3,5},{1,3},{0,1},{10,8},{12,10},{14... | collective-permute-start | bytes 835592 | tf_op jit(solution)/shard_map/ppermute | solution.py:604
  41.1 11.0 %collective-permute-start.12 = (f32[128,512]{1,0:T(8,128)S(1)}, f32[128,512]{1,0:T(8,128)S(1)}, u32[]{:S(2)}, u32[]{:S(2)}) collective-permute-start(f32[128,512]{1,0:T(8,128)S(1)} %collective-permute-done.4.refs_5_.refs_11_), channel_id=1, source_target_pairs={{0,2},{2,4},{4,6},{6,7},{7,5},{5,3},{3,1},{1,0},{8,10},{10,12},{12... | collective-permute-start | bytes 786440 | tf_op jit(solution)/shard_map/ppermute | solution.py:603
  41.1 21.0 %collective-permute-start.14 = (f32[136,512]{1,0:T(8,128)S(1)}, f32[136,512]{1,0:T(8,128)S(1)}, u32[]{:S(2)}, u32[]{:S(2)}) collective-permute-start(f32[136,512]{1,0:T(8,128)S(1)} %collective-permute-done.10.refs_4_.refs_10_), channel_id=1, source_target_pairs={{0,8},{1,9},{2,10},{3,11},{4,12},{5,13},{6,14},{7,15},{8,0},{9,1},... | collective-permute-start | bytes 835592 | tf_op jit(solution)/shard_map/ppermute | solution.py:601
  43.5 18.7 %collective-permute-start.16 = (f32[136,512]{1,0:T(8,128)S(1)}, f32[136,512]{1,0:T(8,128)S(1)}, u32[]{:S(2)}, u32[]{:S(2)}) collective-permute-start(f32[136,512]{1,0:T(8,128)S(1)} %collective-permute-done.11.refs_6_.refs_12_), channel_id=1, source_target_pairs={{0,8},{1,9},{2,10},{3,11},{4,12},{5,13},{6,14},{7,15},{8,0},{9,1},... | collective-permute-start | bytes 835592 | tf_op jit(solution)/shard_map/ppermute | solution.py:601
  52.1 10.1 %collective-permute-start.15 = (f32[128,512]{1,0:T(8,128)S(1)}, f32[128,512]{1,0:T(8,128)S(1)}, u32[]{:S(2)}, u32[]{:S(2)}) collective-permute-start(f32[128,512]{1,0:T(8,128)S(1)} %collective-permute-done.4.refs_5_.refs_11_), channel_id=1, source_target_pairs={{0,8},{1,9},{2,10},{3,11},{4,12},{5,13},{6,14},{7,15},{8,0},{9,1},... | collective-permute-start | bytes 786440 | tf_op jit(solution)/shard_map/ppermute | solution.py:601
  54.2 7.9 %collective-permute-start.13 = (f32[128,512]{1,0:T(8,128)S(1)}, f32[128,512]{1,0:T(8,128)S(1)}, u32[]{:S(2)}, u32[]{:S(2)}) collective-permute-start(f32[128,512]{1,0:T(8,128)S(1)} %collective-permute-done.5.refs_7_.refs_13_), channel_id=1, source_target_pairs={{2,0},{4,2},{6,4},{7,6},{5,7},{3,5},{1,3},{0,1},{10,8},{12,10},{14... | collective-permute-start | bytes 786440 | tf_op jit(solution)/shard_map/ppermute | solution.py:604
  55.7 6.5 %collective-permute-start.17 = (f32[128,512]{1,0:T(8,128)S(1)}, f32[128,512]{1,0:T(8,128)S(1)}, u32[]{:S(2)}, u32[]{:S(2)}) collective-permute-start(f32[128,512]{1,0:T(8,128)S(1)} %collective-permute-done.5.refs_7_.refs_13_), channel_id=1, source_target_pairs={{0,8},{1,9},{2,10},{3,11},{4,12},{5,13},{6,14},{7,15},{8,0},{9,1},... | collective-permute-start | bytes 786440 | tf_op jit(solution)/shard_map/ppermute | solution.py:601
  62.2 7.1 %collective-permute-start.21 = (f32[128,512]{1,0:T(8,128)S(1)}, f32[128,512]{1,0:T(8,128)S(1)}, u32[]{:S(2)}, u32[]{:S(2)}) collective-permute-start(f32[128,512]{1,0:T(8,128)S(1)} %collective-permute-done.13.refs_7_.refs_21_), channel_id=1, source_target_pairs={{2,0},{4,2},{6,4},{7,6},{5,7},{3,5},{1,3},{0,1},{10,8},{12,10},{14... | collective-permute-start | bytes 786440 | tf_op jit(solution)/shard_map/ppermute | solution.py:606
  63.7 11.4 %collective-permute-start.20 = (f32[136,512]{1,0:T(8,128)S(1)}, f32[136,512]{1,0:T(8,128)S(1)}, u32[]{:S(2)}, u32[]{:S(2)}) collective-permute-start(f32[136,512]{1,0:T(8,128)S(1)} %collective-permute-done.18.refs_4_.refs_18_), channel_id=1, source_target_pairs={{0,2},{2,4},{4,6},{6,7},{7,5},{5,3},{3,1},{1,0},{8,10},{10,12},{12... | collective-permute-start | bytes 835592 | tf_op jit(solution)/shard_map/ppermute | solution.py:606
  63.7 11.4 %collective-permute-start.22 = (f32[136,512]{1,0:T(8,128)S(1)}, f32[136,512]{1,0:T(8,128)S(1)}, u32[]{:S(2)}, u32[]{:S(2)}) collective-permute-start(f32[136,512]{1,0:T(8,128)S(1)} %collective-permute-done.18.refs_4_.refs_18_), channel_id=1, source_target_pairs={{0,8},{1,9},{2,10},{3,11},{4,12},{5,13},{6,14},{7,15},{8,0},{9,1},... | collective-permute-start | bytes 835592 | tf_op jit(solution)/shard_map/ppermute | solution.py:601
  65.1 10.1 %collective-permute-start.24 = (f32[136,512]{1,0:T(8,128)S(1)}, f32[136,512]{1,0:T(8,128)S(1)}, u32[]{:S(2)}, u32[]{:S(2)}) collective-permute-start(f32[136,512]{1,0:T(8,128)S(1)} %collective-permute-done.19.refs_6_.refs_20_), channel_id=1, source_target_pairs={{0,8},{1,9},{2,10},{3,11},{4,12},{5,13},{6,14},{7,15},{8,0},{9,1},... | collective-permute-start | bytes 835592 | tf_op jit(solution)/shard_map/ppermute | solution.py:601
  65.1 10.0 %collective-permute-start.23 = (f32[128,512]{1,0:T(8,128)S(1)}, f32[128,512]{1,0:T(8,128)S(1)}, u32[]{:S(2)}, u32[]{:S(2)}) collective-permute-start(f32[128,512]{1,0:T(8,128)S(1)} %collective-permute-done.12.refs_5_.refs_19_), channel_id=1, source_target_pairs={{0,8},{1,9},{2,10},{3,11},{4,12},{5,13},{6,14},{7,15},{8,0},{9,1},... | collective-permute-start | bytes 786440 | tf_op jit(solution)/shard_map/ppermute | solution.py:601
  69.3 5.8 %collective-permute-start.25 = (f32[128,512]{1,0:T(8,128)S(1)}, f32[128,512]{1,0:T(8,128)S(1)}, u32[]{:S(2)}, u32[]{:S(2)}) collective-permute-start(f32[128,512]{1,0:T(8,128)S(1)} %collective-permute-done.13.refs_7_.refs_21_), channel_id=1, source_target_pairs={{0,8},{1,9},{2,10},{3,11},{4,12},{5,13},{6,14},{7,15},{8,0},{9,1},... | collective-permute-start | bytes 786440 | tf_op jit(solution)/shard_map/ppermute | solution.py:601
  (8 other events, 38.3 us)

commit v2 on v0

--- a/solution.py
+++ b/solution.py
@@ -130,16 +130,26 @@
     return lax.div(jnp.clip(live - start, 0, length) + (GROUP - 1), GROUP)
 
 
-def begin_kernel(natoms, lanes, atom_ref, box_ref, projector_ref, info_ref, mine_ref, info_sem, half_sem):
+def begin_kernel(
+    natoms, lanes, atom_hbm, box_hbm, projector_ref, info_ref, mine_ref, atom_ref, box_ref, sem
+):
+    reads = [
+        pltpu.make_async_copy(atom_hbm, atom_ref, sem.at[0]),
+        pltpu.make_async_copy(box_hbm, box_ref, sem.at[1]),
+    ]
+    for c in reads:
+        c.start()
     nslab = lax.axis_size("slab")
     half = mine_ref.shape[0] - INFO
     core = lax.rem(lax.axis_index("band"), 2)
     copy = pltpu.make_async_copy(
         projector_ref.at[pl.ds(pl.multiple_of(core * half, GROUP), half), :],
         mine_ref.at[pl.ds(INFO, half), :],
-        half_sem,
+        sem.at[2],
     )
     copy.start()
+    for c in reads:
+        c.wait()
     atom_dev = natoms // nslab
     below = lax.rem(lax.axis_index("slab") + nslab - 1, nslab) * atom_dev
     atom = atom_ref[...]
@@ -152,7 +162,7 @@
     info_ref[0:1, 0:slots] = box_ref[...].astype(jnp.float32)
     info_ref[1:2, 0:slots] = jnp.broadcast_to(live, (1, slots))
     info_ref[2:3, 0:slots] = jnp.where(atom >= 0, column, -1).astype(jnp.float32)
-    head = pltpu.make_async_copy(info_ref, mine_ref.at[pl.ds(0, INFO), :], info_sem)
+    head = pltpu.make_async_copy(info_ref, mine_ref.at[pl.ds(0, INFO), :], sem.at[0])
     head.start()
     head.wait()
     copy.wait()
@@ -166,14 +176,18 @@
             jax.ShapeDtypeStruct((INFO, depth), jnp.float32),
             jax.ShapeDtypeStruct((INFO + slots // 2, depth), jnp.float32),
         ],
-        in_specs=[VMEM, VMEM, ANY],
+        in_specs=[ANY, ANY, ANY],
         out_specs=[VMEM, ANY],
-        scratch_shapes=[pltpu.SemaphoreType.DMA(()), pltpu.SemaphoreType.DMA(())],
+        scratch_shapes=[
+            pltpu.VMEM((1, slots), jnp.int32),
+            pltpu.VMEM((1, slots), jnp.int32),
+            pltpu.SemaphoreType.DMA((3,)),
+        ],
         compiler_params=params(8 * MIB),
         name="begin",
     )(
-        slot_atom.reshape(1, slots),
-        slot_box.reshape(1, slots),
+        pltpu.with_memory_space_constraint(slot_atom.reshape(1, slots), pltpu.HBM),
+        pltpu.with_memory_space_constraint(slot_box.reshape(1, slots), pltpu.HBM),
         pltpu.with_memory_space_constraint(projectors, pltpu.HBM),
     )
 
@@ -349,7 +363,7 @@
                 beta_sem.at[i],
             )
         )
-    for c in info_copies + copies[: loaded.shape[0]] + beta_copies:
+    for c in info_copies + copies[: loaded.shape[0]]:
         c.start()
     lane_slot = lax.broadcasted_iota(jnp.int32, (rows, width), 1) % GROUP
     for s in range(GROUP):
@@ -375,6 +389,9 @@
             parts[slab] = parts[slab] + loaded[i % loaded.shape[0]]
 
     lane_block = lax.broadcasted_iota(jnp.int32, (rows, width), 1) // GROUP
+    for c in beta_copies:
+        c.start()
+
     def couple(slab, carry):
         following = lax.rem(slab + 1, nslab)
         total = parts[slab, :, lanes:] + parts[following, :, :lanes]
@@ -534,9 +551,7 @@
 
     where = [(0, 0, None)]
     for step in range(1, reach):
-        where += [(1 - step, 0, True), (step - 1, 0, True)] if step > 1 else []
-        where += [(-step, 0, False), (step, 0, False)]
-    where += [(1 - reach, 0, True), (reach - 1, 0, True)]
+        where += [(-step, 0, False), (step, 0, False), (-step, 0, True), (step, 0, True)]
     where += [(reach, 0, False), (reach, quarter, False), (reach, 0, True), (reach, quarter, True)]
     boxes = split.shape[0] // nslab
 
@@ -576,11 +591,8 @@
     project_new()
     up, down, projections, place = lax.optimization_barrier((up, down, projections, place))
     projections = list(projections)
-    near = []
     for step in range(1, reach + 1):
         last = step == reach
-        for array in near:
-            add(array)
         for array in (up,) if last else (up, down):
             infos.append((add(array), len(pieces) - 1))
         if last:
@@ -593,11 +605,14 @@
             up = lax.ppermute(up[: INFO + quarter], AXES, onward)
             down = lax.ppermute(down[INFO + quarter :], AXES, backward)
         project_new()
-        up, down, near, projections = lax.optimization_barrier((up, down, near, projections))
+        near, projections = lax.optimization_barrier((near, projections))
         near, projections = list(near), list(projections)
-    add(near[0])
-    add(near[1], len(arrays) - 1)
-    project_new()
+        add(near[0])
+        add(near[1], len(arrays) - 1 if last else None)
+        project_new()
+        if not last:
+            up, down, projections = lax.optimization_barrier((up, down, projections))
+            projections = list(projections)
     return arrays, pieces, infos, projections, place
 
 

time: 89.9 us -> 90.4 us (level)
  starting transfers between devices: 17.4 us -> 13.1 us
  Pallas kernels: 55.1 us -> 58.9 us
  waiting for transfers between devices: 12.9 us -> 14.7 us
  local copies, waits for them, and re-layouts: 3.91 us -> 2.45 us
    pallas_call x6 -> x9, Pallas kernels: 22.7 us -> 26.9 us  [project(): pl.pallas_call(functools.partial(project_kernel, local, infos), out_shape...]
    ppermute x8, starting transfers between devices: 9.53 us -> 6.46 us  [gather_and_project(): near = [lax.ppermute(up, AXES, sibling), lax.ppermute(down, AXES, sibling)]]
    ppermute x2, starting transfers between devices: 2.25 us -> 0.17 us  [gather_and_project(): down = lax.ppermute(down, AXES, backward)]
    ppermute x2, waiting for transfers between devices: 1.16 us -> 3.15 us  [gather_and_project(): down = lax.ppermute(down, AXES, backward)]
    ppermute x1, waiting for transfers between devices: 2.17 us -> 0.34 us  [gather_and_project(): down = lax.ppermute(down[INFO + quarter:], AXES, backward)]
    ppermute x2, waiting for transfers between devices: 9.56 us -> 11.2 us  [gather_and_project(): up = lax.ppermute(up, AXES, onward)]
    unnamed x8 -> x4, local copies, waits for them, and re-layouts: 2.38 us -> 0.93 us
    ppermute x2, starting transfers between devices: 1.82 us -> 2.76 us  [gather_and_project(): up = lax.ppermute(up, AXES, onward)]
  transfers between devices with their start and end apart: 16 -> 16, of which waited for: 4 -> 5; matrix products, arithmetic and copies ran while one was open for 2% -> 2% of each run, Pallas kernels for 30% -> 35%
where the time goes in v2:
time: 90.4 us; the launch traced here: 89.5 us
  Pallas kernels  58.9 us (65%)
  waiting for transfers between devices  14.7 us (16%)
  starting transfers between devices  13.1 us (14%)
  local copies, waits for them, and re-layouts  2.45 us (3%)
    pallas_call x9, Pallas kernels, project(): pl.pallas_call(functools.partial(project_kernel, local, infos), out_shape...  26.9 us
    pallas_call x1, Pallas kernels, apply(): pl.pallas_call(functools.partial(apply_kernel, nslab, slots, nsum, pieces...  23.3 us
    ppermute x2, waiting for transfers between devices, gather_and_project(): up = lax.ppermute(up, AXES, onward)  11.2 us
    pallas_call x1, Pallas kernels, split_bands(): pl.pallas_call(functools.partial(split_bands_kernel, natoms // nslab), gr...  7.44 us
    ppermute x8, starting transfers between devices, gather_and_project(): near = [lax.ppermute(up, AXES, sibling), lax.ppermute(down, AXES, sibling)]  6.46 us
    ppermute x2, waiting for transfers between devices, gather_and_project(): down = lax.ppermute(down, AXES, backward)  3.15 us
    ppermute x2, starting transfers between devices, gather_and_project(): up = lax.ppermute(up, AXES, onward)  2.76 us
    ppermute x1, starting transfers between devices, gather_and_project(): up = lax.ppermute(mine, AXES, onward)  2.18 us
  transfers between devices with their start and end apart: 16, of which 5 were waited for; matrix products, arithmetic and copies ran while one was open for 2% of the time, Pallas kernels for 35%

profile of v2, /device:TPU:1, one launch (start us, length us, event | category | flops | bytes accessed | tf_op | source)
XLA Modules:
  0.0 89.5 jit_solution(11335351736044043327)
XLA Ops:
  0.0 1.2 %begin.1 = (f32[8,512]{1,0:T(8,128)S(1)}, f32[264,512]{1,0:T(8,128)S(1)}) custom-call(s32[1,512]{1,0:T(1,128)} %bitcast.7, s32[1,512]{1,0:T(1,128)} %bitcast.8, f32[512,512]{1,0:T(8,128)} %refs_1_.3), custom_call_target="tpu_custom_call" | custom-call | tf_op jit(solution)/shard_map/begin/pallas_call | solution.py:173
  1.2 2.2 %collective-permute-start = (f32[264,512]{1,0:T(8,128)S(1)}, f32[264,512]{1,0:T(8,128)S(1)}, u32[]{:S(2)}, u32[]{:S(2)}) collective-permute-start(f32[264,512]{1,0:T(8,128)S(1)} %get-tuple-element.106), channel_id=1, source_target_pairs={{0,2},{2,4},{4,6},{6,7},{7,5},{5,3},{3,1},{1,0},{8,10},{10,12},{12... | collective-permute-start | bytes 1622024 | tf_op jit(solution)/shard_map/ppermute | solution.py:582
  5.8 7.4 %split_bands.1 = (bf16[512,16,256]{2,1,0:T(8,128)(2,1)S(1)}, f32[8,64,128]{2,1,0:T(8,128)S(1)}) custom-call(f32[16,32768]{1,0:T(8,128)} %bitcast.6, f32[64,768]{1,0:T(8,128)S(1)} %bitcast.5, s32[8,768]{1,0:T(8,128)S(1)} %broadcast_in_dim.2.channels_ref), custom_call_target="tpu_custom_call" | custom-call | flops 4194304 | bytes 6291456 | tf_op jit(solution)/shard_map/split_bands/pallas_call | solution.py:84
  13.3 3.0 %project.9.refs_18_ = f32[128,256]{1,0:T(8,128)S(1)} custom-call(s32[51]{0:T(128)S(1)} %reshape.22.place_ref, bf16[512,16,256]{2,1,0:T(8,128)(2,1)S(1)} %get-tuple-element.107.x_ref, f32[8,512]{1,0:T(8,128)S(1)} %get-tuple-element.108.refs_0_, f32[512,512]{1,0:T(8,128)S(1)} %copy-done), custom_call_target="tpu_custom_call" | custom-call | flops 134217728 | bytes 5242880 | tf_op jit(solution)/shard_map/project/pallas_call | solution.py:286
  16.3 1.8 %collective-permute-start.2 = (f32[264,512]{1,0:T(8,128)S(1)}, f32[264,512]{1,0:T(8,128)S(1)}, u32[]{:S(2)}, u32[]{:S(2)}) collective-permute-start(f32[264,512]{1,0:T(8,128)S(1)} %collective-permute-done.refs_0_.refs_2_), channel_id=1, source_target_pairs={{0,8},{1,9},{2,10},{3,11},{4,12},{5,13},{6,14},{7,15},{8,0},{9,1},... | collective-permute-start | bytes 1622024 | tf_op jit(solution)/shard_map/ppermute | solution.py:600
  18.1 1.3 %collective-permute-start.4 = (f32[264,512]{1,0:T(8,128)S(1)}, f32[264,512]{1,0:T(8,128)S(1)}, u32[]{:S(2)}, u32[]{:S(2)}) collective-permute-start(f32[264,512]{1,0:T(8,128)S(1)} %collective-permute-done.refs_0_.refs_2_), channel_id=1, source_target_pairs={{0,2},{2,4},{4,6},{6,7},{7,5},{5,3},{3,1},{1,0},{8,10},{10,12},{12... | collective-permute-start | bytes 1622024 | tf_op jit(solution)/shard_map/ppermute | solution.py:602
  19.5 1.9 %project.10 = (f32[128,256]{1,0:T(8,128)S(1)}, f32[128,256]{1,0:T(8,128)S(1)}) custom-call(s32[51]{0:T(128)S(1)} %reshape.22.place_ref, bf16[512,16,256]{2,1,0:T(8,128)(2,1)S(1)} %get-tuple-element.107.x_ref, f32[264,512]{1,0:T(8,128)S(1)} %collective-permute-done.refs_0_.refs_2_, f32[264,512]{1,0:T(8,128)S(1)} %collective-permute-done.1.refs_1_.refs_3_), custom_call_target="tpu_custom_call" | custom-call | flops 134217728 | bytes 5242880 | tf_op jit(solution)/shard_map/project/pallas_call | solution.py:286
  21.5 4.1 %project.11 = (f32[128,256]{1,0:T(8,128)S(1)}, f32[128,256]{1,0:T(8,128)S(1)}) custom-call(s32[51]{0:T(128)S(1)} %reshape.22.place_ref, bf16[512,16,256]{2,1,0:T(8,128)(2,1)S(1)} %get-tuple-element.107.x_ref, f32[264,512]{1,0:T(8,128)S(1)} %collective-permute-done.2.refs_0_.refs_4_, f32[264,512]{1,0:T(8,128)S(1)} %collective-permute-done.3.refs_1_.refs_5_), custom_call_target="tpu_custom_call" | custom-call | flops 134217728 | bytes 5242880 | tf_op jit(solution)/shard_map/project/pallas_call | solution.py:286
  25.5 5.9 %collective-permute-done.4.refs_0_.refs_6_ = f32[264,512]{1,0:T(8,128)S(1)} collective-permute-done((f32[264,512]{1,0:T(8,128)S(1)}, f32[264,512]{1,0:T(8,128)S(1)}, u32[]{:S(2)}, u32[]{:S(2)}) %collective-permute-start.4) | collective-permute-done | bytes 540704 | tf_op jit(solution)/shard_map/ppermute | solution.py:602
  31.4 2.0 %collective-permute-done.5.refs_1_.refs_7_ = f32[264,512]{1,0:T(8,128)S(1)} collective-permute-done((f32[264,512]{1,0:T(8,128)S(1)}, f32[264,512]{1,0:T(8,128)S(1)}, u32[]{:S(2)}, u32[]{:S(2)}) %collective-permute-start.5) | collective-permute-done | bytes 540704 | tf_op jit(solution)/shard_map/ppermute | solution.py:603
  33.4 1.3 %collective-permute-start.6 = (f32[264,512]{1,0:T(8,128)S(1)}, f32[264,512]{1,0:T(8,128)S(1)}, u32[]{:S(2)}, u32[]{:S(2)}) collective-permute-start(f32[264,512]{1,0:T(8,128)S(1)} %collective-permute-done.4.refs_0_.refs_6_), channel_id=1, source_target_pairs={{0,8},{1,9},{2,10},{3,11},{4,12},{5,13},{6,14},{7,15},{8,0},{9,1},... | collective-permute-start | bytes 1622024 | tf_op jit(solution)/shard_map/ppermute | solution.py:600
  34.7 1.5 %collective-permute-start.8 = (f32[264,512]{1,0:T(8,128)S(1)}, f32[264,512]{1,0:T(8,128)S(1)}, u32[]{:S(2)}, u32[]{:S(2)}) collective-permute-start(f32[264,512]{1,0:T(8,128)S(1)} %collective-permute-done.4.refs_0_.refs_6_), channel_id=1, source_target_pairs={{0,2},{2,4},{4,6},{6,7},{7,5},{5,3},{3,1},{1,0},{8,10},{10,12},{12... | collective-permute-start | bytes 1622024 | tf_op jit(solution)/shard_map/ppermute | solution.py:602
  36.2 3.0 %project.12 = (f32[128,256]{1,0:T(8,128)S(1)}, f32[128,256]{1,0:T(8,128)S(1)}) custom-call(s32[51]{0:T(128)S(1)} %reshape.22.place_ref, bf16[512,16,256]{2,1,0:T(8,128)(2,1)S(1)} %get-tuple-element.107.x_ref, f32[264,512]{1,0:T(8,128)S(1)} %collective-permute-done.4.refs_0_.refs_6_, f32[264,512]{1,0:T(8,128)S(1)} %collective-permute-done.5.refs_1_.refs_7_), custom_call_target="tpu_custom_call" | custom-call | flops 134217728 | bytes 5242880 | tf_op jit(solution)/shard_map/project/pallas_call | solution.py:286
  39.2 3.5 %project.13 = (f32[128,256]{1,0:T(8,128)S(1)}, f32[128,256]{1,0:T(8,128)S(1)}) custom-call(s32[51]{0:T(128)S(1)} %reshape.22.place_ref, bf16[512,16,256]{2,1,0:T(8,128)(2,1)S(1)} %get-tuple-element.107.x_ref, f32[264,512]{1,0:T(8,128)S(1)} %collective-permute-done.6.refs_0_.refs_8_, f32[264,512]{1,0:T(8,128)S(1)} %collective-permute-done.7.refs_1_.refs_9_), custom_call_target="tpu_custom_call" | custom-call | flops 134217728 | bytes 5242880 | tf_op jit(solution)/shard_map/project/pallas_call | solution.py:286
  42.7 5.3 %collective-permute-done.8.refs_0_.refs_10_ = f32[264,512]{1,0:T(8,128)S(1)} collective-permute-done((f32[264,512]{1,0:T(8,128)S(1)}, f32[264,512]{1,0:T(8,128)S(1)}, u32[]{:S(2)}, u32[]{:S(2)}) %collective-permute-start.8) | collective-permute-done | bytes 540704 | tf_op jit(solution)/shard_map/ppermute | solution.py:602
  48.0 1.1 %collective-permute-done.9.refs_1_.refs_11_ = f32[264,512]{1,0:T(8,128)S(1)} collective-permute-done((f32[264,512]{1,0:T(8,128)S(1)}, f32[264,512]{1,0:T(8,128)S(1)}, u32[]{:S(2)}, u32[]{:S(2)}) %collective-permute-start.9) | collective-permute-done | bytes 540704 | tf_op jit(solution)/shard_map/ppermute | solution.py:603
  49.2 1.7 %collective-permute-start.10 = (f32[264,512]{1,0:T(8,128)S(1)}, f32[264,512]{1,0:T(8,128)S(1)}, u32[]{:S(2)}, u32[]{:S(2)}) collective-permute-start(f32[264,512]{1,0:T(8,128)S(1)} %collective-permute-done.8.refs_0_.refs_10_), channel_id=1, source_target_pairs={{0,8},{1,9},{2,10},{3,11},{4,12},{5,13},{6,14},{7,15},{8,0},{9,1},... | collective-permute-start | bytes 1622024 | tf_op jit(solution)/shard_map/ppermute | solution.py:600
  50.9 1.3 %collective-permute-start.12 = (f32[136,512]{1,0:T(8,128)S(1)}, f32[136,512]{1,0:T(8,128)S(1)}, u32[]{:S(2)}, u32[]{:S(2)}) collective-permute-start(f32[136,512]{1,0:T(8,128)S(1)} %slice.6), channel_id=1, source_target_pairs={{0,2},{2,4},{4,6},{6,7},{7,5},{5,3},{3,1},{1,0},{8,10},{10,12},{12... | collective-permute-start | bytes 835592 | tf_op jit(solution)/shard_map/ppermute | solution.py:605
  52.5 3.0 %project.14 = (f32[128,256]{1,0:T(8,128)S(1)}, f32[128,256]{1,0:T(8,128)S(1)}) custom-call(s32[51]{0:T(128)S(1)} %reshape.22.place_ref, bf16[512,16,256]{2,1,0:T(8,128)(2,1)S(1)} %get-tuple-element.107.x_ref, f32[264,512]{1,0:T(8,128)S(1)} %collective-permute-done.8.refs_0_.refs_10_, f32[264,512]{1,0:T(8,128)S(1)} %collective-permute-done.9.refs_1_.refs_11_), custom_call_target="tpu_custom_call" | custom-call | flops 134217728 | bytes 5242880 | tf_op jit(solution)/shard_map/project/pallas_call | solution.py:286
  55.5 3.5 %project.15 = (f32[128,256]{1,0:T(8,128)S(1)}, f32[128,256]{1,0:T(8,128)S(1)}) custom-call(s32[51]{0:T(128)S(1)} %reshape.22.place_ref, bf16[512,16,256]{2,1,0:T(8,128)(2,1)S(1)} %get-tuple-element.107.x_ref, f32[264,512]{1,0:T(8,128)S(1)} %collective-permute-done.10.refs_0_.refs_12_, f32[264,512]{1,0:T(8,128)S(1)} %collective-permute-done.11.refs_1_.refs_13_), custom_call_target="tpu_custom_call" | custom-call | flops 134217728 | bytes 5242880 | tf_op jit(solution)/shard_map/project/pallas_call | solution.py:286
  59.3 1.7 %collective-permute-start.14 = (f32[136,512]{1,0:T(8,128)S(1)}, f32[136,512]{1,0:T(8,128)S(1)}, u32[]{:S(2)}, u32[]{:S(2)}) collective-permute-start(f32[136,512]{1,0:T(8,128)S(1)} %collective-permute-done.12.refs_0_.refs_14_), channel_id=1, source_target_pairs={{0,8},{1,9},{2,10},{3,11},{4,12},{5,13},{6,14},{7,15},{8,0},{9,1},... | collective-permute-start | bytes 835592 | tf_op jit(solution)/shard_map/ppermute | solution.py:600
  61.0 2.1 %project.16 = (f32[128,256]{1,0:T(8,128)S(1)}, f32[128,256]{1,0:T(8,128)S(1)}) custom-call(s32[51]{0:T(128)S(1)} %reshape.22.place_ref, bf16[512,16,256]{2,1,0:T(8,128)(2,1)S(1)} %get-tuple-element.107.x_ref, f32[136,512]{1,0:T(8,128)S(1)} %collective-permute-done.12.refs_0_.refs_14_, f32[128,512]{1,0:T(8,128)S(1)} %collective-permute-done.13.refs_1_.refs_15_), custom_call_target="tpu_custom_call" | custom-call | flops 67108864 | bytes 4718592 | tf_op jit(solution)/shard_map/project/pallas_call | solution.py:286
  63.1 3.0 %project.17 = (f32[128,256]{1,0:T(8,128)S(1)}, f32[128,256]{1,0:T(8,128)S(1)}) custom-call(s32[51]{0:T(128)S(1)} %reshape.22.place_ref, bf16[512,16,256]{2,1,0:T(8,128)(2,1)S(1)} %get-tuple-element.107.x_ref, f32[136,512]{1,0:T(8,128)S(1)} %collective-permute-done.14.refs_0_.refs_16_, f32[128,512]{1,0:T(8,128)S(1)} %collective-permute-done.15.refs_1_.refs_17_), custom_call_target="tpu_custom_call" | custom-call | flops 67108864 | bytes 4718592 | tf_op jit(solution)/shard_map/project/pallas_call | solution.py:286
  66.1 23.3 %apply.1 = f32[16,32768]{1,0:T(8,128)} custom-call(s32[51]{0:T(128)S(1)} %reshape.22.place_ref, f32[8,64,128]{2,1,0:T(8,128)S(1)} %get-tuple-element.110.coupling_ref, f32[8,512]{1,0:T(8,128)S(1)} %get-tuple-element.108.refs_0_, f32[512,512]{1,0:T(8,128)S(1)} %copy-done, f32[264,512]{1,0:T(8,128)S(1)} %collective-permute-done.refs_0_.refs_2_, ...), custom_call_target="tpu_custom_call" | custom-call | tf_op jit(solution)/shard_map/apply/pallas_call | solution.py:524
  (29 shorter events, 3.2 us)
Async XLA Ops:
  0.0 13.2 %copy-start = (f32[512,512]{1,0:T(8,128)S(1)}, f32[512,512]{1,0:T(8,128)}, u32[]{:S(2)}) copy-start(f32[512,512]{1,0:T(8,128)} %refs_1_.3) | copy-start | bytes 3145732
  1.2 15.0 %collective-permute-start = (f32[264,512]{1,0:T(8,128)S(1)}, f32[264,512]{1,0:T(8,128)S(1)}, u32[]{:S(2)}, u32[]{:S(2)}) collective-permute-start(f32[264,512]{1,0:T(8,128)S(1)} %get-tuple-element.106), channel_id=1, source_target_pairs={{0,2},{2,4},{4,6},{6,7},{7,5},{5,3},{3,1},{1,0},{8,10},{10,12},{12... | collective-permute-start | bytes 1622024 | tf_op jit(solution)/shard_map/ppermute | solution.py:582
  3.4 12.9 %collective-permute-start.1 = (f32[264,512]{1,0:T(8,128)S(1)}, f32[264,512]{1,0:T(8,128)S(1)}, u32[]{:S(2)}, u32[]{:S(2)}) collective-permute-start(f32[264,512]{1,0:T(8,128)S(1)} %get-tuple-element.106), channel_id=1, source_target_pairs={{2,0},{4,2},{6,4},{7,6},{5,7},{3,5},{1,3},{0,1},{10,8},{12,10},{14... | collective-permute-start | bytes 1622024 | tf_op jit(solution)/shard_map/ppermute | solution.py:583
  4.9 0.9 %copy-start.1 = (f32[8,8,768]{2,1,0:T(8,128)S(1)}, f32[8,8,768]{2,1,0:T(8,128)}, u32[]{:S(2)}) copy-start(f32[8,8,768]{2,1,0:T(8,128)} %param.12) | copy-start | bytes 589828
  16.3 5.2 %collective-permute-start.2 = (f32[264,512]{1,0:T(8,128)S(1)}, f32[264,512]{1,0:T(8,128)S(1)}, u32[]{:S(2)}, u32[]{:S(2)}) collective-permute-start(f32[264,512]{1,0:T(8,128)S(1)} %collective-permute-done.refs_0_.refs_2_), channel_id=1, source_target_pairs={{0,8},{1,9},{2,10},{3,11},{4,12},{5,13},{6,14},{7,15},{8,0},{9,1},... | collective-permute-start | bytes 1622024 | tf_op jit(solution)/shard_map/ppermute | solution.py:600
  18.1 3.4 %collective-permute-start.3 = (f32[264,512]{1,0:T(8,128)S(1)}, f32[264,512]{1,0:T(8,128)S(1)}, u32[]{:S(2)}, u32[]{:S(2)}) collective-permute-start(f32[264,512]{1,0:T(8,128)S(1)} %collective-permute-done.1.refs_1_.refs_3_), channel_id=1, source_target_pairs={{0,8},{1,9},{2,10},{3,11},{4,12},{5,13},{6,14},{7,15},{8,0},{9,1},... | collective-permute-start | bytes 1622024 | tf_op jit(solution)/shard_map/ppermute | solution.py:600
  18.1 13.3 %collective-permute-start.4 = (f32[264,512]{1,0:T(8,128)S(1)}, f32[264,512]{1,0:T(8,128)S(1)}, u32[]{:S(2)}, u32[]{:S(2)}) collective-permute-start(f32[264,512]{1,0:T(8,128)S(1)} %collective-permute-done.refs_0_.refs_2_), channel_id=1, source_target_pairs={{0,2},{2,4},{4,6},{6,7},{7,5},{5,3},{3,1},{1,0},{8,10},{10,12},{12... | collective-permute-start | bytes 1622024 | tf_op jit(solution)/shard_map/ppermute | solution.py:602
  19.4 14.0 %collective-permute-start.5 = (f32[264,512]{1,0:T(8,128)S(1)}, f32[264,512]{1,0:T(8,128)S(1)}, u32[]{:S(2)}, u32[]{:S(2)}) collective-permute-start(f32[264,512]{1,0:T(8,128)S(1)} %collective-permute-done.1.refs_1_.refs_3_), channel_id=1, source_target_pairs={{2,0},{4,2},{6,4},{7,6},{5,7},{3,5},{1,3},{0,1},{10,8},{12,10},{14... | collective-permute-start | bytes 1622024 | tf_op jit(solution)/shard_map/ppermute | solution.py:603
  33.4 5.7 %collective-permute-start.6 = (f32[264,512]{1,0:T(8,128)S(1)}, f32[264,512]{1,0:T(8,128)S(1)}, u32[]{:S(2)}, u32[]{:S(2)}) collective-permute-start(f32[264,512]{1,0:T(8,128)S(1)} %collective-permute-done.4.refs_0_.refs_6_), channel_id=1, source_target_pairs={{0,8},{1,9},{2,10},{3,11},{4,12},{5,13},{6,14},{7,15},{8,0},{9,1},... | collective-permute-start | bytes 1622024 | tf_op jit(solution)/shard_map/ppermute | solution.py:600
  34.7 4.5 %collective-permute-start.7 = (f32[264,512]{1,0:T(8,128)S(1)}, f32[264,512]{1,0:T(8,128)S(1)}, u32[]{:S(2)}, u32[]{:S(2)}) collective-permute-start(f32[264,512]{1,0:T(8,128)S(1)} %collective-permute-done.5.refs_1_.refs_7_), channel_id=1, source_target_pairs={{0,8},{1,9},{2,10},{3,11},{4,12},{5,13},{6,14},{7,15},{8,0},{9,1},... | collective-permute-start | bytes 1622024 | tf_op jit(solution)/shard_map/ppermute | solution.py:600
  34.7 13.3 %collective-permute-start.8 = (f32[264,512]{1,0:T(8,128)S(1)}, f32[264,512]{1,0:T(8,128)S(1)}, u32[]{:S(2)}, u32[]{:S(2)}) collective-permute-start(f32[264,512]{1,0:T(8,128)S(1)} %collective-permute-done.4.refs_0_.refs_6_), channel_id=1, source_target_pairs={{0,2},{2,4},{4,6},{6,7},{7,5},{5,3},{3,1},{1,0},{8,10},{10,12},{12... | collective-permute-start | bytes 1622024 | tf_op jit(solution)/shard_map/ppermute | solution.py:602
  36.2 13.0 %collective-permute-start.9 = (f32[264,512]{1,0:T(8,128)S(1)}, f32[264,512]{1,0:T(8,128)S(1)}, u32[]{:S(2)}, u32[]{:S(2)}) collective-permute-start(f32[264,512]{1,0:T(8,128)S(1)} %collective-permute-done.5.refs_1_.refs_7_), channel_id=1, source_target_pairs={{2,0},{4,2},{6,4},{7,6},{5,7},{3,5},{1,3},{0,1},{10,8},{12,10},{14... | collective-permute-start | bytes 1622024 | tf_op jit(solution)/shard_map/ppermute | solution.py:603
  49.2 6.3 %collective-permute-start.10 = (f32[264,512]{1,0:T(8,128)S(1)}, f32[264,512]{1,0:T(8,128)S(1)}, u32[]{:S(2)}, u32[]{:S(2)}) collective-permute-start(f32[264,512]{1,0:T(8,128)S(1)} %collective-permute-done.8.refs_0_.refs_10_), channel_id=1, source_target_pairs={{0,8},{1,9},{2,10},{3,11},{4,12},{5,13},{6,14},{7,15},{8,0},{9,1},... | collective-permute-start | bytes 1622024 | tf_op jit(solution)/shard_map/ppermute | solution.py:600
  50.8 4.6 %collective-permute-start.11 = (f32[264,512]{1,0:T(8,128)S(1)}, f32[264,512]{1,0:T(8,128)S(1)}, u32[]{:S(2)}, u32[]{:S(2)}) collective-permute-start(f32[264,512]{1,0:T(8,128)S(1)} %collective-permute-done.9.refs_1_.refs_11_), channel_id=1, source_target_pairs={{0,8},{1,9},{2,10},{3,11},{4,12},{5,13},{6,14},{7,15},{8,0},{9,1},... | collective-permute-start | bytes 1622024 | tf_op jit(solution)/shard_map/ppermute | solution.py:600
  50.9 8.5 %collective-permute-start.12 = (f32[136,512]{1,0:T(8,128)S(1)}, f32[136,512]{1,0:T(8,128)S(1)}, u32[]{:S(2)}, u32[]{:S(2)}) collective-permute-start(f32[136,512]{1,0:T(8,128)S(1)} %slice.6), channel_id=1, source_target_pairs={{0,2},{2,4},{4,6},{6,7},{7,5},{5,3},{3,1},{1,0},{8,10},{10,12},{12... | collective-permute-start | bytes 835592 | tf_op jit(solution)/shard_map/ppermute | solution.py:605
  52.2 7.1 %collective-permute-start.13 = (f32[128,512]{1,0:T(8,128)S(1)}, f32[128,512]{1,0:T(8,128)S(1)}, u32[]{:S(2)}, u32[]{:S(2)}) collective-permute-start(f32[128,512]{1,0:T(8,128)S(1)} %slice.7), channel_id=1, source_target_pairs={{2,0},{4,2},{6,4},{7,6},{5,7},{3,5},{1,3},{0,1},{10,8},{12,10},{14... | collective-permute-start | bytes 786440 | tf_op jit(solution)/shard_map/ppermute | solution.py:606
  59.3 3.8 %collective-permute-start.14 = (f32[136,512]{1,0:T(8,128)S(1)}, f32[136,512]{1,0:T(8,128)S(1)}, u32[]{:S(2)}, u32[]{:S(2)}) collective-permute-start(f32[136,512]{1,0:T(8,128)S(1)} %collective-permute-done.12.refs_0_.refs_14_), channel_id=1, source_target_pairs={{0,8},{1,9},{2,10},{3,11},{4,12},{5,13},{6,14},{7,15},{8,0},{9,1},... | collective-permute-start | bytes 835592 | tf_op jit(solution)/shard_map/ppermute | solution.py:600
  61.0 2.1 %collective-permute-start.15 = (f32[128,512]{1,0:T(8,128)S(1)}, f32[128,512]{1,0:T(8,128)S(1)}, u32[]{:S(2)}, u32[]{:S(2)}) collective-permute-start(f32[128,512]{1,0:T(8,128)S(1)} %collective-permute-done.13.refs_1_.refs_15_), channel_id=1, source_target_pairs={{0,8},{1,9},{2,10},{3,11},{4,12},{5,13},{6,14},{7,15},{8,0},{9,1},... | collective-permute-start | bytes 786440 | tf_op jit(solution)/shard_map/ppermute | solution.py:600

commit v3 on v2

--- a/solution.py
+++ b/solution.py
@@ -597,7 +597,9 @@
             infos.append((add(array), len(pieces) - 1))
         if last:
             add(down, len(arrays) - 1)
-        near = [lax.ppermute(up, AXES, sibling), lax.ppermute(down, AXES, sibling)]
+        near = [up, down]
+        if last:
+            near = [lax.ppermute(x, AXES, sibling) for x in near]
         if step + 1 < reach:
             up = lax.ppermute(up, AXES, onward)
             down = lax.ppermute(down, AXES, backward)
@@ -607,6 +609,8 @@
         project_new()
         near, projections = lax.optimization_barrier((near, projections))
         near, projections = list(near), list(projections)
+        if not last:
+            near = [lax.ppermute(x, AXES, sibling) for x in near]
         add(near[0])
         add(near[1], len(arrays) - 1 if last else None)
         project_new()

time: 90.4 us -> 99.2 us (1.097)
  starting transfers between devices: 13.1 us -> 18.9 us
  waiting for transfers between devices: 14.7 us -> 20.4 us
  Pallas kernels: 58.9 us -> 56.7 us
    ppermute x8, starting transfers between devices: 6.46 us -> 11.8 us  [gather_and_project(): near = [lax.ppermute(x, AXES, sibling) for x in near]]
    ppermute x2, waiting for transfers between devices: 11.2 us -> 14.7 us  [gather_and_project(): up = lax.ppermute(up, AXES, onward)]
    ppermute x8, waiting for transfers between devices: 0.02 us -> 1.85 us  [gather_and_project(): near = [lax.ppermute(x, AXES, sibling) for x in near]]
    ppermute x1, waiting for transfers between devices: 0.34 us -> 1.85 us  [gather_and_project(): down = lax.ppermute(down[INFO + quarter:], AXES, backward)]
    ppermute x2, waiting for transfers between devices: 3.15 us -> 1.96 us  [gather_and_project(): down = lax.ppermute(down, AXES, backward)]
    pallas_call x1, Pallas kernels: 23.3 us -> 22.2 us  [apply(): pl.pallas_call(functools.partial(apply_kernel, nslab, slots, nsum, pieces...]
    pallas_call x9, Pallas kernels: 26.9 us -> 25.9 us  [project(): pl.pallas_call(functools.partial(project_kernel, local, infos), out_shape...]
  transfers between devices with their start and end apart: 16 -> 16, of which waited for: 5 -> 8; matrix products, arithmetic and copies ran while one was open for 2% -> 2% of each run, Pallas kernels for 35% -> 24%
where the time goes in v3:
time: 99.2 us; the launch traced here: 98.7 us
  Pallas kernels  56.7 us (57%)
  waiting for transfers between devices  20.4 us (21%)
  starting transfers between devices  18.9 us (19%)
  local copies, waits for them, and re-layouts  2.45 us (2%)
    pallas_call x9, Pallas kernels, project(): pl.pallas_call(functools.partial(project_kernel, local, infos), out_shape...  25.9 us
    pallas_call x1, Pallas kernels, apply(): pl.pallas_call(functools.partial(apply_kernel, nslab, slots, nsum, pieces...  22.2 us
    ppermute x2, waiting for transfers between devices, gather_and_project(): up = lax.ppermute(up, AXES, onward)  14.7 us
    ppermute x8, starting transfers between devices, gather_and_project(): near = [lax.ppermute(x, AXES, sibling) for x in near]  11.8 us
    pallas_call x1, Pallas kernels, split_bands(): pl.pallas_call(functools.partial(split_bands_kernel, natoms // nslab), gr...  7.44 us
    ppermute x2, starting transfers between devices, gather_and_project(): up = lax.ppermute(up, AXES, onward)  2.6 us
    ppermute x1, starting transfers between devices, gather_and_project(): up = lax.ppermute(mine, AXES, onward)  2.18 us
  transfers between devices with their start and end apart: 16, of which 8 were waited for; matrix products, arithmetic and copies ran while one was open for 2% of the time, Pallas kernels for 24%

profile of v3, /device:TPU:1, one launch (start us, length us, event | category | flops | bytes accessed | tf_op | source)
XLA Modules:
  0.0 98.7 jit_solution(495025925952609179)
XLA Ops:
  0.0 1.2 %begin.1 = (f32[8,512]{1,0:T(8,128)S(1)}, f32[264,512]{1,0:T(8,128)S(1)}) custom-call(s32[1,512]{1,0:T(1,128)} %bitcast.7, s32[1,512]{1,0:T(1,128)} %bitcast.8, f32[512,512]{1,0:T(8,128)} %refs_1_.3), custom_call_target="tpu_custom_call" | custom-call | tf_op jit(solution)/shard_map/begin/pallas_call | solution.py:173
  1.2 2.2 %collective-permute-start = (f32[264,512]{1,0:T(8,128)S(1)}, f32[264,512]{1,0:T(8,128)S(1)}, u32[]{:S(2)}, u32[]{:S(2)}) collective-permute-start(f32[264,512]{1,0:T(8,128)S(1)} %get-tuple-element.106), channel_id=1, source_target_pairs={{0,2},{2,4},{4,6},{6,7},{7,5},{5,3},{3,1},{1,0},{8,10},{10,12},{12... | collective-permute-start | bytes 1622024 | tf_op jit(solution)/shard_map/ppermute | solution.py:582
  4.9 0.9 copy-done.1
  5.8 7.4 %split_bands.1 = (bf16[512,16,256]{2,1,0:T(8,128)(2,1)S(1)}, f32[8,64,128]{2,1,0:T(8,128)S(1)}) custom-call(f32[16,32768]{1,0:T(8,128)} %bitcast.6, f32[64,768]{1,0:T(8,128)S(1)} %bitcast.5, s32[8,768]{1,0:T(8,128)S(1)} %broadcast_in_dim.2.channels_ref), custom_call_target="tpu_custom_call" | custom-call | flops 4194304 | bytes 6291456 | tf_op jit(solution)/shard_map/split_bands/pallas_call | solution.py:84
  13.3 3.0 %project.9.refs_18_ = f32[128,256]{1,0:T(8,128)S(1)} custom-call(s32[51]{0:T(128)S(1)} %reshape.22.place_ref, bf16[512,16,256]{2,1,0:T(8,128)(2,1)S(1)} %get-tuple-element.107.x_ref, f32[8,512]{1,0:T(8,128)S(1)} %get-tuple-element.108.refs_0_, f32[512,512]{1,0:T(8,128)S(1)} %copy-done), custom_call_target="tpu_custom_call" | custom-call | flops 134217728 | bytes 5242880 | tf_op jit(solution)/shard_map/project/pallas_call | solution.py:286
  16.3 1.9 %project.10 = (f32[128,256]{1,0:T(8,128)S(1)}, f32[128,256]{1,0:T(8,128)S(1)}) custom-call(s32[51]{0:T(128)S(1)} %reshape.22.place_ref, bf16[512,16,256]{2,1,0:T(8,128)(2,1)S(1)} %get-tuple-element.107.x_ref, f32[264,512]{1,0:T(8,128)S(1)} %collective-permute-done.refs_0_.refs_2_, f32[264,512]{1,0:T(8,128)S(1)} %collective-permute-done.1.refs_1_.refs_3_), custom_call_target="tpu_custom_call" | custom-call | flops 134217728 | bytes 5242880 | tf_op jit(solution)/shard_map/project/pallas_call | solution.py:286
  18.2 3.5 %collective-permute-start.2 = (f32[264,512]{1,0:T(8,128)S(1)}, f32[264,512]{1,0:T(8,128)S(1)}, u32[]{:S(2)}, u32[]{:S(2)}) collective-permute-start(f32[264,512]{1,0:T(8,128)S(1)} %collective-permute-done.refs_0_.refs_2_), channel_id=1, source_target_pairs={{0,8},{1,9},{2,10},{3,11},{4,12},{5,13},{6,14},{7,15},{8,0},{9,1},... | collective-permute-start | bytes 1622024 | tf_op jit(solution)/shard_map/ppermute | solution.py:613
  21.7 1.8 %collective-permute-start.4 = (f32[264,512]{1,0:T(8,128)S(1)}, f32[264,512]{1,0:T(8,128)S(1)}, u32[]{:S(2)}, u32[]{:S(2)}) collective-permute-start(f32[264,512]{1,0:T(8,128)S(1)} %collective-permute-done.refs_0_.refs_2_), channel_id=1, source_target_pairs={{0,2},{2,4},{4,6},{6,7},{7,5},{5,3},{3,1},{1,0},{8,10},{10,12},{12... | collective-permute-start | bytes 1622024 | tf_op jit(solution)/shard_map/ppermute | solution.py:604
  24.0 3.5 %project.11 = (f32[128,256]{1,0:T(8,128)S(1)}, f32[128,256]{1,0:T(8,128)S(1)}) custom-call(s32[51]{0:T(128)S(1)} %reshape.22.place_ref, bf16[512,16,256]{2,1,0:T(8,128)(2,1)S(1)} %get-tuple-element.107.x_ref, f32[264,512]{1,0:T(8,128)S(1)} %collective-permute-done.2.refs_0_.refs_4_, f32[264,512]{1,0:T(8,128)S(1)} %collective-permute-done.3.refs_1_.refs_5_), custom_call_target="tpu_custom_call" | custom-call | flops 134217728 | bytes 5242880 | tf_op jit(solution)/shard_map/project/pallas_call | solution.py:286
  27.5 7.6 %collective-permute-done.4.refs_0_.refs_6_ = f32[264,512]{1,0:T(8,128)S(1)} collective-permute-done((f32[264,512]{1,0:T(8,128)S(1)}, f32[264,512]{1,0:T(8,128)S(1)}, u32[]{:S(2)}, u32[]{:S(2)}) %collective-permute-start.4) | collective-permute-done | bytes 540704 | tf_op jit(solution)/shard_map/ppermute | solution.py:604
  35.1 1.5 %collective-permute-done.5.refs_1_.refs_7_ = f32[264,512]{1,0:T(8,128)S(1)} collective-permute-done((f32[264,512]{1,0:T(8,128)S(1)}, f32[264,512]{1,0:T(8,128)S(1)}, u32[]{:S(2)}, u32[]{:S(2)}) %collective-permute-start.5) | collective-permute-done | bytes 540704 | tf_op jit(solution)/shard_map/ppermute | solution.py:605
  36.7 1.9 %project.12 = (f32[128,256]{1,0:T(8,128)S(1)}, f32[128,256]{1,0:T(8,128)S(1)}) custom-call(s32[51]{0:T(128)S(1)} %reshape.22.place_ref, bf16[512,16,256]{2,1,0:T(8,128)(2,1)S(1)} %get-tuple-element.107.x_ref, f32[264,512]{1,0:T(8,128)S(1)} %collective-permute-done.4.refs_0_.refs_6_, f32[264,512]{1,0:T(8,128)S(1)} %collective-permute-done.5.refs_1_.refs_7_), custom_call_target="tpu_custom_call" | custom-call | flops 134217728 | bytes 5242880 | tf_op jit(solution)/shard_map/project/pallas_call | solution.py:286
  38.6 3.8 %collective-permute-start.6 = (f32[264,512]{1,0:T(8,128)S(1)}, f32[264,512]{1,0:T(8,128)S(1)}, u32[]{:S(2)}, u32[]{:S(2)}) collective-permute-start(f32[264,512]{1,0:T(8,128)S(1)} %collective-permute-done.4.refs_0_.refs_6_), channel_id=1, source_target_pairs={{0,8},{1,9},{2,10},{3,11},{4,12},{5,13},{6,14},{7,15},{8,0},{9,1},... | collective-permute-start | bytes 1622024 | tf_op jit(solution)/shard_map/ppermute | solution.py:613
  44.7 4.1 %project.13 = (f32[128,256]{1,0:T(8,128)S(1)}, f32[128,256]{1,0:T(8,128)S(1)}) custom-call(s32[51]{0:T(128)S(1)} %reshape.22.place_ref, bf16[512,16,256]{2,1,0:T(8,128)(2,1)S(1)} %get-tuple-element.107.x_ref, f32[264,512]{1,0:T(8,128)S(1)} %collective-permute-done.6.refs_0_.refs_8_, f32[264,512]{1,0:T(8,128)S(1)} %collective-permute-done.7.refs_1_.refs_9_), custom_call_target="tpu_custom_call" | custom-call | flops 134217728 | bytes 5242880 | tf_op jit(solution)/shard_map/project/pallas_call | solution.py:286
  48.8 7.1 %collective-permute-done.8.refs_0_.refs_10_ = f32[264,512]{1,0:T(8,128)S(1)} collective-permute-done((f32[264,512]{1,0:T(8,128)S(1)}, f32[264,512]{1,0:T(8,128)S(1)}, u32[]{:S(2)}, u32[]{:S(2)}) %collective-permute-start.8) | collective-permute-done | bytes 540704 | tf_op jit(solution)/shard_map/ppermute | solution.py:604
  56.3 3.0 %project.14 = (f32[128,256]{1,0:T(8,128)S(1)}, f32[128,256]{1,0:T(8,128)S(1)}) custom-call(s32[51]{0:T(128)S(1)} %reshape.22.place_ref, bf16[512,16,256]{2,1,0:T(8,128)(2,1)S(1)} %get-tuple-element.107.x_ref, f32[264,512]{1,0:T(8,128)S(1)} %collective-permute-done.8.refs_0_.refs_10_, f32[264,512]{1,0:T(8,128)S(1)} %collective-permute-done.9.refs_1_.refs_11_), custom_call_target="tpu_custom_call" | custom-call | flops 134217728 | bytes 5242880 | tf_op jit(solution)/shard_map/project/pallas_call | solution.py:286
  59.3 2.7 %collective-permute-start.10 = (f32[264,512]{1,0:T(8,128)S(1)}, f32[264,512]{1,0:T(8,128)S(1)}, u32[]{:S(2)}, u32[]{:S(2)}) collective-permute-start(f32[264,512]{1,0:T(8,128)S(1)} %collective-permute-done.8.refs_0_.refs_10_), channel_id=1, source_target_pairs={{0,8},{1,9},{2,10},{3,11},{4,12},{5,13},{6,14},{7,15},{8,0},{9,1},... | collective-permute-start | bytes 1622024 | tf_op jit(solution)/shard_map/ppermute | solution.py:613
  62.1 0.9 collective-permute-start.12
  64.4 4.0 %project.15 = (f32[128,256]{1,0:T(8,128)S(1)}, f32[128,256]{1,0:T(8,128)S(1)}) custom-call(s32[51]{0:T(128)S(1)} %reshape.22.place_ref, bf16[512,16,256]{2,1,0:T(8,128)(2,1)S(1)} %get-tuple-element.107.x_ref, f32[264,512]{1,0:T(8,128)S(1)} %collective-permute-done.10.refs_0_.refs_12_, f32[264,512]{1,0:T(8,128)S(1)} %collective-permute-done.11.refs_1_.refs_13_), custom_call_target="tpu_custom_call" | custom-call | flops 134217728 | bytes 5242880 | tf_op jit(solution)/shard_map/project/pallas_call | solution.py:286
  68.4 1.8 %collective-permute-done.13.refs_1_.refs_15_ = f32[128,512]{1,0:T(8,128)S(1)} collective-permute-done((f32[128,512]{1,0:T(8,128)S(1)}, f32[128,512]{1,0:T(8,128)S(1)}, u32[]{:S(2)}, u32[]{:S(2)}) %collective-permute-start.13) | collective-permute-done | bytes 262176 | tf_op jit(solution)/shard_map/ppermute | solution.py:608
  70.3 1.6 %collective-permute-start.14 = (f32[136,512]{1,0:T(8,128)S(1)}, f32[136,512]{1,0:T(8,128)S(1)}, u32[]{:S(2)}, u32[]{:S(2)}) collective-permute-start(f32[136,512]{1,0:T(8,128)S(1)} %collective-permute-done.12.refs_0_.refs_14_), channel_id=1, source_target_pairs={{0,8},{1,9},{2,10},{3,11},{4,12},{5,13},{6,14},{7,15},{8,0},{9,1},... | collective-permute-start | bytes 835592 | tf_op jit(solution)/shard_map/ppermute | solution.py:602
  71.9 2.1 %project.16 = (f32[128,256]{1,0:T(8,128)S(1)}, f32[128,256]{1,0:T(8,128)S(1)}) custom-call(s32[51]{0:T(128)S(1)} %reshape.22.place_ref, bf16[512,16,256]{2,1,0:T(8,128)(2,1)S(1)} %get-tuple-element.107.x_ref, f32[136,512]{1,0:T(8,128)S(1)} %collective-permute-done.12.refs_0_.refs_14_, f32[128,512]{1,0:T(8,128)S(1)} %collective-permute-done.13.refs_1_.refs_15_), custom_call_target="tpu_custom_call" | custom-call | flops 67108864 | bytes 4718592 | tf_op jit(solution)/shard_map/project/pallas_call | solution.py:286
  74.0 2.4 %project.17 = (f32[128,256]{1,0:T(8,128)S(1)}, f32[128,256]{1,0:T(8,128)S(1)}) custom-call(s32[51]{0:T(128)S(1)} %reshape.22.place_ref, bf16[512,16,256]{2,1,0:T(8,128)(2,1)S(1)} %get-tuple-element.107.x_ref, f32[136,512]{1,0:T(8,128)S(1)} %collective-permute-done.14.refs_0_.refs_16_, f32[128,512]{1,0:T(8,128)S(1)} %collective-permute-done.15.refs_1_.refs_17_), custom_call_target="tpu_custom_call" | custom-call | flops 67108864 | bytes 4718592 | tf_op jit(solution)/shard_map/project/pallas_call | solution.py:286
  76.4 22.2 %apply.1 = f32[16,32768]{1,0:T(8,128)} custom-call(s32[51]{0:T(128)S(1)} %reshape.22.place_ref, f32[8,64,128]{2,1,0:T(8,128)S(1)} %get-tuple-element.110.coupling_ref, f32[8,512]{1,0:T(8,128)S(1)} %get-tuple-element.108.refs_0_, f32[512,512]{1,0:T(8,128)S(1)} %copy-done, f32[264,512]{1,0:T(8,128)S(1)} %collective-permute-done.refs_0_.refs_2_, ...), custom_call_target="tpu_custom_call" | custom-call | tf_op jit(solution)/shard_map/apply/pallas_call | solution.py:524
  (29 shorter events, 6.2 us)
Async XLA Ops:
  0.0 13.2 %copy-start = (f32[512,512]{1,0:T(8,128)S(1)}, f32[512,512]{1,0:T(8,128)}, u32[]{:S(2)}) copy-start(f32[512,512]{1,0:T(8,128)} %refs_1_.3) | copy-start | bytes 3145732
  1.2 15.0 %collective-permute-start = (f32[264,512]{1,0:T(8,128)S(1)}, f32[264,512]{1,0:T(8,128)S(1)}, u32[]{:S(2)}, u32[]{:S(2)}) collective-permute-start(f32[264,512]{1,0:T(8,128)S(1)} %get-tuple-element.106), channel_id=1, source_target_pairs={{0,2},{2,4},{4,6},{6,7},{7,5},{5,3},{3,1},{1,0},{8,10},{10,12},{12... | collective-permute-start | bytes 1622024 | tf_op jit(solution)/shard_map/ppermute | solution.py:582
  3.4 12.9 %collective-permute-start.1 = (f32[264,512]{1,0:T(8,128)S(1)}, f32[264,512]{1,0:T(8,128)S(1)}, u32[]{:S(2)}, u32[]{:S(2)}) collective-permute-start(f32[264,512]{1,0:T(8,128)S(1)} %get-tuple-element.106), channel_id=1, source_target_pairs={{2,0},{4,2},{6,4},{7,6},{5,7},{3,5},{1,3},{0,1},{10,8},{12,10},{14... | collective-permute-start | bytes 1622024 | tf_op jit(solution)/shard_map/ppermute | solution.py:583
  4.9 0.9 copy-start.1
  18.2 5.4 %collective-permute-start.2 = (f32[264,512]{1,0:T(8,128)S(1)}, f32[264,512]{1,0:T(8,128)S(1)}, u32[]{:S(2)}, u32[]{:S(2)}) collective-permute-start(f32[264,512]{1,0:T(8,128)S(1)} %collective-permute-done.refs_0_.refs_2_), channel_id=1, source_target_pairs={{0,8},{1,9},{2,10},{3,11},{4,12},{5,13},{6,14},{7,15},{8,0},{9,1},... | collective-permute-start | bytes 1622024 | tf_op jit(solution)/shard_map/ppermute | solution.py:613
  21.7 2.3 %collective-permute-start.3 = (f32[264,512]{1,0:T(8,128)S(1)}, f32[264,512]{1,0:T(8,128)S(1)}, u32[]{:S(2)}, u32[]{:S(2)}) collective-permute-start(f32[264,512]{1,0:T(8,128)S(1)} %collective-permute-done.1.refs_1_.refs_3_), channel_id=1, source_target_pairs={{0,8},{1,9},{2,10},{3,11},{4,12},{5,13},{6,14},{7,15},{8,0},{9,1},... | collective-permute-start | bytes 1622024 | tf_op jit(solution)/shard_map/ppermute | solution.py:613
  21.7 13.4 %collective-permute-start.4 = (f32[264,512]{1,0:T(8,128)S(1)}, f32[264,512]{1,0:T(8,128)S(1)}, u32[]{:S(2)}, u32[]{:S(2)}) collective-permute-start(f32[264,512]{1,0:T(8,128)S(1)} %collective-permute-done.refs_0_.refs_2_), channel_id=1, source_target_pairs={{0,2},{2,4},{4,6},{6,7},{7,5},{5,3},{3,1},{1,0},{8,10},{10,12},{12... | collective-permute-start | bytes 1622024 | tf_op jit(solution)/shard_map/ppermute | solution.py:604
  23.6 13.1 %collective-permute-start.5 = (f32[264,512]{1,0:T(8,128)S(1)}, f32[264,512]{1,0:T(8,128)S(1)}, u32[]{:S(2)}, u32[]{:S(2)}) collective-permute-start(f32[264,512]{1,0:T(8,128)S(1)} %collective-permute-done.1.refs_1_.refs_3_), channel_id=1, source_target_pairs={{2,0},{4,2},{6,4},{7,6},{5,7},{3,5},{1,3},{0,1},{10,8},{12,10},{14... | collective-permute-start | bytes 1622024 | tf_op jit(solution)/shard_map/ppermute | solution.py:605
  38.6 5.4 %collective-permute-start.6 = (f32[264,512]{1,0:T(8,128)S(1)}, f32[264,512]{1,0:T(8,128)S(1)}, u32[]{:S(2)}, u32[]{:S(2)}) collective-permute-start(f32[264,512]{1,0:T(8,128)S(1)} %collective-permute-done.4.refs_0_.refs_6_), channel_id=1, source_target_pairs={{0,8},{1,9},{2,10},{3,11},{4,12},{5,13},{6,14},{7,15},{8,0},{9,1},... | collective-permute-start | bytes 1622024 | tf_op jit(solution)/shard_map/ppermute | solution.py:613
  42.4 2.3 %collective-permute-start.7 = (f32[264,512]{1,0:T(8,128)S(1)}, f32[264,512]{1,0:T(8,128)S(1)}, u32[]{:S(2)}, u32[]{:S(2)}) collective-permute-start(f32[264,512]{1,0:T(8,128)S(1)} %collective-permute-done.5.refs_1_.refs_7_), channel_id=1, source_target_pairs={{0,8},{1,9},{2,10},{3,11},{4,12},{5,13},{6,14},{7,15},{8,0},{9,1},... | collective-permute-start | bytes 1622024 | tf_op jit(solution)/shard_map/ppermute | solution.py:613
  42.5 13.4 %collective-permute-start.8 = (f32[264,512]{1,0:T(8,128)S(1)}, f32[264,512]{1,0:T(8,128)S(1)}, u32[]{:S(2)}, u32[]{:S(2)}) collective-permute-start(f32[264,512]{1,0:T(8,128)S(1)} %collective-permute-done.4.refs_0_.refs_6_), channel_id=1, source_target_pairs={{0,2},{2,4},{4,6},{6,7},{7,5},{5,3},{3,1},{1,0},{8,10},{10,12},{12... | collective-permute-start | bytes 1622024 | tf_op jit(solution)/shard_map/ppermute | solution.py:604
  43.2 13.1 %collective-permute-start.9 = (f32[264,512]{1,0:T(8,128)S(1)}, f32[264,512]{1,0:T(8,128)S(1)}, u32[]{:S(2)}, u32[]{:S(2)}) collective-permute-start(f32[264,512]{1,0:T(8,128)S(1)} %collective-permute-done.5.refs_1_.refs_7_), channel_id=1, source_target_pairs={{2,0},{4,2},{6,4},{7,6},{5,7},{3,5},{1,3},{0,1},{10,8},{12,10},{14... | collective-permute-start | bytes 1622024 | tf_op jit(solution)/shard_map/ppermute | solution.py:605
  59.3 4.4 %collective-permute-start.10 = (f32[264,512]{1,0:T(8,128)S(1)}, f32[264,512]{1,0:T(8,128)S(1)}, u32[]{:S(2)}, u32[]{:S(2)}) collective-permute-start(f32[264,512]{1,0:T(8,128)S(1)} %collective-permute-done.8.refs_0_.refs_10_), channel_id=1, source_target_pairs={{0,8},{1,9},{2,10},{3,11},{4,12},{5,13},{6,14},{7,15},{8,0},{9,1},... | collective-permute-start | bytes 1622024 | tf_op jit(solution)/shard_map/ppermute | solution.py:613
  62.0 2.3 %collective-permute-start.11 = (f32[264,512]{1,0:T(8,128)S(1)}, f32[264,512]{1,0:T(8,128)S(1)}, u32[]{:S(2)}, u32[]{:S(2)}) collective-permute-start(f32[264,512]{1,0:T(8,128)S(1)} %collective-permute-done.9.refs_1_.refs_11_), channel_id=1, source_target_pairs={{0,8},{1,9},{2,10},{3,11},{4,12},{5,13},{6,14},{7,15},{8,0},{9,1},... | collective-permute-start | bytes 1622024 | tf_op jit(solution)/shard_map/ppermute | solution.py:613
  62.1 8.1 %collective-permute-start.12 = (f32[136,512]{1,0:T(8,128)S(1)}, f32[136,512]{1,0:T(8,128)S(1)}, u32[]{:S(2)}, u32[]{:S(2)}) collective-permute-start(f32[136,512]{1,0:T(8,128)S(1)} %slice.6), channel_id=1, source_target_pairs={{0,2},{2,4},{4,6},{6,7},{7,5},{5,3},{3,1},{1,0},{8,10},{10,12},{12... | collective-permute-start | bytes 835592 | tf_op jit(solution)/shard_map/ppermute | solution.py:607
  63.1 7.2 %collective-permute-start.13 = (f32[128,512]{1,0:T(8,128)S(1)}, f32[128,512]{1,0:T(8,128)S(1)}, u32[]{:S(2)}, u32[]{:S(2)}) collective-permute-start(f32[128,512]{1,0:T(8,128)S(1)} %slice.7), channel_id=1, source_target_pairs={{2,0},{4,2},{6,4},{7,6},{5,7},{3,5},{1,3},{0,1},{10,8},{12,10},{14... | collective-permute-start | bytes 786440 | tf_op jit(solution)/shard_map/ppermute | solution.py:608
  70.3 3.7 %collective-permute-start.14 = (f32[136,512]{1,0:T(8,128)S(1)}, f32[136,512]{1,0:T(8,128)S(1)}, u32[]{:S(2)}, u32[]{:S(2)}) collective-permute-start(f32[136,512]{1,0:T(8,128)S(1)} %collective-permute-done.12.refs_0_.refs_14_), channel_id=1, source_target_pairs={{0,8},{1,9},{2,10},{3,11},{4,12},{5,13},{6,14},{7,15},{8,0},{9,1},... | collective-permute-start | bytes 835592 | tf_op jit(solution)/shard_map/ppermute | solution.py:602
  71.9 2.1 %collective-permute-start.15 = (f32[128,512]{1,0:T(8,128)S(1)}, f32[128,512]{1,0:T(8,128)S(1)}, u32[]{:S(2)}, u32[]{:S(2)}) collective-permute-start(f32[128,512]{1,0:T(8,128)S(1)} %collective-permute-done.13.refs_1_.refs_15_), channel_id=1, source_target_pairs={{0,8},{1,9},{2,10},{3,11},{4,12},{5,13},{6,14},{7,15},{8,0},{9,1},... | collective-permute-start | bytes 786440 | tf_op jit(solution)/shard_map/ppermute | solution.py:602

commit v4 on v2

--- a/solution.py
+++ b/solution.py
@@ -551,7 +551,9 @@
 
     where = [(0, 0, None)]
     for step in range(1, reach):
-        where += [(-step, 0, False), (step, 0, False), (-step, 0, True), (step, 0, True)]
+        where += [(1 - step, 0, True), (step - 1, 0, True)] if step > 1 else []
+        where += [(-step, 0, False), (step, 0, False)]
+    where += [(1 - reach, 0, True), (reach - 1, 0, True)]
     where += [(reach, 0, False), (reach, quarter, False), (reach, 0, True), (reach, quarter, True)]
     boxes = split.shape[0] // nslab
 
@@ -591,8 +593,11 @@
     project_new()
     up, down, projections, place = lax.optimization_barrier((up, down, projections, place))
     projections = list(projections)
+    near = []
     for step in range(1, reach + 1):
         last = step == reach
+        for array in near:
+            add(array)
         for array in (up,) if last else (up, down):
             infos.append((add(array), len(pieces) - 1))
         if last:
@@ -605,14 +610,11 @@
             up = lax.ppermute(up[: INFO + quarter], AXES, onward)
             down = lax.ppermute(down[INFO + quarter :], AXES, backward)
         project_new()
-        near, projections = lax.optimization_barrier((near, projections))
+        up, down, near, projections = lax.optimization_barrier((up, down, near, projections))
         near, projections = list(near), list(projections)
-        add(near[0])
-        add(near[1], len(arrays) - 1 if last else None)
-        project_new()
-        if not last:
-            up, down, projections = lax.optimization_barrier((up, down, projections))
-            projections = list(projections)
+    add(near[0])
+    add(near[1], len(arrays) - 1)
+    project_new()
     return arrays, pieces, infos, projections, place
 
 

time: 90.4 us -> 86.3 us (0.955)
  Pallas kernels: 58.9 us -> 53 us
  starting transfers between devices: 13.1 us -> 17.7 us
  waiting for transfers between devices: 14.7 us -> 12.6 us
    pallas_call x9 -> x6, Pallas kernels: 26.9 us -> 21.6 us  [project(): pl.pallas_call(functools.partial(project_kernel, local, infos), out_shape...]
    ppermute x8, starting transfers between devices: 6.46 us -> 9.91 us  [gather_and_project(): near = [lax.ppermute(up, AXES, sibling), lax.ppermute(down, AXES, sibling)]]
    ppermute x2, waiting for transfers between devices: 11.2 us -> 7.75 us  [gather_and_project(): up = lax.ppermute(up, AXES, onward)]
    ppermute x1, waiting for transfers between devices: 0.34 us -> 2.33 us  [gather_and_project(): down = lax.ppermute(down[INFO + quarter:], AXES, backward)]
  transfers between devices with their start and end apart: 16 -> 16, of which waited for: 5 -> 6; matrix products, arithmetic and copies ran while one was open for 2% -> 2% of each run, Pallas kernels for 35% -> 30%
where the time goes in v4:
time: 86.3 us; the launch traced here: 86 us
  Pallas kernels  53 us (61%)
  starting transfers between devices  17.7 us (21%)
  waiting for transfers between devices  12.6 us (15%)
  local copies, waits for them, and re-layouts  2.45 us (3%)
    pallas_call x1, Pallas kernels, apply(): pl.pallas_call(functools.partial(apply_kernel, nslab, slots, nsum, pieces...  22.8 us
    pallas_call x6, Pallas kernels, project(): pl.pallas_call(functools.partial(project_kernel, local, infos), out_shape...  21.6 us
    ppermute x8, starting transfers between devices, gather_and_project(): near = [lax.ppermute(up, AXES, sibling), lax.ppermute(down, AXES, sibling)]  9.91 us
    ppermute x2, waiting for transfers between devices, gather_and_project(): up = lax.ppermute(up, AXES, onward)  7.75 us
    pallas_call x1, Pallas kernels, split_bands(): pl.pallas_call(functools.partial(split_bands_kernel, natoms // nslab), gr...  7.44 us
    ppermute x2, starting transfers between devices, gather_and_project(): up = lax.ppermute(up, AXES, onward)  3.33 us
    ppermute x2, waiting for transfers between devices, gather_and_project(): down = lax.ppermute(down, AXES, backward)  2.37 us
    ppermute x1, waiting for transfers between devices, gather_and_project(): down = lax.ppermute(down[INFO + quarter:], AXES, backward)  2.33 us
  transfers between devices with their start and end apart: 16, of which 6 were waited for; matrix products, arithmetic and copies ran while one was open for 2% of the time, Pallas kernels for 30%

profile of v4, /device:TPU:1, one launch (start us, length us, event | category | flops | bytes accessed | tf_op | source)
XLA Modules:
  0.0 86.0 jit_solution(12523644084474416281)
XLA Ops:
  0.0 1.2 %begin.1 = (f32[8,512]{1,0:T(8,128)S(1)}, f32[264,512]{1,0:T(8,128)S(1)}) custom-call(s32[1,512]{1,0:T(1,128)} %bitcast.7, s32[1,512]{1,0:T(1,128)} %bitcast.8, f32[512,512]{1,0:T(8,128)} %refs_1_.3), custom_call_target="tpu_custom_call" | custom-call | tf_op jit(solution)/shard_map/begin/pallas_call | solution.py:173
  1.2 2.2 %collective-permute-start = (f32[264,512]{1,0:T(8,128)S(1)}, f32[264,512]{1,0:T(8,128)S(1)}, u32[]{:S(2)}, u32[]{:S(2)}) collective-permute-start(f32[264,512]{1,0:T(8,128)S(1)} %get-tuple-element.79), channel_id=1, source_target_pairs={{0,2},{2,4},{4,6},{6,7},{7,5},{5,3},{3,1},{1,0},{8,10},{10,12},{12... | collective-permute-start | bytes 1622024 | tf_op jit(solution)/shard_map/ppermute | solution.py:584
  3.4 0.7 constant_dynamic-slice_fusion
  4.9 0.9 %copy-done.1 = f32[8,8,768]{2,1,0:T(8,128)S(1)} copy-done((f32[8,8,768]{2,1,0:T(8,128)S(1)}, f32[8,8,768]{2,1,0:T(8,128)}, u32[]{:S(2)}) %copy-start.1) | copy-done | bytes 196632
  5.8 7.4 %split_bands.1 = (bf16[512,16,256]{2,1,0:T(8,128)(2,1)S(1)}, f32[8,64,128]{2,1,0:T(8,128)S(1)}) custom-call(f32[16,32768]{1,0:T(8,128)} %bitcast.6, f32[64,768]{1,0:T(8,128)S(1)} %bitcast.5, s32[8,768]{1,0:T(8,128)S(1)} %broadcast_in_dim.2.channels_ref), custom_call_target="tpu_custom_call" | custom-call | flops 4194304 | bytes 6291456 | tf_op jit(solution)/shard_map/split_bands/pallas_call | solution.py:84
  13.3 3.0 %project.6.refs_18_ = f32[128,256]{1,0:T(8,128)S(1)} custom-call(s32[51]{0:T(128)S(1)} %reshape.22.place_ref, bf16[512,16,256]{2,1,0:T(8,128)(2,1)S(1)} %get-tuple-element.80.x_ref, f32[8,512]{1,0:T(8,128)S(1)} %get-tuple-element.81.refs_0_, f32[512,512]{1,0:T(8,128)S(1)} %copy-done), custom_call_target="tpu_custom_call" | custom-call | flops 134217728 | bytes 5242880 | tf_op jit(solution)/shard_map/project/pallas_call | solution.py:286
  16.2 2.6 %collective-permute-start.2 = (f32[264,512]{1,0:T(8,128)S(1)}, f32[264,512]{1,0:T(8,128)S(1)}, u32[]{:S(2)}, u32[]{:S(2)}) collective-permute-start(f32[264,512]{1,0:T(8,128)S(1)} %collective-permute-done.refs_0_.refs_2_), channel_id=1, source_target_pairs={{0,2},{2,4},{4,6},{6,7},{7,5},{5,3},{3,1},{1,0},{8,10},{10,12},{12... | collective-permute-start | bytes 1622024 | tf_op jit(solution)/shard_map/ppermute | solution.py:607
  18.8 1.5 %collective-permute-start.4 = (f32[264,512]{1,0:T(8,128)S(1)}, f32[264,512]{1,0:T(8,128)S(1)}, u32[]{:S(2)}, u32[]{:S(2)}) collective-permute-start(f32[264,512]{1,0:T(8,128)S(1)} %collective-permute-done.refs_0_.refs_2_), channel_id=1, source_target_pairs={{0,8},{1,9},{2,10},{3,11},{4,12},{5,13},{6,14},{7,15},{8,0},{9,1},... | collective-permute-start | bytes 1622024 | tf_op jit(solution)/shard_map/ppermute | solution.py:605
  20.4 3.0 %project.7 = (f32[128,256]{1,0:T(8,128)S(1)}, f32[128,256]{1,0:T(8,128)S(1)}) custom-call(s32[51]{0:T(128)S(1)} %reshape.22.place_ref, bf16[512,16,256]{2,1,0:T(8,128)(2,1)S(1)} %get-tuple-element.80.x_ref, f32[264,512]{1,0:T(8,128)S(1)} %collective-permute-done.refs_0_.refs_2_, f32[264,512]{1,0:T(8,128)S(1)} %collective-permute-done.1.refs_1_.refs_3_), custom_call_target="tpu_custom_call" | custom-call | flops 134217728 | bytes 5242880 | tf_op jit(solution)/shard_map/project/pallas_call | solution.py:286
  23.4 5.8 %collective-permute-done.2.refs_2_.refs_6_ = f32[264,512]{1,0:T(8,128)S(1)} collective-permute-done((f32[264,512]{1,0:T(8,128)S(1)}, f32[264,512]{1,0:T(8,128)S(1)}, u32[]{:S(2)}, u32[]{:S(2)}) %collective-permute-start.2) | collective-permute-done | bytes 540704 | tf_op jit(solution)/shard_map/ppermute | solution.py:607
  29.2 1.9 %collective-permute-done.3.refs_3_.refs_7_ = f32[264,512]{1,0:T(8,128)S(1)} collective-permute-done((f32[264,512]{1,0:T(8,128)S(1)}, f32[264,512]{1,0:T(8,128)S(1)}, u32[]{:S(2)}, u32[]{:S(2)}) %collective-permute-start.3) | collective-permute-done | bytes 540704 | tf_op jit(solution)/shard_map/ppermute | solution.py:608
  31.1 0.7 collective-permute-start.6
  31.8 0.7 collective-permute-start.7
  32.6 3.0 %collective-permute-start.8 = (f32[264,512]{1,0:T(8,128)S(1)}, f32[264,512]{1,0:T(8,128)S(1)}, u32[]{:S(2)}, u32[]{:S(2)}) collective-permute-start(f32[264,512]{1,0:T(8,128)S(1)} %collective-permute-done.2.refs_2_.refs_6_), channel_id=1, source_target_pairs={{0,8},{1,9},{2,10},{3,11},{4,12},{5,13},{6,14},{7,15},{8,0},{9,1},... | collective-permute-start | bytes 1622024 | tf_op jit(solution)/shard_map/ppermute | solution.py:605
  35.6 4.9 %project.8 = (f32[128,256]{1,0:T(8,128)S(1)}, f32[128,256]{1,0:T(8,128)S(1)}, f32[128,256]{1,0:T(8,128)S(1)}, f32[128,256]{1,0:T(8,128)S(1)}) custom-call(s32[51]{0:T(128)S(1)} %reshape.22.place_ref, bf16[512,16,256]{2,1,0:T(8,128)(2,1)S(1)} %get-tuple-element.80.x_ref, f32[264,512]{1,0:T(8,128)S(1)} %collective-permute-done.4.refs_0_.refs_4_, ...), custom_call_target="tpu_custom_call" | custom-call | flops 268435456 | bytes 6291456 | tf_op jit(solution)/shard_map/project/pallas_call | solution.py:286
  40.5 1.9 %collective-permute-done.6.refs_2_.refs_10_ = f32[264,512]{1,0:T(8,128)S(1)} collective-permute-done((f32[264,512]{1,0:T(8,128)S(1)}, f32[264,512]{1,0:T(8,128)S(1)}, u32[]{:S(2)}, u32[]{:S(2)}) %collective-permute-start.6) | collective-permute-done | bytes 540704 | tf_op jit(solution)/shard_map/ppermute | solution.py:607
  42.9 3.6 %collective-permute-start.12 = (f32[264,512]{1,0:T(8,128)S(1)}, f32[264,512]{1,0:T(8,128)S(1)}, u32[]{:S(2)}, u32[]{:S(2)}) collective-permute-start(f32[264,512]{1,0:T(8,128)S(1)} %collective-permute-done.6.refs_2_.refs_10_), channel_id=1, source_target_pairs={{0,8},{1,9},{2,10},{3,11},{4,12},{5,13},{6,14},{7,15},{8,0},{9,1},... | collective-permute-start | bytes 1622024 | tf_op jit(solution)/shard_map/ppermute | solution.py:605
  47.2 1.0 %collective-permute-start.11 = (f32[128,512]{1,0:T(8,128)S(1)}, f32[128,512]{1,0:T(8,128)S(1)}, u32[]{:S(2)}, u32[]{:S(2)}) collective-permute-start(f32[128,512]{1,0:T(8,128)S(1)} %slice.7), channel_id=1, source_target_pairs={{2,0},{4,2},{6,4},{7,6},{5,7},{3,5},{1,3},{0,1},{10,8},{12,10},{14... | collective-permute-start | bytes 786440 | tf_op jit(solution)/shard_map/ppermute | solution.py:611
  48.2 3.8 %project.9 = (f32[128,256]{1,0:T(8,128)S(1)}, f32[128,256]{1,0:T(8,128)S(1)}, f32[128,256]{1,0:T(8,128)S(1)}, f32[128,256]{1,0:T(8,128)S(1)}) custom-call(s32[51]{0:T(128)S(1)} %reshape.22.place_ref, bf16[512,16,256]{2,1,0:T(8,128)(2,1)S(1)} %get-tuple-element.80.x_ref, f32[264,512]{1,0:T(8,128)S(1)} %collective-permute-done.8.refs_0_.refs_8_, ...), custom_call_target="tpu_custom_call" | custom-call | flops 268435456 | bytes 6291456 | tf_op jit(solution)/shard_map/project/pallas_call | solution.py:286
  52.1 2.3 %collective-permute-done.11.refs_3_.refs_15_ = f32[128,512]{1,0:T(8,128)S(1)} collective-permute-done((f32[128,512]{1,0:T(8,128)S(1)}, f32[128,512]{1,0:T(8,128)S(1)}, u32[]{:S(2)}, u32[]{:S(2)}) %collective-permute-start.11) | collective-permute-done | bytes 262176 | tf_op jit(solution)/shard_map/ppermute | solution.py:611
  54.5 1.6 %collective-permute-start.14 = (f32[136,512]{1,0:T(8,128)S(1)}, f32[136,512]{1,0:T(8,128)S(1)}, u32[]{:S(2)}, u32[]{:S(2)}) collective-permute-start(f32[136,512]{1,0:T(8,128)S(1)} %collective-permute-done.10.refs_2_.refs_14_), channel_id=1, source_target_pairs={{0,8},{1,9},{2,10},{3,11},{4,12},{5,13},{6,14},{7,15},{8,0},{9,1},... | collective-permute-start | bytes 835592 | tf_op jit(solution)/shard_map/ppermute | solution.py:605
  56.2 3.9 %project.10 = (f32[128,256]{1,0:T(8,128)S(1)}, f32[128,256]{1,0:T(8,128)S(1)}, f32[128,256]{1,0:T(8,128)S(1)}, f32[128,256]{1,0:T(8,128)S(1)}) custom-call(s32[51]{0:T(128)S(1)} %reshape.22.place_ref, bf16[512,16,256]{2,1,0:T(8,128)(2,1)S(1)} %get-tuple-element.80.x_ref, f32[264,512]{1,0:T(8,128)S(1)} %collective-permute-done.12.refs_0_.refs_12_, ...), custom_call_target="tpu_custom_call" | custom-call | flops 201326592 | bytes 5767168 | tf_op jit(solution)/shard_map/project/pallas_call | solution.py:286
  60.1 2.9 %project.11 = (f32[128,256]{1,0:T(8,128)S(1)}, f32[128,256]{1,0:T(8,128)S(1)}) custom-call(s32[51]{0:T(128)S(1)} %reshape.22.place_ref, bf16[512,16,256]{2,1,0:T(8,128)(2,1)S(1)} %get-tuple-element.80.x_ref, f32[136,512]{1,0:T(8,128)S(1)} %collective-permute-done.14.refs_0_.refs_16_, f32[128,512]{1,0:T(8,128)S(1)} %collective-permute-done.15.refs_1_.refs_17_), custom_call_target="tpu_custom_call" | custom-call | flops 67108864 | bytes 4718592 | tf_op jit(solution)/shard_map/project/pallas_call | solution.py:286
  63.1 22.8 %apply.1 = f32[16,32768]{1,0:T(8,128)} custom-call(s32[51]{0:T(128)S(1)} %reshape.22.place_ref, f32[8,64,128]{2,1,0:T(8,128)S(1)} %get-tuple-element.83.coupling_ref, f32[8,512]{1,0:T(8,128)S(1)} %get-tuple-element.81.refs_0_, f32[512,512]{1,0:T(8,128)S(1)} %copy-done, f32[264,512]{1,0:T(8,128)S(1)} %collective-permute-done.refs_0_.refs_2_, ...), custom_call_target="tpu_custom_call" | custom-call | tf_op jit(solution)/shard_map/apply/pallas_call | solution.py:524
  (26 shorter events, 2.1 us)
Async XLA Ops:
  0.0 13.2 %copy-start = (f32[512,512]{1,0:T(8,128)S(1)}, f32[512,512]{1,0:T(8,128)}, u32[]{:S(2)}) copy-start(f32[512,512]{1,0:T(8,128)} %refs_1_.3) | copy-start | bytes 3145732
  1.2 15.0 %collective-permute-start = (f32[264,512]{1,0:T(8,128)S(1)}, f32[264,512]{1,0:T(8,128)S(1)}, u32[]{:S(2)}, u32[]{:S(2)}) collective-permute-start(f32[264,512]{1,0:T(8,128)S(1)} %get-tuple-element.79), channel_id=1, source_target_pairs={{0,2},{2,4},{4,6},{6,7},{7,5},{5,3},{3,1},{1,0},{8,10},{10,12},{12... | collective-permute-start | bytes 1622024 | tf_op jit(solution)/shard_map/ppermute | solution.py:584
  3.4 12.9 %collective-permute-start.1 = (f32[264,512]{1,0:T(8,128)S(1)}, f32[264,512]{1,0:T(8,128)S(1)}, u32[]{:S(2)}, u32[]{:S(2)}) collective-permute-start(f32[264,512]{1,0:T(8,128)S(1)} %get-tuple-element.79), channel_id=1, source_target_pairs={{2,0},{4,2},{6,4},{7,6},{5,7},{3,5},{1,3},{0,1},{10,8},{12,10},{14... | collective-permute-start | bytes 1622024 | tf_op jit(solution)/shard_map/ppermute | solution.py:585
  4.9 0.9 %copy-start.1 = (f32[8,8,768]{2,1,0:T(8,128)S(1)}, f32[8,8,768]{2,1,0:T(8,128)}, u32[]{:S(2)}) copy-start(f32[8,8,768]{2,1,0:T(8,128)} %param.12) | copy-start | bytes 589828
  16.2 12.9 %collective-permute-start.2 = (f32[264,512]{1,0:T(8,128)S(1)}, f32[264,512]{1,0:T(8,128)S(1)}, u32[]{:S(2)}, u32[]{:S(2)}) collective-permute-start(f32[264,512]{1,0:T(8,128)S(1)} %collective-permute-done.refs_0_.refs_2_), channel_id=1, source_target_pairs={{0,2},{2,4},{4,6},{6,7},{7,5},{5,3},{3,1},{1,0},{8,10},{10,12},{12... | collective-permute-start | bytes 1622024 | tf_op jit(solution)/shard_map/ppermute | solution.py:607
  18.8 12.3 %collective-permute-start.3 = (f32[264,512]{1,0:T(8,128)S(1)}, f32[264,512]{1,0:T(8,128)S(1)}, u32[]{:S(2)}, u32[]{:S(2)}) collective-permute-start(f32[264,512]{1,0:T(8,128)S(1)} %collective-permute-done.1.refs_1_.refs_3_), channel_id=1, source_target_pairs={{2,0},{4,2},{6,4},{7,6},{5,7},{3,5},{1,3},{0,1},{10,8},{12,10},{14... | collective-permute-start | bytes 1622024 | tf_op jit(solution)/shard_map/ppermute | solution.py:608
  18.8 12.3 %collective-permute-start.4 = (f32[264,512]{1,0:T(8,128)S(1)}, f32[264,512]{1,0:T(8,128)S(1)}, u32[]{:S(2)}, u32[]{:S(2)}) collective-permute-start(f32[264,512]{1,0:T(8,128)S(1)} %collective-permute-done.refs_0_.refs_2_), channel_id=1, source_target_pairs={{0,8},{1,9},{2,10},{3,11},{4,12},{5,13},{6,14},{7,15},{8,0},{9,1},... | collective-permute-start | bytes 1622024 | tf_op jit(solution)/shard_map/ppermute | solution.py:605
  20.4 10.7 %collective-permute-start.5 = (f32[264,512]{1,0:T(8,128)S(1)}, f32[264,512]{1,0:T(8,128)S(1)}, u32[]{:S(2)}, u32[]{:S(2)}) collective-permute-start(f32[264,512]{1,0:T(8,128)S(1)} %collective-permute-done.1.refs_1_.refs_3_), channel_id=1, source_target_pairs={{0,8},{1,9},{2,10},{3,11},{4,12},{5,13},{6,14},{7,15},{8,0},{9,1},... | collective-permute-start | bytes 1622024 | tf_op jit(solution)/shard_map/ppermute | solution.py:605
  31.1 11.3 %collective-permute-start.6 = (f32[264,512]{1,0:T(8,128)S(1)}, f32[264,512]{1,0:T(8,128)S(1)}, u32[]{:S(2)}, u32[]{:S(2)}) collective-permute-start(f32[264,512]{1,0:T(8,128)S(1)} %collective-permute-done.2.refs_2_.refs_6_), channel_id=1, source_target_pairs={{0,2},{2,4},{4,6},{6,7},{7,5},{5,3},{3,1},{1,0},{8,10},{10,12},{12... | collective-permute-start | bytes 1622024 | tf_op jit(solution)/shard_map/ppermute | solution.py:607
  31.8 11.0 %collective-permute-start.7 = (f32[264,512]{1,0:T(8,128)S(1)}, f32[264,512]{1,0:T(8,128)S(1)}, u32[]{:S(2)}, u32[]{:S(2)}) collective-permute-start(f32[264,512]{1,0:T(8,128)S(1)} %collective-permute-done.3.refs_3_.refs_7_), channel_id=1, source_target_pairs={{2,0},{4,2},{6,4},{7,6},{5,7},{3,5},{1,3},{0,1},{10,8},{12,10},{14... | collective-permute-start | bytes 1622024 | tf_op jit(solution)/shard_map/ppermute | solution.py:608
  32.6 10.3 %collective-permute-start.8 = (f32[264,512]{1,0:T(8,128)S(1)}, f32[264,512]{1,0:T(8,128)S(1)}, u32[]{:S(2)}, u32[]{:S(2)}) collective-permute-start(f32[264,512]{1,0:T(8,128)S(1)} %collective-permute-done.2.refs_2_.refs_6_), channel_id=1, source_target_pairs={{0,8},{1,9},{2,10},{3,11},{4,12},{5,13},{6,14},{7,15},{8,0},{9,1},... | collective-permute-start | bytes 1622024 | tf_op jit(solution)/shard_map/ppermute | solution.py:605
  35.6 7.3 %collective-permute-start.9 = (f32[264,512]{1,0:T(8,128)S(1)}, f32[264,512]{1,0:T(8,128)S(1)}, u32[]{:S(2)}, u32[]{:S(2)}) collective-permute-start(f32[264,512]{1,0:T(8,128)S(1)} %collective-permute-done.3.refs_3_.refs_7_), channel_id=1, source_target_pairs={{0,8},{1,9},{2,10},{3,11},{4,12},{5,13},{6,14},{7,15},{8,0},{9,1},... | collective-permute-start | bytes 1622024 | tf_op jit(solution)/shard_map/ppermute | solution.py:605
  42.9 11.6 %collective-permute-start.12 = (f32[264,512]{1,0:T(8,128)S(1)}, f32[264,512]{1,0:T(8,128)S(1)}, u32[]{:S(2)}, u32[]{:S(2)}) collective-permute-start(f32[264,512]{1,0:T(8,128)S(1)} %collective-permute-done.6.refs_2_.refs_10_), channel_id=1, source_target_pairs={{0,8},{1,9},{2,10},{3,11},{4,12},{5,13},{6,14},{7,15},{8,0},{9,1},... | collective-permute-start | bytes 1622024 | tf_op jit(solution)/shard_map/ppermute | solution.py:605
  46.5 7.9 %collective-permute-start.13 = (f32[264,512]{1,0:T(8,128)S(1)}, f32[264,512]{1,0:T(8,128)S(1)}, u32[]{:S(2)}, u32[]{:S(2)}) collective-permute-start(f32[264,512]{1,0:T(8,128)S(1)} %collective-permute-done.7.refs_3_.refs_11_), channel_id=1, source_target_pairs={{0,8},{1,9},{2,10},{3,11},{4,12},{5,13},{6,14},{7,15},{8,0},{9,1},... | collective-permute-start | bytes 1622024 | tf_op jit(solution)/shard_map/ppermute | solution.py:605
  46.6 7.8 %collective-permute-start.10 = (f32[136,512]{1,0:T(8,128)S(1)}, f32[136,512]{1,0:T(8,128)S(1)}, u32[]{:S(2)}, u32[]{:S(2)}) collective-permute-start(f32[136,512]{1,0:T(8,128)S(1)} %slice.6), channel_id=1, source_target_pairs={{0,2},{2,4},{4,6},{6,7},{7,5},{5,3},{3,1},{1,0},{8,10},{10,12},{12... | collective-permute-start | bytes 835592 | tf_op jit(solution)/shard_map/ppermute | solution.py:610
  47.2 7.2 %collective-permute-start.11 = (f32[128,512]{1,0:T(8,128)S(1)}, f32[128,512]{1,0:T(8,128)S(1)}, u32[]{:S(2)}, u32[]{:S(2)}) collective-permute-start(f32[128,512]{1,0:T(8,128)S(1)} %slice.7), channel_id=1, source_target_pairs={{2,0},{4,2},{6,4},{7,6},{5,7},{3,5},{1,3},{0,1},{10,8},{12,10},{14... | collective-permute-start | bytes 786440 | tf_op jit(solution)/shard_map/ppermute | solution.py:611
  54.5 5.6 %collective-permute-start.14 = (f32[136,512]{1,0:T(8,128)S(1)}, f32[136,512]{1,0:T(8,128)S(1)}, u32[]{:S(2)}, u32[]{:S(2)}) collective-permute-start(f32[136,512]{1,0:T(8,128)S(1)} %collective-permute-done.10.refs_2_.refs_14_), channel_id=1, source_target_pairs={{0,8},{1,9},{2,10},{3,11},{4,12},{5,13},{6,14},{7,15},{8,0},{9,1},... | collective-permute-start | bytes 835592 | tf_op jit(solution)/shard_map/ppermute | solution.py:605
  56.1 4.0 %collective-permute-start.15 = (f32[128,512]{1,0:T(8,128)S(1)}, f32[128,512]{1,0:T(8,128)S(1)}, u32[]{:S(2)}, u32[]{:S(2)}) collective-permute-start(f32[128,512]{1,0:T(8,128)S(1)} %collective-permute-done.11.refs_3_.refs_15_), channel_id=1, source_target_pairs={{0,8},{1,9},{2,10},{3,11},{4,12},{5,13},{6,14},{7,15},{8,0},{9,1},... | collective-permute-start | bytes 786440 | tf_op jit(solution)/shard_map/ppermute | solution.py:605

commit v5 on v4

--- a/solution.py
+++ b/solution.py
@@ -610,6 +610,11 @@
             up = lax.ppermute(up[: INFO + quarter], AXES, onward)
             down = lax.ppermute(down[INFO + quarter :], AXES, backward)
         project_new()
+        if step + 1 == reach:
+            for array in near:
+                add(array)
+            near = []
+            project_new()
         up, down, near, projections = lax.optimization_barrier((up, down, near, projections))
         near, projections = list(near), list(projections)
     add(near[0])

time: 86.3 us -> 84.9 us (0.984)
  Pallas kernels: 53 us -> 55.7 us
  waiting for transfers between devices: 12.6 us -> 10.2 us
  starting transfers between devices: 17.7 us -> 16.6 us
    ppermute x1, waiting for transfers between devices: 2.33 us -> 0.01 us  [gather_and_project(): down = lax.ppermute(down[INFO + quarter:], AXES, backward)]
    pallas_call x6 -> x7, Pallas kernels: 21.6 us -> 23.8 us  [project(): pl.pallas_call(functools.partial(project_kernel, local, infos), out_shape...]
    ppermute x8, starting transfers between devices: 9.91 us -> 8.81 us  [gather_and_project(): near = [lax.ppermute(up, AXES, sibling), lax.ppermute(down, AXES, sibling)]]
  transfers between devices with their start and end apart: 16 -> 16, of which waited for: 6 -> 4; matrix products, arithmetic and copies ran while one was open for 2% -> 2% of each run, Pallas kernels for 30% -> 33%
where the time goes in v5:
time: 84.9 us; the launch traced here: 85.3 us
  Pallas kernels  55.7 us (66%)
  starting transfers between devices  16.6 us (20%)
  waiting for transfers between devices  10.2 us (12%)
  local copies, waits for them, and re-layouts  2.45 us (3%)
    pallas_call x7, Pallas kernels, project(): pl.pallas_call(functools.partial(project_kernel, local, infos), out_shape...  23.8 us
    pallas_call x1, Pallas kernels, apply(): pl.pallas_call(functools.partial(apply_kernel, nslab, slots, nsum, pieces...  23.3 us
    ppermute x8, starting transfers between devices, gather_and_project(): near = [lax.ppermute(up, AXES, sibling), lax.ppermute(down, AXES, sibling)]  8.81 us
    ppermute x2, waiting for transfers between devices, gather_and_project(): up = lax.ppermute(up, AXES, onward)  7.74 us
    pallas_call x1, Pallas kernels, split_bands(): pl.pallas_call(functools.partial(split_bands_kernel, natoms // nslab), gr...  7.44 us
    ppermute x2, starting transfers between devices, gather_and_project(): up = lax.ppermute(up, AXES, onward)  3.34 us
    ppermute x2, waiting for transfers between devices, gather_and_project(): down = lax.ppermute(down, AXES, backward)  2.4 us
    ppermute x1, starting transfers between devices, gather_and_project(): up = lax.ppermute(mine, AXES, onward)  2.18 us
  transfers between devices with their start and end apart: 16, of which 4 were waited for; matrix products, arithmetic and copies ran while one was open for 2% of the time, Pallas kernels for 33%

profile of v5, /device:TPU:1, one launch (start us, length us, event | category | flops | bytes accessed | tf_op | source)
XLA Modules:
  0.0 85.3 jit_solution(14624614801261985667)
XLA Ops:
  0.0 1.2 %begin.1 = (f32[8,512]{1,0:T(8,128)S(1)}, f32[264,512]{1,0:T(8,128)S(1)}) custom-call(s32[1,512]{1,0:T(1,128)} %bitcast.7, s32[1,512]{1,0:T(1,128)} %bitcast.8, f32[512,512]{1,0:T(8,128)} %refs_1_.3), custom_call_target="tpu_custom_call" | custom-call | tf_op jit(solution)/shard_map/begin/pallas_call | solution.py:173
  1.2 2.2 %collective-permute-start = (f32[264,512]{1,0:T(8,128)S(1)}, f32[264,512]{1,0:T(8,128)S(1)}, u32[]{:S(2)}, u32[]{:S(2)}) collective-permute-start(f32[264,512]{1,0:T(8,128)S(1)} %get-tuple-element.79), channel_id=1, source_target_pairs={{0,2},{2,4},{4,6},{6,7},{7,5},{5,3},{3,1},{1,0},{8,10},{10,12},{12... | collective-permute-start | bytes 1622024 | tf_op jit(solution)/shard_map/ppermute | solution.py:584
  3.4 0.7 constant_dynamic-slice_fusion
  4.2 0.7 broadcast_in_dim.2.channels_ref
  4.9 0.9 %copy-done.1 = f32[8,8,768]{2,1,0:T(8,128)S(1)} copy-done((f32[8,8,768]{2,1,0:T(8,128)S(1)}, f32[8,8,768]{2,1,0:T(8,128)}, u32[]{:S(2)}) %copy-start.1) | copy-done | bytes 196632
  5.8 7.4 %split_bands.1 = (bf16[512,16,256]{2,1,0:T(8,128)(2,1)S(1)}, f32[8,64,128]{2,1,0:T(8,128)S(1)}) custom-call(f32[16,32768]{1,0:T(8,128)} %bitcast.6, f32[64,768]{1,0:T(8,128)S(1)} %bitcast.5, s32[8,768]{1,0:T(8,128)S(1)} %broadcast_in_dim.2.channels_ref), custom_call_target="tpu_custom_call" | custom-call | flops 4194304 | bytes 6291456 | tf_op jit(solution)/shard_map/split_bands/pallas_call | solution.py:84
  13.3 3.0 %project.7.refs_18_ = f32[128,256]{1,0:T(8,128)S(1)} custom-call(s32[51]{0:T(128)S(1)} %reshape.22.place_ref, bf16[512,16,256]{2,1,0:T(8,128)(2,1)S(1)} %get-tuple-element.80.x_ref, f32[8,512]{1,0:T(8,128)S(1)} %get-tuple-element.81.refs_0_, f32[512,512]{1,0:T(8,128)S(1)} %copy-done), custom_call_target="tpu_custom_call" | custom-call | flops 134217728 | bytes 5242880 | tf_op jit(solution)/shard_map/project/pallas_call | solution.py:286
  16.3 2.6 %collective-permute-start.2 = (f32[264,512]{1,0:T(8,128)S(1)}, f32[264,512]{1,0:T(8,128)S(1)}, u32[]{:S(2)}, u32[]{:S(2)}) collective-permute-start(f32[264,512]{1,0:T(8,128)S(1)} %collective-permute-done.refs_0_.refs_2_), channel_id=1, source_target_pairs={{0,2},{2,4},{4,6},{6,7},{7,5},{5,3},{3,1},{1,0},{8,10},{10,12},{12... | collective-permute-start | bytes 1622024 | tf_op jit(solution)/shard_map/ppermute | solution.py:607
  18.8 1.5 %collective-permute-start.4 = (f32[264,512]{1,0:T(8,128)S(1)}, f32[264,512]{1,0:T(8,128)S(1)}, u32[]{:S(2)}, u32[]{:S(2)}) collective-permute-start(f32[264,512]{1,0:T(8,128)S(1)} %collective-permute-done.refs_0_.refs_2_), channel_id=1, source_target_pairs={{0,8},{1,9},{2,10},{3,11},{4,12},{5,13},{6,14},{7,15},{8,0},{9,1},... | collective-permute-start | bytes 1622024 | tf_op jit(solution)/shard_map/ppermute | solution.py:605
  20.4 3.0 %project.8 = (f32[128,256]{1,0:T(8,128)S(1)}, f32[128,256]{1,0:T(8,128)S(1)}) custom-call(s32[51]{0:T(128)S(1)} %reshape.22.place_ref, bf16[512,16,256]{2,1,0:T(8,128)(2,1)S(1)} %get-tuple-element.80.x_ref, f32[264,512]{1,0:T(8,128)S(1)} %collective-permute-done.refs_0_.refs_2_, f32[264,512]{1,0:T(8,128)S(1)} %collective-permute-done.1.refs_1_.refs_3_), custom_call_target="tpu_custom_call" | custom-call | flops 134217728 | bytes 5242880 | tf_op jit(solution)/shard_map/project/pallas_call | solution.py:286
  23.4 5.8 %collective-permute-done.2.refs_2_.refs_6_ = f32[264,512]{1,0:T(8,128)S(1)} collective-permute-done((f32[264,512]{1,0:T(8,128)S(1)}, f32[264,512]{1,0:T(8,128)S(1)}, u32[]{:S(2)}, u32[]{:S(2)}) %collective-permute-start.2) | collective-permute-done | bytes 540704 | tf_op jit(solution)/shard_map/ppermute | solution.py:607
  29.2 1.9 %collective-permute-done.3.refs_3_.refs_7_ = f32[264,512]{1,0:T(8,128)S(1)} collective-permute-done((f32[264,512]{1,0:T(8,128)S(1)}, f32[264,512]{1,0:T(8,128)S(1)}, u32[]{:S(2)}, u32[]{:S(2)}) %collective-permute-start.3) | collective-permute-done | bytes 540704 | tf_op jit(solution)/shard_map/ppermute | solution.py:608
  31.1 0.8 collective-permute-start.6
  31.9 0.7 collective-permute-start.7
  32.6 3.0 %collective-permute-start.8 = (f32[264,512]{1,0:T(8,128)S(1)}, f32[264,512]{1,0:T(8,128)S(1)}, u32[]{:S(2)}, u32[]{:S(2)}) collective-permute-start(f32[264,512]{1,0:T(8,128)S(1)} %collective-permute-done.2.refs_2_.refs_6_), channel_id=1, source_target_pairs={{0,8},{1,9},{2,10},{3,11},{4,12},{5,13},{6,14},{7,15},{8,0},{9,1},... | collective-permute-start | bytes 1622024 | tf_op jit(solution)/shard_map/ppermute | solution.py:605
  35.6 4.9 %project.9 = (f32[128,256]{1,0:T(8,128)S(1)}, f32[128,256]{1,0:T(8,128)S(1)}, f32[128,256]{1,0:T(8,128)S(1)}, f32[128,256]{1,0:T(8,128)S(1)}) custom-call(s32[51]{0:T(128)S(1)} %reshape.22.place_ref, bf16[512,16,256]{2,1,0:T(8,128)(2,1)S(1)} %get-tuple-element.80.x_ref, f32[264,512]{1,0:T(8,128)S(1)} %collective-permute-done.4.refs_0_.refs_4_, ...), custom_call_target="tpu_custom_call" | custom-call | flops 268435456 | bytes 6291456 | tf_op jit(solution)/shard_map/project/pallas_call | solution.py:286
  40.5 1.9 %collective-permute-done.6.refs_2_.refs_10_ = f32[264,512]{1,0:T(8,128)S(1)} collective-permute-done((f32[264,512]{1,0:T(8,128)S(1)}, f32[264,512]{1,0:T(8,128)S(1)}, u32[]{:S(2)}, u32[]{:S(2)}) %collective-permute-start.6) | collective-permute-done | bytes 540704 | tf_op jit(solution)/shard_map/ppermute | solution.py:607
  42.9 3.6 %collective-permute-start.10 = (f32[264,512]{1,0:T(8,128)S(1)}, f32[264,512]{1,0:T(8,128)S(1)}, u32[]{:S(2)}, u32[]{:S(2)}) collective-permute-start(f32[264,512]{1,0:T(8,128)S(1)} %collective-permute-done.6.refs_2_.refs_10_), channel_id=1, source_target_pairs={{0,8},{1,9},{2,10},{3,11},{4,12},{5,13},{6,14},{7,15},{8,0},{9,1},... | collective-permute-start | bytes 1622024 | tf_op jit(solution)/shard_map/ppermute | solution.py:605
  47.2 1.0 %collective-permute-start.13 = (f32[128,512]{1,0:T(8,128)S(1)}, f32[128,512]{1,0:T(8,128)S(1)}, u32[]{:S(2)}, u32[]{:S(2)}) collective-permute-start(f32[128,512]{1,0:T(8,128)S(1)} %slice.7), channel_id=1, source_target_pairs={{2,0},{4,2},{6,4},{7,6},{5,7},{3,5},{1,3},{0,1},{10,8},{12,10},{14... | collective-permute-start | bytes 786440 | tf_op jit(solution)/shard_map/ppermute | solution.py:611
  48.2 3.8 %project.10 = (f32[128,256]{1,0:T(8,128)S(1)}, f32[128,256]{1,0:T(8,128)S(1)}, f32[128,256]{1,0:T(8,128)S(1)}, f32[128,256]{1,0:T(8,128)S(1)}) custom-call(s32[51]{0:T(128)S(1)} %reshape.22.place_ref, bf16[512,16,256]{2,1,0:T(8,128)(2,1)S(1)} %get-tuple-element.80.x_ref, f32[264,512]{1,0:T(8,128)S(1)} %collective-permute-done.8.refs_0_.refs_8_, ...), custom_call_target="tpu_custom_call" | custom-call | flops 268435456 | bytes 6291456 | tf_op jit(solution)/shard_map/project/pallas_call | solution.py:286
  52.1 4.1 %project.11 = (f32[128,256]{1,0:T(8,128)S(1)}, f32[128,256]{1,0:T(8,128)S(1)}) custom-call(s32[51]{0:T(128)S(1)} %reshape.22.place_ref, bf16[512,16,256]{2,1,0:T(8,128)(2,1)S(1)} %get-tuple-element.80.x_ref, f32[264,512]{1,0:T(8,128)S(1)} %collective-permute-done.10.refs_0_.refs_12_, f32[264,512]{1,0:T(8,128)S(1)} %collective-permute-done.11.refs_1_.refs_13_), custom_call_target="tpu_custom_call" | custom-call | flops 134217728 | bytes 5242880 | tf_op jit(solution)/shard_map/project/pallas_call | solution.py:286
  56.8 2.1 %project.12 = (f32[128,256]{1,0:T(8,128)S(1)}, f32[128,256]{1,0:T(8,128)S(1)}) custom-call(s32[51]{0:T(128)S(1)} %reshape.22.place_ref, bf16[512,16,256]{2,1,0:T(8,128)(2,1)S(1)} %get-tuple-element.80.x_ref, f32[136,512]{1,0:T(8,128)S(1)} %collective-permute-done.12.refs_0_.refs_14_, f32[128,512]{1,0:T(8,128)S(1)} %collective-permute-done.13.refs_1_.refs_15_), custom_call_target="tpu_custom_call" | custom-call | flops 67108864 | bytes 4718592 | tf_op jit(solution)/shard_map/project/pallas_call | solution.py:286
  58.9 2.9 %project.13 = (f32[128,256]{1,0:T(8,128)S(1)}, f32[128,256]{1,0:T(8,128)S(1)}) custom-call(s32[51]{0:T(128)S(1)} %reshape.22.place_ref, bf16[512,16,256]{2,1,0:T(8,128)(2,1)S(1)} %get-tuple-element.80.x_ref, f32[136,512]{1,0:T(8,128)S(1)} %collective-permute-done.14.refs_0_.refs_16_, f32[128,512]{1,0:T(8,128)S(1)} %collective-permute-done.15.refs_1_.refs_17_), custom_call_target="tpu_custom_call" | custom-call | flops 67108864 | bytes 4718592 | tf_op jit(solution)/shard_map/project/pallas_call | solution.py:286
  61.8 23.3 %apply.1 = f32[16,32768]{1,0:T(8,128)} custom-call(s32[51]{0:T(128)S(1)} %reshape.22.place_ref, f32[8,64,128]{2,1,0:T(8,128)S(1)} %get-tuple-element.83.coupling_ref, f32[8,512]{1,0:T(8,128)S(1)} %get-tuple-element.81.refs_0_, f32[512,512]{1,0:T(8,128)S(1)} %copy-done, f32[264,512]{1,0:T(8,128)S(1)} %collective-permute-done.refs_0_.refs_2_, ...), custom_call_target="tpu_custom_call" | custom-call | tf_op jit(solution)/shard_map/apply/pallas_call | solution.py:524
  (27 shorter events, 1.9 us)
Async XLA Ops:
  0.0 13.2 %copy-start = (f32[512,512]{1,0:T(8,128)S(1)}, f32[512,512]{1,0:T(8,128)}, u32[]{:S(2)}) copy-start(f32[512,512]{1,0:T(8,128)} %refs_1_.3) | copy-start | bytes 3145732
  1.2 15.0 %collective-permute-start = (f32[264,512]{1,0:T(8,128)S(1)}, f32[264,512]{1,0:T(8,128)S(1)}, u32[]{:S(2)}, u32[]{:S(2)}) collective-permute-start(f32[264,512]{1,0:T(8,128)S(1)} %get-tuple-element.79), channel_id=1, source_target_pairs={{0,2},{2,4},{4,6},{6,7},{7,5},{5,3},{3,1},{1,0},{8,10},{10,12},{12... | collective-permute-start | bytes 1622024 | tf_op jit(solution)/shard_map/ppermute | solution.py:584
  3.4 12.9 %collective-permute-start.1 = (f32[264,512]{1,0:T(8,128)S(1)}, f32[264,512]{1,0:T(8,128)S(1)}, u32[]{:S(2)}, u32[]{:S(2)}) collective-permute-start(f32[264,512]{1,0:T(8,128)S(1)} %get-tuple-element.79), channel_id=1, source_target_pairs={{2,0},{4,2},{6,4},{7,6},{5,7},{3,5},{1,3},{0,1},{10,8},{12,10},{14... | collective-permute-start | bytes 1622024 | tf_op jit(solution)/shard_map/ppermute | solution.py:585
  4.9 0.9 %copy-start.1 = (f32[8,8,768]{2,1,0:T(8,128)S(1)}, f32[8,8,768]{2,1,0:T(8,128)}, u32[]{:S(2)}) copy-start(f32[8,8,768]{2,1,0:T(8,128)} %param.12) | copy-start | bytes 589828
  16.3 12.9 %collective-permute-start.2 = (f32[264,512]{1,0:T(8,128)S(1)}, f32[264,512]{1,0:T(8,128)S(1)}, u32[]{:S(2)}, u32[]{:S(2)}) collective-permute-start(f32[264,512]{1,0:T(8,128)S(1)} %collective-permute-done.refs_0_.refs_2_), channel_id=1, source_target_pairs={{0,2},{2,4},{4,6},{6,7},{7,5},{5,3},{3,1},{1,0},{8,10},{10,12},{12... | collective-permute-start | bytes 1622024 | tf_op jit(solution)/shard_map/ppermute | solution.py:607
  18.8 12.2 %collective-permute-start.3 = (f32[264,512]{1,0:T(8,128)S(1)}, f32[264,512]{1,0:T(8,128)S(1)}, u32[]{:S(2)}, u32[]{:S(2)}) collective-permute-start(f32[264,512]{1,0:T(8,128)S(1)} %collective-permute-done.1.refs_1_.refs_3_), channel_id=1, source_target_pairs={{2,0},{4,2},{6,4},{7,6},{5,7},{3,5},{1,3},{0,1},{10,8},{12,10},{14... | collective-permute-start | bytes 1622024 | tf_op jit(solution)/shard_map/ppermute | solution.py:608
  18.8 12.2 %collective-permute-start.4 = (f32[264,512]{1,0:T(8,128)S(1)}, f32[264,512]{1,0:T(8,128)S(1)}, u32[]{:S(2)}, u32[]{:S(2)}) collective-permute-start(f32[264,512]{1,0:T(8,128)S(1)} %collective-permute-done.refs_0_.refs_2_), channel_id=1, source_target_pairs={{0,8},{1,9},{2,10},{3,11},{4,12},{5,13},{6,14},{7,15},{8,0},{9,1},... | collective-permute-start | bytes 1622024 | tf_op jit(solution)/shard_map/ppermute | solution.py:605
  20.4 10.7 %collective-permute-start.5 = (f32[264,512]{1,0:T(8,128)S(1)}, f32[264,512]{1,0:T(8,128)S(1)}, u32[]{:S(2)}, u32[]{:S(2)}) collective-permute-start(f32[264,512]{1,0:T(8,128)S(1)} %collective-permute-done.1.refs_1_.refs_3_), channel_id=1, source_target_pairs={{0,8},{1,9},{2,10},{3,11},{4,12},{5,13},{6,14},{7,15},{8,0},{9,1},... | collective-permute-start | bytes 1622024 | tf_op jit(solution)/shard_map/ppermute | solution.py:605
  31.1 11.3 %collective-permute-start.6 = (f32[264,512]{1,0:T(8,128)S(1)}, f32[264,512]{1,0:T(8,128)S(1)}, u32[]{:S(2)}, u32[]{:S(2)}) collective-permute-start(f32[264,512]{1,0:T(8,128)S(1)} %collective-permute-done.2.refs_2_.refs_6_), channel_id=1, source_target_pairs={{0,2},{2,4},{4,6},{6,7},{7,5},{5,3},{3,1},{1,0},{8,10},{10,12},{12... | collective-permute-start | bytes 1622024 | tf_op jit(solution)/shard_map/ppermute | solution.py:607
  31.9 11.0 %collective-permute-start.7 = (f32[264,512]{1,0:T(8,128)S(1)}, f32[264,512]{1,0:T(8,128)S(1)}, u32[]{:S(2)}, u32[]{:S(2)}) collective-permute-start(f32[264,512]{1,0:T(8,128)S(1)} %collective-permute-done.3.refs_3_.refs_7_), channel_id=1, source_target_pairs={{2,0},{4,2},{6,4},{7,6},{5,7},{3,5},{1,3},{0,1},{10,8},{12,10},{14... | collective-permute-start | bytes 1622024 | tf_op jit(solution)/shard_map/ppermute | solution.py:608
  32.6 10.3 %collective-permute-start.8 = (f32[264,512]{1,0:T(8,128)S(1)}, f32[264,512]{1,0:T(8,128)S(1)}, u32[]{:S(2)}, u32[]{:S(2)}) collective-permute-start(f32[264,512]{1,0:T(8,128)S(1)} %collective-permute-done.2.refs_2_.refs_6_), channel_id=1, source_target_pairs={{0,8},{1,9},{2,10},{3,11},{4,12},{5,13},{6,14},{7,15},{8,0},{9,1},... | collective-permute-start | bytes 1622024 | tf_op jit(solution)/shard_map/ppermute | solution.py:605
  35.6 7.3 %collective-permute-start.9 = (f32[264,512]{1,0:T(8,128)S(1)}, f32[264,512]{1,0:T(8,128)S(1)}, u32[]{:S(2)}, u32[]{:S(2)}) collective-permute-start(f32[264,512]{1,0:T(8,128)S(1)} %collective-permute-done.3.refs_3_.refs_7_), channel_id=1, source_target_pairs={{0,8},{1,9},{2,10},{3,11},{4,12},{5,13},{6,14},{7,15},{8,0},{9,1},... | collective-permute-start | bytes 1622024 | tf_op jit(solution)/shard_map/ppermute | solution.py:605
  42.9 9.2 %collective-permute-start.10 = (f32[264,512]{1,0:T(8,128)S(1)}, f32[264,512]{1,0:T(8,128)S(1)}, u32[]{:S(2)}, u32[]{:S(2)}) collective-permute-start(f32[264,512]{1,0:T(8,128)S(1)} %collective-permute-done.6.refs_2_.refs_10_), channel_id=1, source_target_pairs={{0,8},{1,9},{2,10},{3,11},{4,12},{5,13},{6,14},{7,15},{8,0},{9,1},... | collective-permute-start | bytes 1622024 | tf_op jit(solution)/shard_map/ppermute | solution.py:605
  46.6 5.5 %collective-permute-start.11 = (f32[264,512]{1,0:T(8,128)S(1)}, f32[264,512]{1,0:T(8,128)S(1)}, u32[]{:S(2)}, u32[]{:S(2)}) collective-permute-start(f32[264,512]{1,0:T(8,128)S(1)} %collective-permute-done.7.refs_3_.refs_11_), channel_id=1, source_target_pairs={{0,8},{1,9},{2,10},{3,11},{4,12},{5,13},{6,14},{7,15},{8,0},{9,1},... | collective-permute-start | bytes 1622024 | tf_op jit(solution)/shard_map/ppermute | solution.py:605
  46.6 9.5 %collective-permute-start.12 = (f32[136,512]{1,0:T(8,128)S(1)}, f32[136,512]{1,0:T(8,128)S(1)}, u32[]{:S(2)}, u32[]{:S(2)}) collective-permute-start(f32[136,512]{1,0:T(8,128)S(1)} %slice.6), channel_id=1, source_target_pairs={{0,2},{2,4},{4,6},{6,7},{7,5},{5,3},{3,1},{1,0},{8,10},{10,12},{12... | collective-permute-start | bytes 835592 | tf_op jit(solution)/shard_map/ppermute | solution.py:610
  47.2 8.9 %collective-permute-start.13 = (f32[128,512]{1,0:T(8,128)S(1)}, f32[128,512]{1,0:T(8,128)S(1)}, u32[]{:S(2)}, u32[]{:S(2)}) collective-permute-start(f32[128,512]{1,0:T(8,128)S(1)} %slice.7), channel_id=1, source_target_pairs={{2,0},{4,2},{6,4},{7,6},{5,7},{3,5},{1,3},{0,1},{10,8},{12,10},{14... | collective-permute-start | bytes 786440 | tf_op jit(solution)/shard_map/ppermute | solution.py:611
  56.2 2.7 %collective-permute-start.14 = (f32[136,512]{1,0:T(8,128)S(1)}, f32[136,512]{1,0:T(8,128)S(1)}, u32[]{:S(2)}, u32[]{:S(2)}) collective-permute-start(f32[136,512]{1,0:T(8,128)S(1)} %collective-permute-done.12.refs_0_.refs_14_), channel_id=1, source_target_pairs={{0,8},{1,9},{2,10},{3,11},{4,12},{5,13},{6,14},{7,15},{8,0},{9,1},... | collective-permute-start | bytes 835592 | tf_op jit(solution)/shard_map/ppermute | solution.py:605
  56.3 2.6 %collective-permute-start.15 = (f32[128,512]{1,0:T(8,128)S(1)}, f32[128,512]{1,0:T(8,128)S(1)}, u32[]{:S(2)}, u32[]{:S(2)}) collective-permute-start(f32[128,512]{1,0:T(8,128)S(1)} %collective-permute-done.13.refs_1_.refs_15_), channel_id=1, source_target_pairs={{0,8},{1,9},{2,10},{3,11},{4,12},{5,13},{6,14},{7,15},{8,0},{9,1},... | collective-permute-start | bytes 786440 | tf_op jit(solution)/shard_map/ppermute | solution.py:605
